TPU v7x, 32 devices: a whole 2x2x4 slice. The times are simulated.
32 devices in a mesh: slab: 4 (over x, core), clip: 8 (over z, y).
Axes of the slice: x: 2, y: 2, z: 4, core: 2. Of those that a mesh axis runs over, the one named last changes fastest.
Arguments:
- tokens: bfloat16 [8, 4, 1024, 512], P('clip', 'slab'), may hold values from -6 to 6
- y_grad: bfloat16 [8, 4, 1024, 512], P('clip', 'slab'), may hold values from -6 to 6
- clip_rows: int32 [8, 4], P('clip'), may hold values from 0 to 192, as said below
- qkv_weight: float32 [512, 1536], P('clip', 'slab'), may hold values from -0.25 to 0.25
- proj_weight: float32 [512, 512], P('clip', 'slab'), may hold values from -0.75 to 0.75
- up_weight: float32 [512, 2048], P('clip', 'slab'), may hold values from -0.25 to 0.25
- down_weight: float32 [2048, 512], P('clip', 'slab'), may hold values from -0.1875 to 0.1875
- qkv_m: float32 [512, 1536], P('clip', 'slab'), may hold values from -1.2 to 1.2
- proj_m: float32 [512, 512], P('clip', 'slab'), may hold values from -1.2 to 1.2
- up_m: float32 [512, 2048], P('clip', 'slab'), may hold values from -1.2 to 1.2
- down_m: float32 [2048, 512], P('clip', 'slab'), may hold values from -1.2 to 1.2
- qkv_v: float32 [512, 1536], P('clip', 'slab'), may hold values from 0.05 to 0.35
- proj_v: float32 [512, 512], P('clip', 'slab'), may hold values from 0.05 to 0.35
- up_v: float32 [512, 2048], P('clip', 'slab'), may hold values from 0.05 to 0.35
- down_v: float32 [2048, 512], P('clip', 'slab'), may hold values from 0.05 to 0.35
- vectors: float32 [12, 512], replicated, may hold values from -1.2 to 1.5, as said below
- vectors_m: float32 [12, 512], replicated, may hold values from -1.2 to 1.2
- vectors_v: float32 [12, 512], replicated, may hold values from 0.05 to 0.35
- table: float32 [49, 16], replicated, may hold values from -3 to 3
- table_m: float32 [49, 16], replicated, may hold values from -1.2 to 1.2
- table_v: float32 [49, 16], replicated, may hold values from 0.05 to 0.35
Outputs:
- block_out: bfloat16 [8, 4, 1024, 512], P('clip', 'slab')
- x_grad: float32 [8, 4, 1024, 512], P('clip', 'slab')
- qkv_new: float32 [512, 1536], P('clip', 'slab')
- qkv_m_new: float32 [512, 1536], P('clip', 'slab')
- qkv_v_new: float32 [512, 1536], P('clip', 'slab')
- proj_new: float32 [512, 512], P('clip', 'slab')
- proj_m_new: float32 [512, 512], P('clip', 'slab')
- proj_v_new: float32 [512, 512], P('clip', 'slab')
- up_new: float32 [512, 2048], P('clip', 'slab')
- up_m_new: float32 [512, 2048], P('clip', 'slab')
- up_v_new: float32 [512, 2048], P('clip', 'slab')
- down_new: float32 [2048, 512], P('clip', 'slab')
- down_m_new: float32 [2048, 512], P('clip', 'slab')
- down_v_new: float32 [2048, 512], P('clip', 'slab')
- vectors_new: float32 [12, 512], replicated
- vectors_m_new: float32 [12, 512], replicated
- vectors_v_new: float32 [12, 512], replicated
- table_new: float32 [49, 16], replicated
- table_m_new: float32 [49, 16], replicated
- table_v_new: float32 [49, 16], replicated
Inputs may be any that keep to these rules, and one draw needn't show every extreme that they name: `clip_rows`: each entry is 0 (no clip), 64 or 192; in a row the nonzero entries come first and there is at least one; a row's entries sum to at most 512, and in every draw some row sums to exactly that and holds a clip of 192 rows. `vectors`: rows 0 and 5 lie in 0.5 to 1.5.
All inputs are finite; a program needn't handle non-finite values.
Results may differ from a plain program's by a relative error of at most 0.015.
Values may be sent and summed in bfloat16 or wider, within the bound.
A program may use at most 128 MiB of HBM per device.

v0:
```python
import jax
import jax.numpy as jnp
from jax import lax
from jax.sharding import PartitionSpec as P

HEADS = 16
BINS = 8
WIN = 4
STEP = 10
RELS = 49


HIGHEST = lax.Precision.HIGHEST
norm_epsilon = 1e-06
beta_first = 0.5
beta_second = 0.5
adam_epsilon = 1e-08
rate_matrix = 0.05
rate_vector = 0.5
weight_decay = 0.05
masked_score = -1e30


def from_behind(block, axis, distance):
    devices = range(lax.axis_size(axis))
    route = [((i - distance) % len(devices), i) for i in devices]
    return lax.ppermute(block, axis, route)


def layer_norm(values):
    center = values - jnp.mean(values, -1, keepdims=True)
    spread = jnp.mean(center * center, -1, keepdims=True)
    return center * lax.rsqrt(spread + norm_epsilon)


def affine_norm(values, gain, offset):
    return layer_norm(values) * gain + offset


def gelu_exact(values):
    return jax.nn.gelu(values, approximate=False)


def window_rows(lengths, slab_index, slab_count, rows_dev):
    segment = lengths // slab_count
    seg_ends = jnp.cumsum(segment)
    seg_starts = seg_ends - segment
    row_base = WIN * jnp.arange(rows_dev // WIN, dtype=jnp.int32)
    inside = (row_base[:, None] >= seg_starts[None, :]) & (row_base[:, None] < seg_ends[None, :])
    in_clip = jnp.any(inside, axis=1)
    slot_ids = jnp.arange(lengths.shape[0], dtype=jnp.int32)
    clip_end = jnp.sum(jnp.where(inside, seg_ends[None, :], 0), axis=1)
    clip_slot = jnp.sum(jnp.where(inside, slot_ids[None, :], 0), axis=1)
    row_ids = (
        row_base[:, None]
        + jnp.where(in_clip, WIN // 2, 0)[:, None]
        + jnp.arange(WIN, dtype=jnp.int32)[None, :]
    )
    beyond = in_clip[:, None] & (row_ids >= clip_end[:, None])
    source = jnp.where(
        beyond, rows_dev + 2 * clip_slot[:, None] + row_ids - clip_end[:, None], row_ids
    )
    time_wraps = in_clip & (row_base + WIN == clip_end) & (slab_index == slab_count - 1)
    return (source, time_wraps, seg_starts)


def window_mask(time_wraps, bin_folds):
    positions = jnp.arange(WIN * WIN, dtype=jnp.int32)
    row_half = positions // WIN >= WIN // 2
    bin_half = positions % WIN >= WIN // 2
    same_row = row_half[:, None] == row_half[None, :]
    same_bin = bin_half[:, None] == bin_half[None, :]
    return (~time_wraps[:, None, None] | same_row[None]) & (
        ~bin_folds[:, None, None] | same_bin[None]
    )


def offset_table():
    positions = jnp.arange(WIN * WIN, dtype=jnp.int32)
    row_pos = positions // WIN
    bin_pos = positions % WIN
    offsets = (row_pos[:, None] - row_pos[None, :] + WIN - 1) * (2 * WIN - 1) + (
        bin_pos[:, None] - bin_pos[None, :] + WIN - 1
    )
    return (offsets.reshape(-1)[:, None] == jnp.arange(RELS, dtype=jnp.int32)[None, :]).astype(
        jnp.float32
    )


def to_windows(extended, source):
    gathered = jnp.roll(extended[source], -(WIN // 2), axis=2)
    win_rows = source.shape[0]
    width = extended.shape[-1]
    gathered = gathered.reshape(win_rows, WIN, BINS // WIN, WIN, width).transpose(0, 2, 1, 3, 4)
    return gathered.reshape(win_rows * (BINS // WIN), WIN * WIN, width)


def from_windows(windows, source, total_rows):
    win_rows = source.shape[0]
    width = windows.shape[-1]
    placed = windows.reshape(win_rows, BINS // WIN, WIN, WIN, width).transpose(0, 2, 1, 3, 4)
    placed = jnp.roll(placed.reshape(win_rows, WIN, BINS, width), WIN // 2, axis=2)
    blank = jnp.zeros((total_rows, BINS, width), windows.dtype)
    return blank.at[source.reshape(-1)].set(placed.reshape(win_rows * WIN, BINS, width))


def adamw(weight, first, second, grad, rate, decay):
    first = beta_first * first + (1.0 - beta_first) * grad
    second = beta_second * second + (1.0 - beta_second) * grad * grad
    fix_first = 1.0 - beta_first**STEP
    fix_second = 1.0 - beta_second**STEP
    update = first / fix_first / (jnp.sqrt(second / fix_second) + adam_epsilon)
    return (weight - rate * (update + decay * weight), first, second)


def shards(
    tokens,
    y_grad,
    clip_rows,
    qkv_weight,
    proj_weight,
    up_weight,
    down_weight,
    qkv_m,
    proj_m,
    up_m,
    down_m,
    qkv_v,
    proj_v,
    up_v,
    down_v,
    vectors,
    vectors_m,
    vectors_v,
    table,
    table_m,
    table_v,
):
    lengths = clip_rows[0]
    slab_count = lax.axis_size("slab")
    inputs = tokens[0, 0].astype(jnp.float32)
    tok_count, width = inputs.shape
    rows_dev = tok_count // BINS
    head_dim = width // HEADS
    score_scale = head_dim ** (-0.5)
    source, time_wraps, seg_starts = window_rows(
        lengths, lax.axis_index("slab"), slab_count, rows_dev
    )
    total_rows = rows_dev + 2 * lengths.shape[0]
    head_rows = jnp.minimum(
        seg_starts[:, None] + jnp.arange(2, dtype=jnp.int32)[None, :], rows_dev - 1
    ).reshape(-1)
    windows_count = source.shape[0] * (BINS // WIN)
    bin_folds = jnp.arange(windows_count) % (BINS // WIN) == BINS // WIN - 1
    allowed = window_mask(jnp.repeat(time_wraps, BINS // WIN), bin_folds)[:, None]
    offset_hot = offset_table()
    rel_bias = (
        jnp.dot(offset_hot, table, precision=HIGHEST)
        .reshape(WIN * WIN, WIN * WIN, HEADS)
        .transpose(2, 0, 1)
    )
    used_rows = jnp.sum(lengths) // slab_count
    live_rows = (jnp.arange(tok_count) // BINS < used_rows).astype(jnp.float32)[:, None]
    part_copies = (
        lax.all_gather(qkv_weight.astype(jnp.bfloat16), "clip", axis=0, tiled=True),
        lax.all_gather(proj_weight.astype(jnp.bfloat16), "clip", axis=0, tiled=True),
        lax.all_gather(up_weight.astype(jnp.bfloat16), "clip", axis=0, tiled=True),
        lax.all_gather(down_weight.astype(jnp.bfloat16), "clip", axis=0, tiled=True),
    )
    copies = (
        lax.all_gather(part_copies[0], "slab", axis=1, tiled=True),
        lax.all_gather(part_copies[1], "slab", axis=1, tiled=True),
        lax.all_gather(part_copies[2], "slab", axis=1, tiled=True),
        lax.all_gather(part_copies[3], "slab", axis=1, tiled=True),
    )
    qkv_copy, proj_copy, up_copy, down_copy = copies
    attn_input = affine_norm(inputs, vectors[0], vectors[1]).astype(jnp.bfloat16)
    bias_row = jnp.concatenate([vectors[2], jnp.zeros_like(vectors[2]), vectors[3]])
    qkv_rows = (
        jnp.dot(attn_input, qkv_copy, preferred_element_type=jnp.float32) + bias_row
    ).astype(jnp.bfloat16)
    qkv_grid = qkv_rows.reshape(rows_dev, BINS, 3 * width)
    borrowed = from_behind(qkv_grid[head_rows], "slab", -1)
    qkv_windows = to_windows(jnp.concatenate([qkv_grid, borrowed], 0), source)
    query_win = qkv_windows[:, :, :width].reshape(windows_count, WIN * WIN, HEADS, head_dim)
    key_win = qkv_windows[:, :, width : 2 * width].reshape(
        windows_count, WIN * WIN, HEADS, head_dim
    )
    value_win = qkv_windows[:, :, 2 * width :].reshape(windows_count, WIN * WIN, HEADS, head_dim)

    def scores_of(queries, keys_all):
        raw = (
            jnp.einsum("wqhd,wkhd->whqk", queries, keys_all, preferred_element_type=jnp.float32)
            * score_scale
            + rel_bias[None]
        )
        return jnp.where(allowed, raw, masked_score)

    scores = scores_of(query_win, key_win)
    top_score = jnp.max(scores, -1, keepdims=True)
    exp_sum = jnp.sum(jnp.exp(scores - top_score), -1, keepdims=True)
    probs_low = (jnp.exp(scores - top_score) / exp_sum).astype(jnp.bfloat16)
    attended = jnp.einsum(
        "whqk,wkhd->wqhd", probs_low, value_win, preferred_element_type=jnp.float32
    )
    attended = attended.astype(jnp.bfloat16).reshape(windows_count, WIN * WIN, width)
    spread_out = from_windows(attended, source, total_rows)
    returned = from_behind(spread_out[rows_dev:], "slab", 1)
    attended_rows = spread_out[:rows_dev].at[head_rows].add(returned).reshape(tok_count, width)
    residual = (
        inputs + jnp.dot(attended_rows, proj_copy, preferred_element_type=jnp.float32) + vectors[4]
    )
    mlp_input = affine_norm(residual, vectors[5], vectors[6]).astype(jnp.bfloat16)
    pre_gelu = jnp.dot(mlp_input, up_copy, preferred_element_type=jnp.float32) + vectors[
        8:
    ].reshape(-1)
    activated, gelu_pull = jax.vjp(gelu_exact, pre_gelu)
    activated_low = activated.astype(jnp.bfloat16)
    block_out = (
        residual
        + jnp.dot(activated_low, down_copy, preferred_element_type=jnp.float32)
        + vectors[7]
    ) * live_rows
    out_grad = y_grad[0, 0].astype(jnp.float32) * live_rows
    out_low = out_grad.astype(jnp.bfloat16)
    down_grad = jnp.dot(activated_low.T, out_low, preferred_element_type=jnp.float32)
    act_grad = jnp.dot(out_low, down_copy.T, preferred_element_type=jnp.float32)
    pre_low = gelu_pull(act_grad)[0].astype(jnp.bfloat16)
    up_grad = jnp.dot(mlp_input.T, pre_low, preferred_element_type=jnp.float32)
    mlp_in_grad = jnp.dot(pre_low, up_copy.T, preferred_element_type=jnp.float32)
    norm_value, norm_pull = jax.vjp(affine_norm, residual, vectors[5], vectors[6])
    resid_norm_grad, gain_two_grad, shift_two_grad = norm_pull(mlp_in_grad)
    resid_grad = out_grad + resid_norm_grad
    attn_low = resid_grad.astype(jnp.bfloat16)
    proj_grad = jnp.dot(attended_rows.T, attn_low, preferred_element_type=jnp.float32)
    mixed_grad = jnp.dot(attn_low, proj_copy.T, preferred_element_type=jnp.float32).astype(
        jnp.bfloat16
    )
    mixed_grid = mixed_grad.reshape(rows_dev, BINS, width)
    sent_back = from_behind(mixed_grid[head_rows], "slab", -1)
    grad_windows = to_windows(jnp.concatenate([mixed_grid, sent_back], 0), source)
    grad_windows = grad_windows.reshape(windows_count, WIN * WIN, HEADS, head_dim)
    probs = jnp.exp(scores_of(query_win, key_win) - top_score) / exp_sum
    prob_grad = jnp.einsum(
        "wqhd,wkhd->whqk", grad_windows, value_win, preferred_element_type=jnp.float32
    )
    value_grad = jnp.einsum(
        "whqk,wqhd->wkhd", probs_low, grad_windows, preferred_element_type=jnp.float32
    )
    score_grad = (probs * (prob_grad - jnp.sum(probs * prob_grad, -1, keepdims=True))).astype(
        jnp.bfloat16
    )
    bias_grad = (
        jnp.sum(score_grad.astype(jnp.float32), 0)
        .transpose(1, 2, 0)
        .reshape(WIN * WIN * WIN * WIN, HEADS)
    )
    table_grad = jnp.dot(offset_hot.T, bias_grad, precision=HIGHEST)
    query_grad = (
        jnp.einsum("whqk,wkhd->wqhd", score_grad, key_win, preferred_element_type=jnp.float32)
        * score_scale
    )
    key_grad = (
        jnp.einsum("whqk,wqhd->wkhd", score_grad, query_win, preferred_element_type=jnp.float32)
        * score_scale
    )
    qkv_grad_win = jnp.concatenate(
        [
            query_grad.reshape(windows_count, WIN * WIN, width),
            key_grad.reshape(windows_count, WIN * WIN, width),
            value_grad.reshape(windows_count, WIN * WIN, width),
        ],
        -1,
    ).astype(jnp.bfloat16)
    qkv_spread = from_windows(qkv_grad_win, source, total_rows)
    given_back = from_behind(qkv_spread[rows_dev:], "slab", 1)
    qkv_grad_rows = (
        qkv_spread[:rows_dev].at[head_rows].add(given_back).reshape(tok_count, 3 * width)
    )
    qkv_w_grad = jnp.dot(attn_input.T, qkv_grad_rows, preferred_element_type=jnp.float32)
    bias_sums = jnp.sum(qkv_grad_rows.astype(jnp.float32), 0)
    attn_in_grad = jnp.dot(qkv_grad_rows, qkv_copy.T, preferred_element_type=jnp.float32)
    first_value, norm_pull_one = jax.vjp(affine_norm, inputs, vectors[0], vectors[1])
    inputs_norm_grad, gain_one_grad, shift_one_grad = norm_pull_one(attn_in_grad)
    x_grad = resid_grad + inputs_norm_grad
    vector_grad = jnp.concatenate(
        [
            jnp.stack(
                [
                    gain_one_grad,
                    shift_one_grad,
                    bias_sums[:width],
                    bias_sums[2 * width :],
                    jnp.sum(attn_low.astype(jnp.float32), 0),
                    gain_two_grad,
                    shift_two_grad,
                    jnp.sum(out_grad, 0),
                ]
            ),
            jnp.sum(pre_low.astype(jnp.float32), 0).reshape(-1, width),
        ],
        0,
    )
    grad_scale = float(tok_count * slab_count * lax.axis_size("clip")) ** (-0.5)
    part_sums = (
        lax.psum_scatter(
            (qkv_w_grad * grad_scale).astype(jnp.bfloat16), "slab", scatter_dimension=1, tiled=True
        ).astype(jnp.float32),
        lax.psum_scatter(
            (proj_grad * grad_scale).astype(jnp.bfloat16), "slab", scatter_dimension=1, tiled=True
        ).astype(jnp.float32),
        lax.psum_scatter(
            (up_grad * grad_scale).astype(jnp.bfloat16), "slab", scatter_dimension=1, tiled=True
        ).astype(jnp.float32),
        lax.psum_scatter(
            (down_grad * grad_scale).astype(jnp.bfloat16), "slab", scatter_dimension=1, tiled=True
        ).astype(jnp.float32),
    )
    owned = (
        lax.psum_scatter(part_sums[0], "clip", scatter_dimension=0, tiled=True),
        lax.psum_scatter(part_sums[1], "clip", scatter_dimension=0, tiled=True),
        lax.psum_scatter(part_sums[2], "clip", scatter_dimension=0, tiled=True),
        lax.psum_scatter(part_sums[3], "clip", scatter_dimension=0, tiled=True),
    )
    small_sums = lax.psum((vector_grad * grad_scale, table_grad * grad_scale), ("slab", "clip"))
    qkv_new, qkv_m_new, qkv_v_new = adamw(
        qkv_weight, qkv_m, qkv_v, owned[0], rate_matrix, weight_decay
    )
    proj_new, proj_m_new, proj_v_new = adamw(
        proj_weight, proj_m, proj_v, owned[1], rate_matrix, weight_decay
    )
    up_new, up_m_new, up_v_new = adamw(up_weight, up_m, up_v, owned[2], rate_matrix, weight_decay)
    down_new, down_m_new, down_v_new = adamw(
        down_weight, down_m, down_v, owned[3], rate_matrix, weight_decay
    )
    vectors_new, vectors_m_new, vectors_v_new = adamw(
        vectors, vectors_m, vectors_v, small_sums[0], rate_vector, 0.0
    )
    table_new, table_m_new, table_v_new = adamw(
        table, table_m, table_v, small_sums[1], rate_vector, 0.0
    )
    out_shape = (1, 1, tok_count, width)
    return (
        block_out.astype(jnp.bfloat16).reshape(out_shape),
        x_grad.reshape(out_shape),
        qkv_new,
        qkv_m_new,
        qkv_v_new,
        proj_new,
        proj_m_new,
        proj_v_new,
        up_new,
        up_m_new,
        up_v_new,
        down_new,
        down_m_new,
        down_v_new,
        vectors_new,
        vectors_m_new,
        vectors_v_new,
        table_new,
        table_m_new,
        table_v_new,
    )


def solution(mesh):
    return jax.shard_map(
        shards,
        mesh=mesh,
        in_specs=(
            P("clip", "slab", None, None),
            P("clip", "slab", None, None),
            P("clip", None),
            P("clip", "slab"),
            P("clip", "slab"),
            P("clip", "slab"),
            P("clip", "slab"),
            P("clip", "slab"),
            P("clip", "slab"),
            P("clip", "slab"),
            P("clip", "slab"),
            P("clip", "slab"),
            P("clip", "slab"),
            P("clip", "slab"),
            P("clip", "slab"),
            P(),
            P(),
            P(),
            P(),
            P(),
            P(),
        ),
        out_specs=(
            P("clip", "slab", None, None),
            P("clip", "slab", None, None),
            P("clip", "slab"),
            P("clip", "slab"),
            P("clip", "slab"),
            P("clip", "slab"),
            P("clip", "slab"),
            P("clip", "slab"),
            P("clip", "slab"),
            P("clip", "slab"),
            P("clip", "slab"),
            P("clip", "slab"),
            P("clip", "slab"),
            P("clip", "slab"),
            P(),
            P(),
            P(),
            P(),
            P(),
            P(),
        ),
        check_vma=False,
    )
```

profile of v0, /device:TPU:0, one launch (start us, length us, event | category | flops | bytes accessed | tf_op | source)
XLA Modules:
  0.0 840.3 jit_solution(1453344243937595426)
XLA Ops:
  8.2 34.8 %all_gather.24 = bf16[512,384]{1,0:T(8,128)(2,1)} all-gather(bf16[64,384]{1,0:T(8,128)(2,1)S(1)} %convert_element_type.119), channel_id=1, replica_groups=mesh['slab'=4,'clip'=8] {'clip'}, dimensions={0}, use_global_device_ids=true | all-gather | bytes 442368 | tf_op jit(solution)/shard_map/all_gather | solution.py:165
  44.1 33.3 %all_gather.28 = bf16[512,512]{1,0:T(8,128)(2,1)} all-gather(bf16[64,512]{1,0:T(8,128)(2,1)S(1)} %convert_element_type.126), channel_id=1, replica_groups=mesh['slab'=4,'clip'=8] {'clip'}, dimensions={0}, use_global_device_ids=true | all-gather | bytes 589824 | tf_op jit(solution)/shard_map/all_gather | solution.py:167
  85.9 30.5 %all_gather.26 = bf16[512,128]{1,0:T(8,128)(2,1)S(1)} all-gather(bf16[64,128]{1,0:T(8,128)(2,1)S(1)} %convert_element_type.124), channel_id=1, replica_groups=mesh['slab'=4,'clip'=8] {'clip'}, dimensions={0}, use_global_device_ids=true | all-gather | bytes 147456 | tf_op jit(solution)/shard_map/all_gather | solution.py:166
  122.8 5.1 fusion.18
  127.9 2.4 gather_fusion
  130.5 9.3 %all_gather.27 = bf16[512,512]{1,0:T(8,128)(2,1)} all-gather(bf16[512,128]{1,0:T(8,128)(2,1)S(1)} %all_gather.26), channel_id=1, replica_groups=mesh['slab'=4,'clip'=8] {'slab'}, dimensions={1}, use_global_device_ids=true | all-gather | bytes 655360 | tf_op jit(solution)/shard_map/all_gather | solution.py:172
  139.7 3.9 pad_maximum_fusion
  143.6 4.4 gather_fusion.1
  150.3 2.6 slice.122
  156.3 4.1 copy.219
  160.4 6.1 reshape.760
  166.5 3.6 fusion.104
  170.1 2.4 copy.220
  172.5 6.9 copy.226
  181.7 6.8 copy.223
  190.8 6.8 copy.224
  197.6 11.3 %fusion.108 = (f32[64,16,16]{2,1,0:T(8,128)S(1)}, f32[64,16,16,16]{2,3,1,0:T(8,128)}) fusion(f32[16,16,16]{1,2,0:T(8,128)S(1)} %bitcast.220, pred[64,16,16]{1,2,0:T(8,128)(4,1)S(1)} %or_and_fusion, bf16[64,16,16,32]{3,1,2,0:T(8,128)(2,1)} %copy.223, bf16[64,16,16,32]{3,1,2,0:T(8,128)(2,1)} %copy.224), kind=kOutput, calls=%fused_computation.228 | convolution fusion | flops 18087952 | bytes 3244032 | tf_op jit(solution)/shard_map/sub | solution.py:202
  208.9 6.2 convert_bitcast_fusion.1
  215.1 3.0 copy.228
  218.1 5.9 reshape_reshape.6
  225.5 4.3 scatter_fusion
  230.3 3.3 collective-permute-done.1
  238.0 25.2 %multiply_convert_fusion.3 = (bf16[1024,2048]{1,0:T(8,128)(2,1)S(1)}, f32[1024,2048]{1,0:T(8,128)}, f32[1024,2048]{1,0:T(8,128)}) fusion(f32[2048]{0:T(1024)S(1)} %bitcast.237, bf16[512,2048]{1,0:T(8,128)(2,1)} %all-gather.6.cloned.1.call-done, f32[1024,512]{0,1:T(8,128)S(1)} %get-tuple-element.215, f32[512]{0:T(512)S(1)} %bitcast.242, ...), kind=kOutput, calls=%fused_computation.18 | convolution fusion | flops 2288517120 | bytes 25186304 | tf_op jit(solution)/shard_map/dot_general | solution.py:214
  265.2 3.8 multiply_convert_fusion.4
  269.0 4.0 copy.260
  273.1 31.9 %reduce-scatter.29.cloned.1.call-done = bf16[128,2048]{1,0:T(8,128)(2,1)} async-done(((bf16[512,2048]{1,0:T(8,128)(2,1)}), bf16[128,2048]{1,0:T(8,128)(2,1)}) %reduce-scatter.29.cloned.1.call-update) | async-done | bytes 524304
  309.2 63.6 %reduce-scatter.23.cloned.1.call-done = f32[256,128]{1,0:T(8,128)} async-done(((f32[2048,128]{1,0:T(8,128)}), f32[256,128]{1,0:T(8,128)}) %reduce-scatter.23.cloned.1.call-update) | async-done | bytes 131088 | tf_op jit(solution)/shard_map/reduce_scatter | solution.py:323
  374.5 33.3 %all_gather.30 = bf16[2048,128]{1,0:T(8,128)(2,1)} all-gather(bf16[256,128]{1,0:T(8,128)(2,1)S(1)} %get-tuple-element.199), channel_id=1, replica_groups=mesh['slab'=4,'clip'=8] {'clip'}, dimensions={0}, use_global_device_ids=true | all-gather | bytes 589824 | tf_op jit(solution)/shard_map/all_gather | solution.py:168
  407.8 22.2 %all-gather.8.cloned.1.call-done = bf16[2048,512]{1,0:T(8,128)(2,1)} async-done(((bf16[2048,128]{1,0:T(8,128)(2,1)}), bf16[2048,512]{1,0:T(8,128)(2,1)}) %all-gather.8.cloned.1.call-update) | async-done | bytes 2097168 | tf_op jit(solution)/shard_map/all_gather | solution.py:174
  430.1 9.5 %convert_reduce_fusion.1 = (f32[2048]{0:T(1024)S(1)}, bf16[1024,2048]{1,0:T(8,128)(2,1)S(1)}) fusion(f32[1024,2048]{1,0:T(8,128)} %get-tuple-element.193, bf16[2048,512]{1,0:T(8,128)(2,1)} %all-gather.8.cloned.1.call-done, bf16[1,1,1024,512]{2,3,1,0:T(8,128)(2,1)S(1)} %copy-done.10, f32[1024]{0:T(1024)S(1)} %fusion.85, ...), kind=kOutput, calls=%fused_computation.12 | convolution fusion | flops 2184706048 | bytes 24137728 | tf_op jit(solution)/shard_map/dot_general | solution.py:227
  439.6 4.3 fusion.111
  443.9 2.9 copy.233
  446.8 3.0 multiply_reduce_fusion.1
  461.4 4.0 reshape_reshape.7
  465.4 9.2 %convert_bitcast_fusion = bf16[64,16,16,32]{3,1,2,0:T(8,128)(2,1)} fusion(bf16[64,16,16,32]{3,2,1,0:T(8,128)(2,1)} %reshape_reshape.7, f32[64,16,16,16]{2,3,1,0:T(8,128)} %get-tuple-element.213, f32[64,16,16]{2,1,0:T(8,128)S(1)} %copy-done.18), kind=kOutput, calls=%fused_computation.41 | convolution fusion | flops 17825792 | bytes 3211264 | tf_op jit(solution)/shard_map/whqk,wqhd->wkhd/dot_general | solution.py:247
  474.6 10.7 %multiply_reduce_fusion = (f32[64,16,16]{2,1,0:T(8,128)S(1)}, f32[64,16,16,16]{2,3,1,0:T(8,128)}) fusion(f32[64,16,16,16]{2,3,1,0:T(8,128)} %get-tuple-element.213, f32[64,16,16]{2,1,0:T(8,128)S(1)} %copy-done.18, bf16[64,16,16,32]{3,1,2,0:T(8,128)(2,1)} %copy.226, bf16[64,16,16,32]{3,2,1,0:T(8,128)(2,1)S(1)} %copy-done.11), kind=kOutput, calls=%fused_computation.16 | convolution fusion | flops 17547264 | bytes 4325376 | tf_op jit(solution)/shard_map/wqhd,wkhd->whqk/dot_general | solution.py:244
  485.3 7.6 convert_reduce_fusion
  492.9 4.3 fusion.9
  497.2 3.1 fusion.8
  500.3 3.0 copy.244
  503.4 6.0 concatenate.47
  509.4 5.2 copy.242
  514.7 5.9 concatenate.46
  520.5 5.2 copy.240
  525.8 5.9 concatenate.45
  531.7 4.9 maximum_bitcast_fusion
  538.9 3.4 copy.246
  542.5 12.3 %scatter_fusion.2 = bf16[136,8,1536]{2,1,0:T(8,128)(2,1)S(1)} fusion(bf16[136,8,1536]{2,1,0:T(8,128)(2,1)S(1)} %broadcast_in_dim.67, s32[128]{0:T(128)S(1)} %copy-done.44, bf16[128,8,1536]{2,1,0:T(8,128)(2,1)} %bitcast.203), kind=kCustom, calls=%fused_computation.6 | custom fusion | bytes 9437696 | tf_op jit(solution)/shard_map/scatter | solution.py:104
  557.1 3.7 slice.135
  561.9 2.7 scatter_fusion.3
  564.5 5.0 fusion.22
  569.5 2.8 copy.256
  572.4 6.0 multiply_convert_fusion.5
  580.3 6.6 fusion.50
  587.0 2.4 copy.251
  589.6 12.3 %reduce-scatter.25.cloned.1.call-done = bf16[384,512]{1,0:T(8,128)(2,1)} async-done(((bf16[1536,512]{1,0:T(8,128)(2,1)}), bf16[384,512]{1,0:T(8,128)(2,1)}) %reduce-scatter.25.cloned.1.call-update) | async-done | bytes 393232
  605.0 5.6 fusion.110
  614.6 21.4 %reduce-scatter.19.cloned.1.call-done = bf16[512,512]{1,0:T(8,128)(2,1)} async-done(((bf16[512,2048]{1,0:T(8,128)(2,1)}), bf16[512,512]{1,0:T(8,128)(2,1)}) %reduce-scatter.19.cloned.1.call-update) | async-done | bytes 524304 | tf_op jit(solution)/shard_map/reduce_scatter | solution.py:312
  638.1 4.2 add_bitcast_fusion
  642.3 3.0 copy.252
  646.7 39.8 %all-reduce = (f32[12,512]{1,0:T(8,128)S(1)}, f32[49,16]{0,1:T(8,128)S(1)}) all-reduce(f32[12,512]{1,0:T(8,128)S(1)} %broadcast_multiply_fusion, f32[49,16]{0,1:T(8,128)} %convolution_multiply_fusion.2), channel_id=1, replica_groups=mesh['slab'=4,'clip'=8] {'slab','clip'}, use_global_device_ids=true, to_apply=%region_36.37 | all-reduce | flops 6928 | bytes 55424 | tf_op jit(solution)/shard_map/psum | solution.py:325
  689.3 11.6 %reduce-scatter.17.cloned.1.call-done = f32[64,128]{1,0:T(8,128)} async-done(((f32[512,128]{1,0:T(8,128)}), f32[64,128]{1,0:T(8,128)}) %reduce-scatter.17.cloned.1.call-update) | async-done | bytes 32784 | tf_op jit(solution)/shard_map/reduce_scatter | solution.py:321
  702.3 63.6 %reduce-scatter.15.cloned.1.call-done = f32[64,384]{1,0:T(8,128)} async-done(((f32[512,384]{1,0:T(8,128)}), f32[64,384]{1,0:T(8,128)}) %reduce-scatter.15.cloned.1.call-update) | async-done | bytes 98320 | tf_op jit(solution)/shard_map/reduce_scatter | solution.py:320
  767.7 64.1 %reduce-scatter.21.cloned.1.call-done = f32[64,512]{1,0:T(8,128)} async-done(((f32[512,512]{1,0:T(8,128)}), f32[64,512]{1,0:T(8,128)}) %reduce-scatter.21.cloned.1.call-update) | async-done | bytes 131088 | tf_op jit(solution)/shard_map/reduce_scatter | solution.py:322
  (266 shorter events, 76.5 us)
Async XLA Ops:
  7.2 110.2 %copy-start.15 = (bf16[1,1,1024,512]{3,2,1,0:T(8,128)(2,1)S(1)}, bf16[1,1,1024,512]{3,2,1,0:T(8,128)(2,1)}, u32[]{:S(2)}) copy-start(bf16[1,1,1024,512]{3,2,1,0:T(8,128)(2,1)} %param.21) | copy-start | bytes 3145732
  7.2 115.6 %all-gather.4.cloned.1.call-start = ((), (), s32[]{:S(2)}) async-start(), calls=%async_computation.8 | async-start | bytes 1966080 | tf_op jit(solution)/shard_map/all_gather | solution.py:171
  8.2 110.9 %copy-start.38 = (f32[49,16]{0,1:T(8,128)S(1)}, f32[49,16]{0,1:T(8,128)}, u32[]{:S(2)}) copy-start(f32[49,16]{0,1:T(8,128)} %param.39) | copy-start | bytes 9412
  43.1 77.4 %copy-start.16 = (bf16[1,1,1024,512]{3,2,1,0:T(8,128)(2,1)S(1)}, bf16[1,1,1024,512]{3,2,1,0:T(8,128)(2,1)}, u32[]{:S(2)}) copy-start(bf16[1,1,1024,512]{3,2,1,0:T(8,128)(2,1)} %param.22) | copy-start | bytes 3145732
  43.1 194.9 %all-gather.6.cloned.1.call-start = ((), (), s32[]{:S(2)}) async-start(), calls=%async_computation.9 | async-start | bytes 2621440 | tf_op jit(solution)/shard_map/all_gather | solution.py:173
  77.5 227.5 %reduce-scatter.29.cloned.1.call-start = ((), (), s32[]{:S(2)}) async-start(), calls=%async_computation.18 | async-start | bytes 2621440
  82.5 40.3 %copy-start.32 = (f32[1,512]{1,0:T(1,128)}, f32[1,512]{1,0:T(1,128)S(1)}, u32[]{:S(2)}) copy-start(f32[1,512]{1,0:T(1,128)S(1)} %get-tuple-element.207) | copy-start | bytes 6148
  117.9 117.5 %copy-start = (bf16[1,1,1024,512]{2,3,1,0:T(8,128)(2,1)}, bf16[1,1,1024,512]{2,3,1,0:T(8,128)(2,1)S(1)}, u32[]{:S(2)}) copy-start(bf16[1,1,1024,512]{2,3,1,0:T(8,128)(2,1)S(1)} %copy.217) | copy-start | bytes 3145732
  118.0 4.6 copy-start.53
  118.0 4.9 copy-start.48
  118.2 9.8 %copy-start.26 = (f32[1024]{0:T(1024)}, f32[1024]{0:T(1024)S(1)}, u32[]{:S(2)}) copy-start(f32[1024]{0:T(1024)S(1)} %broadcast_multiply_fusion.2) | copy-start | bytes 12292
  118.5 9.4 %copy-start.28 = (f32[1024]{0:T(1024)}, f32[1024]{0:T(1024)S(1)}, u32[]{:S(2)}) copy-start(f32[1024]{0:T(1024)S(1)} %fusion.86) | copy-start | bytes 12292
  118.7 114.9 %copy-start.41 = (s32[8]{0:T(128)}, s32[8]{0:T(128)S(1)}, u32[]{:S(2)}) copy-start(s32[8]{0:T(128)S(1)} %fusion.89) | copy-start | bytes 100
  118.7 9.2 %copy-start.40 = (s32[1024]{0:T(1024)}, s32[1024]{0:T(1024)S(1)}, u32[]{:S(2)}) copy-start(s32[1024]{0:T(1024)S(1)} %pad_clamp_fusion.1) | copy-start | bytes 12292
  122.6 102.9 %copy-start.43 = (s32[128]{0:T(128)}, s32[128]{0:T(128)S(1)}, u32[]{:S(2)}) copy-start(s32[128]{0:T(128)S(1)} %fusion.88) | copy-start | bytes 1540
  130.4 9.3 %collective-permute-start = (bf16[8,8,1536]{2,1,0:T(8,128)(2,1)S(1)}, bf16[8,8,1536]{2,1,0:T(8,128)(2,1)S(1)}, u32[]{:S(2)}, u32[]{:S(2)}) collective-permute-start(bf16[8,8,1536]{2,1,0:T(8,128)(2,1)S(1)} %gather_fusion), channel_id=1, source_target_pairs={{8,0},{16,8},{24,16},{0,24},{9,1},{17,9},{25,17},{1,25},{10,2},{18... | collective-permute-start | bytes 589832 | tf_op jit(solution)/shard_map/ppermute | solution.py:27
  208.9 6.2 copy-start.17
  225.4 10.0 %copy-start.50 = (f32[1,512]{1,0:T(1,128)S(1)}, f32[1,512]{1,0:T(1,128)}, u32[]{:S(2)}) copy-start(f32[1,512]{1,0:T(1,128)} %get-tuple-element.203) | copy-start | bytes 6148
  229.8 3.7 collective-permute-start.1
  235.4 2.6 copy-start.39
  235.4 2.6 copy-start.46
  237.6 212.1 %copy-start.3 = (f32[1024,512]{0,1:T(8,128)}, f32[1024,512]{0,1:T(8,128)S(1)}, u32[]{:S(2)}) copy-start(f32[1024,512]{0,1:T(8,128)S(1)} %get-tuple-element.215) | copy-start | bytes 6291460
  238.0 27.2 %copy-start.10 = (bf16[1,1,1024,512]{2,3,1,0:T(8,128)(2,1)S(1)}, bf16[1,1,1024,512]{2,3,1,0:T(8,128)(2,1)}, u32[]{:S(2)}) copy-start(bf16[1,1,1024,512]{2,3,1,0:T(8,128)(2,1)} %copy.232) | copy-start | bytes 3145732
  273.0 99.8 %copy-start.22 = (f32[256,128]{1,0:T(8,128)S(1)}, f32[256,128]{1,0:T(8,128)}, u32[]{:S(2)}) copy-start(f32[256,128]{1,0:T(8,128)} %param.27) | copy-start | bytes 393220
  273.0 99.8 %copy-start.23 = (f32[256,128]{1,0:T(8,128)S(1)}, f32[256,128]{1,0:T(8,128)}, u32[]{:S(2)}) copy-start(f32[256,128]{1,0:T(8,128)} %param.31) | copy-start | bytes 393220
  273.0 99.7 %reduce-scatter.23.cloned.1.call-start = ((), (), s32[]{:S(2)}) async-start(), calls=%async_computation.15 | async-start | bytes 1179648 | tf_op jit(solution)/shard_map/reduce_scatter | solution.py:323
  309.1 121.0 %all-gather.8.cloned.1.call-start = ((), (), s32[]{:S(2)}) async-start(), calls=%async_computation.10 | async-start | bytes 2621440 | tf_op jit(solution)/shard_map/all_gather | solution.py:174
  407.8 170.7 %reduce-scatter.27.cloned.1.call-start = ((), (), s32[]{:S(2)}) async-start(), calls=%async_computation.17 | async-start | bytes 655360
  430.1 9.5 %copy-start.54 = (bf16[512,2048]{1,0:T(8,128)(2,1)S(1)}, bf16[512,2048]{1,0:T(8,128)(2,1)}, u32[]{:S(2)}) copy-start(bf16[512,2048]{1,0:T(8,128)(2,1)} %all-gather.6.cloned.1.call-done) | copy-start | bytes 6291460
  439.6 4.3 copy-start.56
  446.8 3.0 copy-start.5
  451.7 2.9 copy-start.14
  454.3 3.9 collective-permute-start.2
  458.2 143.7 %reduce-scatter.25.cloned.1.call-start = ((), (), s32[]{:S(2)}) async-start(), calls=%async_computation.16 | async-start | bytes 1966080
  460.6 4.8 copy-start.18
  465.4 9.2 %copy-start.11 = (bf16[64,16,16,32]{3,2,1,0:T(8,128)(2,1)S(1)}, bf16[64,16,16,32]{3,2,1,0:T(8,128)(2,1)}, u32[]{:S(2)}) copy-start(bf16[64,16,16,32]{3,2,1,0:T(8,128)(2,1)} %reshape_reshape.7) | copy-start | bytes 3145732
  485.3 7.6 copy-start.7
  492.9 4.3 copy-start.8
  497.2 3.1 copy-start.12
  538.9 3.6 copy-start.44
  556.6 5.2 copy-start.42
  556.6 7.9 copy-start.1
  556.7 7.9 copy-start.27
  556.7 7.9 copy-start.29
  556.7 7.8 copy-start.33
  556.7 7.8 copy-start.49
  556.7 5.1 collective-permute-start.3
  569.5 2.9 copy-start.4
  569.5 2.9 copy-start.35
  569.5 2.9 copy-start.47
  572.3 8.0 copy-start.45
  572.3 63.6 %reduce-scatter.19.cloned.1.call-start = ((), (), s32[]{:S(2)}) async-start(), calls=%async_computation.13 | async-start | bytes 2621440 | tf_op jit(solution)/shard_map/reduce_scatter | solution.py:312
  578.4 122.4 %reduce-scatter.17.cloned.1.call-start = ((), (), s32[]{:S(2)}) async-start(), calls=%async_computation.12 | async-start | bytes 294912 | tf_op jit(solution)/shard_map/reduce_scatter | solution.py:321
  580.3 185.7 %reduce-scatter.15.cloned.1.call-start = ((), (), s32[]{:S(2)}) async-start(), calls=%async_computation.11 | async-start | bytes 884736 | tf_op jit(solution)/shard_map/reduce_scatter | solution.py:320
  587.0 17.2 %copy-start.52 = (s32[256]{0:T(256)S(1)}, s32[256]{0:T(256)}, u32[]{:S(2)}) copy-start(s32[256]{0:T(256)} %copy-done.51) | copy-start | bytes 3076
  587.0 18.0 %copy-start.55 = (bf16[512,1536]{1,0:T(8,128)(2,1)S(1)}, bf16[512,1536]{1,0:T(8,128)(2,1)}, u32[]{:S(2)}) copy-start(bf16[512,1536]{1,0:T(8,128)(2,1)} %all-gather.4.cloned.1.call-done) | copy-start | bytes 4718596
  604.1 227.7 %reduce-scatter.21.cloned.1.call-start = ((), (), s32[]{:S(2)}) async-start(), calls=%async_computation.14 | async-start | bytes 1179648 | tf_op jit(solution)/shard_map/reduce_scatter | solution.py:322
  642.3 3.1 copy-start.9
  642.3 3.6 copy-start.36
  642.3 3.6 copy-start.37
  642.3 58.6 %copy-start.25 = (f32[64,128]{1,0:T(8,128)S(1)}, f32[64,128]{1,0:T(8,128)}, u32[]{:S(2)}) copy-start(f32[64,128]{1,0:T(8,128)} %param.25) | copy-start | bytes 98308
  642.3 123.7 %copy-start.21 = (f32[64,384]{1,0:T(8,128)S(1)}, f32[64,384]{1,0:T(8,128)}, u32[]{:S(2)}) copy-start(f32[64,384]{1,0:T(8,128)} %param.24) | copy-start | bytes 294916
  642.3 189.5 %copy-start.20 = (f32[64,512]{1,0:T(8,128)S(1)}, f32[64,512]{1,0:T(8,128)}, u32[]{:S(2)}) copy-start(f32[64,512]{1,0:T(8,128)} %param.26) | copy-start | bytes 393220
  642.3 189.5 %copy-start.24 = (f32[64,512]{1,0:T(8,128)S(1)}, f32[64,512]{1,0:T(8,128)}, u32[]{:S(2)}) copy-start(f32[64,512]{1,0:T(8,128)} %param.30) | copy-start | bytes 393220
  (9 other events, 14.7 us)
Sparse Core Ops, SparseCore 0:
  43.2 20.6 all-gather.3
  77.6 23.9 all-gather.5
  273.1 31.7 reduce-scatter.28
  309.2 63.4 reduce-scatter.22
  407.9 22.1 all-gather.7
  458.3 22.7 reduce-scatter.26
  572.4 29.4 reduce-scatter.24
  604.4 31.4 reduce-scatter.18
  639.6 61.2 reduce-scatter.16
  704.4 61.5 reduce-scatter.14
  769.4 62.3 reduce-scatter.20
where the time goes:
time: 847 us; the launch traced here: 840 us
  waiting for transfers between devices  295 us (35%)
  blocking collectives  181 us (21%)
  local copies, waits for them, and re-layouts  167 us (20%)
  matrix products  121 us (14%)
  other arithmetic  56.8 us (7%)
  between operations  17.8 us (2%)
    reduce_scatter x1, waiting for transfers between devices, shards(): lax.psum_scatter(part_sums[2], 'clip', scatter_dimension=0, tiled=True)  64.1 us
    reduce_scatter x1, waiting for transfers between devices, shards(): lax.psum_scatter(part_sums[0], 'clip', scatter_dimension=0, tiled=True)  63.6 us
    reduce_scatter x1, waiting for transfers between devices, shards(): lax.psum_scatter(part_sums[3], 'clip', scatter_dimension=0, tiled=True)  63.6 us
    unnamed x14, waiting for transfers between devices  44.4 us
    psum x1, blocking collectives, shards(): lax.psum((vector_grad * grad_scale, table_grad * grad_scale), ('slab', 'c...  39.8 us
    all_gather x1, blocking collectives, shards(): lax.all_gather(qkv_weight.astype(jnp.bfloat16), 'clip', axis=0, tiled=True)  34.8 us
    all_gather x1, blocking collectives, shards(): lax.all_gather(up_weight.astype(jnp.bfloat16), 'clip', axis=0, tiled=True)  33.3 us
    all_gather x1, blocking collectives, shards(): lax.all_gather(down_weight.astype(jnp.bfloat16), 'clip', axis=0, tiled=True)  33.3 us
  transfers between devices with their start and end apart: 15, of which 10 were waited for; matrix products, arithmetic and copies ran while one was open for 33% of the time, Pallas kernels for 0%

commit v1 on v0

--- a/solution.py
+++ b/solution.py
@@ -1,6 +1,11 @@
+import functools
+import itertools
+
 import jax
 import jax.numpy as jnp
 from jax import lax
+from jax.experimental import pallas as pl
+from jax.experimental.pallas import tpu as pltpu
 from jax.sharding import PartitionSpec as P
 
 HEADS = 16
@@ -111,6 +116,365 @@
     fix_second = 1.0 - beta_second**STEP
     update = first / fix_first / (jnp.sqrt(second / fix_second) + adam_epsilon)
     return (weight - rate * (update + decay * weight), first, second)
+
+
+MESH = pl.DeviceIdType.MESH
+
+
+class Links:
+    def __init__(self, send_sems, recv_sems):
+        self.send_sems, self.recv_sems = send_sems, recv_sems
+        self.count, self.started = 0, []
+
+    def send(self, source, target, device):
+        copy = pltpu.make_async_remote_copy(
+            src_ref=source,
+            dst_ref=target,
+            send_sem=self.send_sems.at[self.count],
+            recv_sem=self.recv_sems.at[self.count],
+            device_id=device,
+            device_id_type=MESH,
+        )
+        copy.start()
+        self.count += 1
+        self.started.append(copy)
+        return copy
+
+    def drain(self):
+        for copy in self.started:
+            copy.wait_send()
+
+
+class Place:
+    def __init__(self, clip_size):
+        self.slab, self.clip = lax.axis_index("slab"), lax.axis_index("clip")
+        self.x, self.core = self.slab // 2, self.slab % 2
+        self.z, self.y = self.clip // 2, self.clip % 2
+        self.depth = clip_size // 2
+        self.over_core = (self.x * 2 + 1 - self.core, self.clip)
+        self.over_x = ((1 - self.x) * 2 + self.core, self.clip)
+        self.over_y = (self.slab, self.z * 2 + 1 - self.y)
+        self.x_slab = (1 - self.x) * 2 + self.core
+        self.core_slab = self.x * 2 + 1 - self.core
+
+    def z_at(self, step):
+        return lax.rem(self.z + step, self.depth)
+
+    def over_z(self, step):
+        return (self.slab, self.z_at(step) * 2 + self.y)
+
+    def greet(self):
+        barrier = pltpu.get_barrier_semaphore()
+        partners = [self.over_core, self.over_x, self.over_y]
+        partners += [self.over_z(step) for step in range(1, self.depth)]
+        for partner in partners:
+            pl.semaphore_signal(barrier, inc=1, device_id=partner, device_id_type=MESH)
+        pl.semaphore_wait(barrier, len(partners))
+
+
+def wait_all(copies):
+    for copy in copies:
+        copy.wait_recv()
+
+
+class Gather:
+    def __init__(self, place, links, whole, width):
+        self.place, self.links, self.whole, self.width = place, links, whole, width
+
+    def columns(self, slab):
+        return pl.ds(pl.multiple_of(slab * self.width, 128), self.width)
+
+    def move(self, device, *index):
+        block = self.whole.at[index]
+        return self.links.send(block, block, device)
+
+    def begin(self, master):
+        place = self.place
+        rows = self.whole.shape[3]
+        for half in range(2):
+            self.whole[place.z, place.y, half, :, self.columns(place.slab)] = master[
+                half * rows : (half + 1) * rows, :
+            ].astype(jnp.bfloat16)
+        self.over_z = [
+            [
+                self.move(
+                    place.over_z(step), place.z, place.y, half, slice(None), self.columns(place.slab)
+                )
+                for step in range(1, place.depth)
+            ]
+            for half in range(2)
+        ]
+
+    def second(self):
+        place, every = self.place, slice(None)
+        mine = self.columns(place.slab)
+        wait_all(self.over_z[0])
+        self.first_x = self.move(place.over_x, every, place.y, 0, every, mine)
+        wait_all(self.over_z[1])
+        self.first_y = self.move(place.over_y, every, place.y, 1, every, mine)
+
+    def third(self):
+        place, every = self.place, slice(None)
+        mine, across = self.columns(place.slab), self.columns(place.x_slab)
+        self.first_x.wait_recv()
+        self.last_y = [
+            self.move(place.over_y, every, place.y, 0, every, mine),
+            self.move(place.over_y, every, place.y, 0, every, across),
+        ]
+        self.first_y.wait_recv()
+        self.last_x = [self.move(place.over_x, every, every, 1, every, mine)]
+
+    def fourth(self):
+        place, every = self.place, slice(None)
+        mine, across = self.columns(place.slab), self.columns(place.x_slab)
+        wait_all(self.last_y)
+        self.over_core = [
+            self.move(place.over_core, every, every, 0, every, mine),
+            self.move(place.over_core, every, every, 0, every, across),
+        ]
+        wait_all(self.last_x)
+        self.over_core += [
+            self.move(place.over_core, every, every, 1, every, mine),
+            self.move(place.over_core, every, every, 1, every, across),
+        ]
+
+    def end(self):
+        wait_all(self.over_core)
+
+
+def gather_copies(place, clip_size):
+    return 2 * (place - 1) + 9
+
+
+def add_into(held, index, arrived, arrived_index):
+    lead = arrived.shape[len(arrived_index) : -2]
+    for at in itertools.product(*[range(n) for n in lead]):
+        total = held[index + at].astype(jnp.float32) + arrived[arrived_index + at].astype(jnp.float32)
+        held[index + at] = total.astype(jnp.bfloat16)
+
+
+class Scatter:
+    def __init__(self, place, links, held, from_core, first_y, first_x, last_x, last_y, from_z):
+        self.place, self.links, self.held = place, links, held
+        self.from_core, self.first_y, self.first_x = from_core, first_y, first_x
+        self.last_x, self.last_y, self.from_z = last_x, last_y, from_z
+
+    def begin(self):
+        place = self.place
+        self.copies = [
+            self.links.send(
+                self.held.at[2 * x + 1 - place.core], self.from_core.at[x], place.over_core
+            )
+            for x in range(2)
+        ]
+
+    def second(self):
+        place = self.place
+        for x in range(2):
+            self.copies[x].wait_recv()
+            add_into(self.held, (2 * x + place.core,), self.from_core, (x,))
+        self.copies_a = [
+            self.links.send(
+                self.held.at[2 * x + place.core, 1 - place.y, 0], self.first_y.at[x], place.over_y
+            )
+            for x in range(2)
+        ]
+        self.copies_b = [
+            self.links.send(
+                self.held.at[place.x_slab, y, 1], self.first_x.at[y], place.over_x
+            )
+            for y in range(2)
+        ]
+
+    def third(self):
+        place = self.place
+        for x in range(2):
+            self.copies_a[x].wait_recv()
+            add_into(self.held, (2 * x + place.core, place.y, 0), self.first_y, (x,))
+        self.copy_a = self.links.send(
+            self.held.at[place.x_slab, place.y, 0], self.last_x, place.over_x
+        )
+        for y in range(2):
+            self.copies_b[y].wait_recv()
+            add_into(self.held, (place.slab, y, 1), self.first_x, (y,))
+        self.copy_b = self.links.send(
+            self.held.at[place.slab, 1 - place.y, 1], self.last_y, place.over_y
+        )
+
+    def fourth(self):
+        place = self.place
+        self.copies = []
+        for half, copy, arrived in ((0, self.copy_a, self.last_x), (1, self.copy_b, self.last_y)):
+            copy.wait_recv()
+            add_into(self.held, (place.slab, place.y, half), arrived, ())
+            self.copies.append([
+                self.links.send(
+                    self.held.at[place.slab, place.y, half, place.z_at(step)],
+                    self.from_z.at[half, step - 1],
+                    place.over_z(step),
+                )
+                for step in range(1, place.depth)
+            ])
+
+    def end(self):
+        place, parts = self.place, []
+        for half in range(2):
+            total = self.held[place.slab, place.y, half, place.z].astype(jnp.float32)
+            for step in range(1, place.depth):
+                self.copies[half][step - 1].wait_recv()
+                total += self.from_z[half, step - 1].astype(jnp.float32)
+            parts.append(total)
+        return parts
+
+
+class Small:
+    def __init__(self, place, links, held, arrived, line):
+        self.place, self.links, self.held = place, links, held
+        self.arrived, self.line = arrived, line
+
+    def begin(self):
+        self.copy = self.links.send(self.held.at[0], self.arrived.at[0], self.place.over_core)
+
+    def second(self):
+        self.copy.wait_recv()
+        self.held[1] = self.held[0] + self.arrived[0]
+        self.copy = self.links.send(self.held.at[1], self.arrived.at[1], self.place.over_x)
+
+    def third(self):
+        self.copy.wait_recv()
+        self.held[2] = self.held[1] + self.arrived[1]
+        self.copy = self.links.send(self.held.at[2], self.arrived.at[2], self.place.over_y)
+
+    def fourth(self):
+        place = self.place
+        self.copy.wait_recv()
+        self.line[place.z] = self.held[2] + self.arrived[2]
+        self.copies = [
+            self.links.send(self.line.at[place.z], self.line.at[place.z], place.over_z(step))
+            for step in range(1, place.depth)
+        ]
+
+    def end(self):
+        wait_all(self.copies)
+        total = self.line[0]
+        for z in range(1, self.place.depth):
+            total += self.line[z]
+        return total
+
+
+def gather_kernel(clip_size, *refs):
+    masters, wholes = refs[:4], refs[4:8]
+    place, links = Place(clip_size), Links(*refs[8:])
+    place.greet()
+    flows = [
+        Gather(place, links, whole, master.shape[1]) for master, whole in zip(masters, wholes)
+    ]
+    for stage in ("begin", "second", "third", "fourth", "end"):
+        for position, flow in enumerate(flows):
+            if stage == "begin":
+                flow.begin(masters[position])
+            else:
+                getattr(flow, stage)()
+    links.drain()
+
+
+def gather_all(masters, clip_size):
+    vmem = pl.BlockSpec(memory_space=pltpu.VMEM)
+    depth = clip_size // 2
+    shapes = [
+        jax.ShapeDtypeStruct((depth, 2, 2, m.shape[0] // 2, 4 * m.shape[1]), jnp.bfloat16)
+        for m in masters
+    ]
+    copies = 4 * (2 * (depth - 1) + 9)
+    wholes = pl.pallas_call(
+        functools.partial(gather_kernel, clip_size),
+        out_shape=shapes,
+        in_specs=[vmem] * 4,
+        out_specs=[vmem] * 4,
+        scratch_shapes=[pltpu.SemaphoreType.DMA((copies,)), pltpu.SemaphoreType.DMA((copies,))],
+        compiler_params=pltpu.CompilerParams(
+            collective_id=0, has_side_effects=True, vmem_limit_bytes=48 << 20
+        ),
+        name="gather_weights",
+    )(*masters)
+    return [w.reshape(-1, w.shape[-1]) for w in wholes]
+
+
+def scatter_kernel(clip_size, shapes, *refs):
+    small_in, helds_in = refs[0], refs[1:5]
+    small_out, outs = refs[5], refs[6:10]
+    rest = list(refs[10:])
+    place = Place(clip_size)
+    links = Links(rest.pop(0), rest.pop(0))
+    place.greet()
+    small = Small(place, links, rest.pop(0), rest.pop(0), rest.pop(0))
+    small.held[0] = small_in[...]
+    flows = []
+    loads = rest.pop(0)
+    for position, source in enumerate(helds_in):
+        held = rest.pop(0)
+        load = pltpu.make_async_copy(source, held, loads.at[position])
+        load.start()
+        flows.append(Scatter(place, links, held, *[rest.pop(0) for _ in range(6)]))
+        flows[-1].load = load
+    for flow in flows:
+        flow.load.wait()
+    flows = [small] + flows
+    for stage in ("begin", "second", "third", "fourth"):
+        for flow in flows:
+            getattr(flow, stage)()
+    small_out[...] = small.end()
+    for flow, out in zip(flows[1:], outs):
+        first, last = flow.end()
+        rows = first.shape[0]
+        out[:rows, :] = first
+        out[rows:, :] = last
+    links.drain()
+
+
+def scatter_buffers(shape):
+    slabs, _, _, depth, rows, columns = shape
+    return [
+        pltpu.VMEM((2, 2, 2, depth, rows, columns), jnp.bfloat16),
+        pltpu.VMEM((2, depth, rows, columns), jnp.bfloat16),
+        pltpu.VMEM((2, depth, rows, columns), jnp.bfloat16),
+        pltpu.VMEM((depth, rows, columns), jnp.bfloat16),
+        pltpu.VMEM((depth, rows, columns), jnp.bfloat16),
+        pltpu.VMEM((2, depth - 1, rows, columns), jnp.bfloat16),
+    ]
+
+
+def scatter_all(small, grads, clip_size):
+    vmem = pl.BlockSpec(memory_space=pltpu.VMEM)
+    depth = clip_size // 2
+    helds = []
+    for grad in grads:
+        rows, columns = grad.shape[0] // clip_size // 2, grad.shape[1] // 4
+        held = grad.reshape(depth, 2, 2, rows, 4, columns).transpose(4, 1, 2, 0, 3, 5)
+        helds.append(held.astype(jnp.bfloat16))
+    copies = 4 * (2 + 4 + 2 + 2 * (depth - 1)) + 3 + depth - 1
+    scratch = [
+        pltpu.SemaphoreType.DMA((copies,)),
+        pltpu.SemaphoreType.DMA((copies,)),
+        pltpu.VMEM((3,) + small.shape, jnp.float32),
+        pltpu.VMEM((3,) + small.shape, jnp.float32),
+        pltpu.VMEM((depth,) + small.shape, jnp.float32),
+        pltpu.SemaphoreType.DMA((4,)),
+    ]
+    for held in helds:
+        scratch += [pltpu.VMEM(held.shape, held.dtype)] + scatter_buffers(held.shape)
+    return pl.pallas_call(
+        functools.partial(scatter_kernel, clip_size, [h.shape for h in helds]),
+        out_shape=[jax.ShapeDtypeStruct(small.shape, jnp.float32)]
+        + [jax.ShapeDtypeStruct((2 * h.shape[4], h.shape[5]), jnp.float32) for h in helds],
+        in_specs=[vmem] + [pl.BlockSpec(memory_space=pl.ANY)] * 4,
+        out_specs=[vmem] * 5,
+        scratch_shapes=scratch,
+        compiler_params=pltpu.CompilerParams(
+            collective_id=1, has_side_effects=True, vmem_limit_bytes=48 << 20
+        ),
+        name="scatter_grads",
+    )(small, *helds)
 
 
 def shards(
@@ -161,18 +525,24 @@
     )
     used_rows = jnp.sum(lengths) // slab_count
     live_rows = (jnp.arange(tok_count) // BINS < used_rows).astype(jnp.float32)[:, None]
-    part_copies = (
-        lax.all_gather(qkv_weight.astype(jnp.bfloat16), "clip", axis=0, tiled=True),
-        lax.all_gather(proj_weight.astype(jnp.bfloat16), "clip", axis=0, tiled=True),
-        lax.all_gather(up_weight.astype(jnp.bfloat16), "clip", axis=0, tiled=True),
-        lax.all_gather(down_weight.astype(jnp.bfloat16), "clip", axis=0, tiled=True),
-    )
-    copies = (
-        lax.all_gather(part_copies[0], "slab", axis=1, tiled=True),
-        lax.all_gather(part_copies[1], "slab", axis=1, tiled=True),
-        lax.all_gather(part_copies[2], "slab", axis=1, tiled=True),
-        lax.all_gather(part_copies[3], "slab", axis=1, tiled=True),
-    )
+    masters = (qkv_weight, proj_weight, up_weight, down_weight)
+    clip_size = lax.axis_size("clip")
+    aligned = slab_count == 4 and clip_size % 2 == 0 and all(m.shape[0] % 32 == 0 for m in masters)
+    if aligned:
+        copies = gather_all(masters, clip_size)
+    else:
+        part_copies = (
+            lax.all_gather(qkv_weight.astype(jnp.bfloat16), "clip", axis=0, tiled=True),
+            lax.all_gather(proj_weight.astype(jnp.bfloat16), "clip", axis=0, tiled=True),
+            lax.all_gather(up_weight.astype(jnp.bfloat16), "clip", axis=0, tiled=True),
+            lax.all_gather(down_weight.astype(jnp.bfloat16), "clip", axis=0, tiled=True),
+        )
+        copies = (
+            lax.all_gather(part_copies[0], "slab", axis=1, tiled=True),
+            lax.all_gather(part_copies[1], "slab", axis=1, tiled=True),
+            lax.all_gather(part_copies[2], "slab", axis=1, tiled=True),
+            lax.all_gather(part_copies[3], "slab", axis=1, tiled=True),
+        )
     qkv_copy, proj_copy, up_copy, down_copy = copies
     attn_input = affine_norm(inputs, vectors[0], vectors[1]).astype(jnp.bfloat16)
     bias_row = jnp.concatenate([vectors[2], jnp.zeros_like(vectors[2]), vectors[3]])
@@ -302,27 +672,39 @@
         0,
     )
     grad_scale = float(tok_count * slab_count * lax.axis_size("clip")) ** (-0.5)
-    part_sums = (
-        lax.psum_scatter(
-            (qkv_w_grad * grad_scale).astype(jnp.bfloat16), "slab", scatter_dimension=1, tiled=True
-        ).astype(jnp.float32),
-        lax.psum_scatter(
-            (proj_grad * grad_scale).astype(jnp.bfloat16), "slab", scatter_dimension=1, tiled=True
-        ).astype(jnp.float32),
-        lax.psum_scatter(
-            (up_grad * grad_scale).astype(jnp.bfloat16), "slab", scatter_dimension=1, tiled=True
-        ).astype(jnp.float32),
-        lax.psum_scatter(
-            (down_grad * grad_scale).astype(jnp.bfloat16), "slab", scatter_dimension=1, tiled=True
-        ).astype(jnp.float32),
-    )
-    owned = (
-        lax.psum_scatter(part_sums[0], "clip", scatter_dimension=0, tiled=True),
-        lax.psum_scatter(part_sums[1], "clip", scatter_dimension=0, tiled=True),
-        lax.psum_scatter(part_sums[2], "clip", scatter_dimension=0, tiled=True),
-        lax.psum_scatter(part_sums[3], "clip", scatter_dimension=0, tiled=True),
-    )
-    small_sums = lax.psum((vector_grad * grad_scale, table_grad * grad_scale), ("slab", "clip"))
+    if aligned:
+        size = vector_grad.size + table_grad.size
+        flat = jnp.concatenate([vector_grad.reshape(-1), table_grad.reshape(-1)]) * grad_scale
+        flat = jnp.pad(flat, (0, -size % (8 * width))).reshape(-1, width)
+        grads = [g * grad_scale for g in (qkv_w_grad, proj_grad, up_grad, down_grad)]
+        summed, *owned = scatter_all(flat, grads, clip_size)
+        summed = summed.reshape(-1)
+        small_sums = (
+            summed[: vector_grad.size].reshape(vector_grad.shape),
+            summed[vector_grad.size : size].reshape(table_grad.shape),
+        )
+    else:
+        part_sums = (
+            lax.psum_scatter(
+                (qkv_w_grad * grad_scale).astype(jnp.bfloat16), "slab", scatter_dimension=1, tiled=True
+            ).astype(jnp.float32),
+            lax.psum_scatter(
+                (proj_grad * grad_scale).astype(jnp.bfloat16), "slab", scatter_dimension=1, tiled=True
+            ).astype(jnp.float32),
+            lax.psum_scatter(
+                (up_grad * grad_scale).astype(jnp.bfloat16), "slab", scatter_dimension=1, tiled=True
+            ).astype(jnp.float32),
+            lax.psum_scatter(
+                (down_grad * grad_scale).astype(jnp.bfloat16), "slab", scatter_dimension=1, tiled=True
+            ).astype(jnp.float32),
+        )
+        owned = (
+            lax.psum_scatter(part_sums[0], "clip", scatter_dimension=0, tiled=True),
+            lax.psum_scatter(part_sums[1], "clip", scatter_dimension=0, tiled=True),
+            lax.psum_scatter(part_sums[2], "clip", scatter_dimension=0, tiled=True),
+            lax.psum_scatter(part_sums[3], "clip", scatter_dimension=0, tiled=True),
+        )
+        small_sums = lax.psum((vector_grad * grad_scale, table_grad * grad_scale), ("slab", "clip"))
     qkv_new, qkv_m_new, qkv_v_new = adamw(
         qkv_weight, qkv_m, qkv_v, owned[0], rate_matrix, weight_decay
     )

time: 847 us -> 483 us (0.57)
  waiting for transfers between devices: 295 us -> 5.73 us
  blocking collectives: 181 us -> 0 us
  Pallas kernels: 0 us -> 96 us
  local copies, waits for them, and re-layouts: 167 us -> 216 us
  other arithmetic: 56.8 us -> 41.1 us
  between operations: 17.8 us -> 4.59 us
  matrix products: 121 us -> 111 us
    reduce_scatter x5 -> x0, waiting for transfers between devices: 224 us -> none  [the longest x1 64.1 us: shards(): lax.psum_scatter(part_sums[2], 'clip', scatter_dimension=0, tiled=True)]
    all_gather x5 -> x0, blocking collectives: 141 us -> none  [the longest x1 34.8 us: shards(): lax.all_gather(qkv_weight.astype(jnp.bfloat16), 'clip', axis=0, tiled=True)]
    pallas_call x0 -> x2, Pallas kernels: none -> 96 us  [the longest x1 49.3 us: gather_all(): pl.pallas_call(functools.partial(gather_kernel, clip_size), out_shape=sha...]
    unnamed x14 -> x0, waiting for transfers between devices: 44.4 us -> none
    psum x1 -> x0, blocking collectives: 39.8 us -> none  [shards(): lax.psum((vector_grad * grad_scale, table_grad * grad_scale), ('slab', 'c...]
    all_gather x3 -> x0, waiting for transfers between devices: 22.3 us -> none  [the longest x1 22.2 us: shards(): lax.all_gather(part_copies[3], 'slab', axis=1, tiled=True)]
    convert_element_type x0 -> x8, local copies, waits for them, and re-layouts: none -> 19.7 us  [scatter_all(): helds.append(held.astype(jnp.bfloat16))]
    scatter x2, local copies, waits for them, and re-layouts: 16.7 us -> 34.2 us  [from_windows(): blank.at[source.reshape(-1)]]
  transfers between devices with their start and end apart: 15 -> 4, of which waited for: 10 -> 2; matrix products, arithmetic and copies ran while one was open for 33% -> 7% of each run, Pallas kernels for 0% -> 0%
where the time goes in v1:
time: 483 us; the launch traced here: 476 us
  local copies, waits for them, and re-layouts  216 us (45%)
  matrix products  111 us (23%)
  Pallas kernels  96 us (20%)
  other arithmetic  41.1 us (9%)
  waiting for transfers between devices  5.73 us (1%)
    pallas_call x1, Pallas kernels, gather_all(): pl.pallas_call(functools.partial(gather_kernel, clip_size), out_shape=sha...  49.3 us
    pallas_call x1, Pallas kernels, scatter_all(): pl.pallas_call(functools.partial(scatter_kernel, clip_size, [h.shape for...  46.7 us
    scatter x2, local copies, waits for them, and re-layouts, from_windows(): blank.at[source.reshape(-1)]  34.2 us
    dot_general x1, matrix products, shards(): jnp.dot(mlp_input, up_copy, preferred_element_type=jnp.float32)  22.9 us
    concatenate x3, local copies, waits for them, and re-layouts, shards(): jnp.concatenate([query_grad.reshape(windows_count, WIN * WIN, width), key...  19.9 us
    convert_element_type x8, local copies, waits for them, and re-layouts, scatter_all(): helds.append(held.astype(jnp.bfloat16))  19.7 us
    unnamed x141, local copies, waits for them, and re-layouts  15.9 us
    dot_general x1, matrix products, shards(): jnp.einsum('wqhd,wkhd->whqk', grad_windows, value_win, preferred_element_...  11.9 us
  transfers between devices with their start and end apart: 4, of which 2 were waited for; matrix products, arithmetic and copies ran while one was open for 7% of the time, Pallas kernels for 0%

profile of v1, /device:TPU:0, one launch (start us, length us, event | category | flops | bytes accessed | tf_op | source)
XLA Modules:
  0.0 476.1 jit_solution(14219097174453843279)
XLA Ops:
  3.4 49.3 %gather_weights.1 = (bf16[4,2,2,32,1536]{4,3,2,1,0:T(8,128)(2,1)S(1)}, bf16[4,2,2,32,512]{4,3,2,1,0:T(8,128)(2,1)S(1)}, bf16[4,2,2,32,2048]{4,3,2,1,0:T(8,128)(2,1)S(1)}, bf16[4,2,2,128,512]{4,3,2,1,0:T(8,128)(2,1)}) custom-call(f32[64,384]{1,0:T(8,128)S(1)} %copy-done.5, f32[64,128]{1,0:T(8,128)S(1)} %copy-done.7, f32[64,512]{1,0:T(8,128)S(1)} %copy-done.3, ...), custom_call_target="tpu_custom_call" | custom-call | tf_op jit(solution)/shard_map/gather_weights/pallas_call | solution.py:389
  53.9 4.9 %fusion.18 = bf16[128,8,1536]{2,1,0:T(8,128)(2,1)} fusion(bf16[512,1536]{1,0:T(8,128)(2,1)S(1)} %bitcast.217, f32[1536]{0:T(1024)S(1)} %pad_maximum_fusion.6, bf16[1,1,1024,512]{2,3,1,0:T(8,128)(2,1)} %copy-done.11, f32[512]{0:T(512)S(1)} %bitcast.259, f32[512]{0:T(512)S(1)} %bitcast.240, f32[1024]{0:T(1024)S(1)} %fusion.81, ...), kind=kOutput, calls=%fused_computation.54 | convolution fusion | flops 1616904192 | bytes 5785600 | tf_op jit(solution)/shard_map/dot_general | solution.py:550
  58.8 2.4 gather_fusion
  67.6 2.4 copy.341
  70.4 3.9 pad_maximum_fusion
  74.3 4.4 gather_fusion.1
  78.6 2.6 slice.135
  81.3 2.3 slice.136
  86.9 4.1 copy.328
  91.0 5.9 %reshape.832 = bf16[64,16,1536]{2,1,0:T(8,128)(2,1)} reshape(bf16[32,2,4,4,1536]{4,3,2,1,0:T(4,128)(2,1)} %copy.328) | data formatting | bytes 6291456 | tf_op jit(solution)/shard_map/reshape | solution.py:100
  96.9 3.7 fusion.101
  100.6 3.1 copy.330
  103.8 7.7 %copy.332 = bf16[64,16,16,32]{3,1,2,0:T(8,128)(2,1)} copy(bf16[64,16,16,32]{0,3,2,1:T(8,128)(2,1)} %bitcast.228) | data formatting | bytes 2097152 | tf_op jit(solution)/shard_map/reshape | solution.py:555
  111.5 3.1 copy.331
  114.6 8.0 %copy.333 = bf16[64,16,16,32]{3,1,2,0:T(8,128)(2,1)} copy(bf16[64,16,16,32]{0,3,2,1:T(8,128)(2,1)} %bitcast.229) | data formatting | bytes 2097152 | tf_op jit(solution)/shard_map/reshape | solution.py:556
  122.6 3.1 copy.329
  125.7 7.7 %copy.335 = bf16[64,16,16,32]{3,1,2,0:T(8,128)(2,1)} copy(bf16[64,16,16,32]{0,3,2,1:T(8,128)(2,1)} %bitcast.230) | data formatting | bytes 2097152 | tf_op jit(solution)/shard_map/reshape | solution.py:559
  133.4 11.3 %fusion.105 = (f32[64,16,16]{2,1,0:T(8,128)S(1)}, f32[64,16,16,16]{2,3,1,0:T(8,128)}) fusion(f32[16,16,16]{1,2,0:T(8,128)S(1)} %bitcast.239, pred[64,16,16]{1,2,0:T(8,128)(4,1)S(1)} %or_and_fusion, bf16[64,16,16,32]{3,1,2,0:T(8,128)(2,1)} %copy.332, bf16[64,16,16,32]{3,1,2,0:T(8,128)(2,1)} %copy.333), kind=kOutput, calls=%fused_computation.228 | convolution fusion | flops 18087952 | bytes 3244032 | tf_op jit(solution)/shard_map/sub | solution.py:572
  144.7 5.7 %convert_bitcast_fusion.1 = bf16[64,16,16,32]{3,1,2,0:T(8,128)(2,1)S(1)} fusion(bf16[64,16,16,32]{3,1,2,0:T(8,128)(2,1)} %copy.335, f32[64,16,16,16]{2,3,1,0:T(8,128)} %get-tuple-element.249, f32[64,16,16]{2,1,0:T(8,128)S(1)} %get-tuple-element.248), kind=kOutput, calls=%fused_computation.42 | convolution fusion | flops 17825792 | bytes 3211264 | tf_op jit(solution)/shard_map/whqk,wkhd->wqhd/dot_general | solution.py:573
  150.4 3.0 copy.337
  153.5 6.7 %reshape_reshape.6 = bf16[32,2,4,4,512]{4,3,2,1,0:T(4,128)(2,1)} reshape(bf16[64,16,16,32]{3,2,1,0:T(8,128)(2,1)} %copy.337) | data formatting | bytes 2097152 | tf_op jit(solution)/shard_map/reshape;reshape | solution.py:106
  164.7 15.9 %scatter_fusion = bf16[136,8,512]{2,1,0:T(8,128)(2,1)} fusion(bf16[136,8,512]{2,1,0:T(8,128)(2,1)} %broadcast_in_dim.52, s32[128]{0:T(128)S(1)} %fusion.83, bf16[128,8,512]{2,1,0:T(8,128)(2,1)} %bitcast.236), kind=kCustom, calls=%fused_computation.4 | custom fusion | bytes 3146240 | tf_op jit(solution)/shard_map/scatter | solution.py:109
  181.5 2.3 slice.142
  187.3 2.3 fusion.106
  190.0 22.9 %multiply_convert_fusion.3 = (bf16[1024,2048]{1,0:T(8,128)(2,1)}, f32[1024,2048]{1,0:T(8,128)S(1)}, f32[1024,2048]{1,0:T(8,128)}) fusion(f32[2048]{0:T(1024)S(1)} %bitcast.255, bf16[512,2048]{1,0:T(8,128)(2,1)S(1)} %bitcast.215, f32[1024,512]{0,1:T(8,128)S(1)} %get-tuple-element.251, f32[512]{0:T(512)S(1)} %bitcast.262, f32[512]{0:T(512)S(1)} %bitcast.245, ...), kind=kOutput, calls=%fused_computation.18 | convolution fusion | flops 2288517120 | bytes 25186304 | tf_op jit(solution)/shard_map/dot_general | solution.py:584
  212.8 7.7 %convert_reduce_fusion.1 = (f32[2048]{0:T(1024)S(1)}, bf16[1024,2048]{1,0:T(8,128)(2,1)S(1)}) fusion(f32[1024,2048]{1,0:T(8,128)S(1)} %get-tuple-element.229, bf16[2048,512]{1,0:T(8,128)(2,1)S(1)} %bitcast.268, bf16[1,1,1024,512]{2,3,1,0:T(8,128)(2,1)S(1)} %copy-done.22, f32[1024]{0:T(1024)S(1)} %fusion.80, f32[1024,2048]{1,0:T(8,128)} %get-tuple-element.252, ...), kind=kOutput, calls=%fused_computation.12 | convolution fusion | flops 2184706048 | bytes 24137728 | tf_op jit(solution)/shard_map/dot_general | solution.py:597
  220.5 3.8 multiply_convert_fusion.5
  224.3 3.7 fusion.108
  228.0 3.1 copy.342
  231.1 2.4 multiply_reduce_fusion.1
  240.8 6.4 %multiply_convert_fusion.4 = bf16[2048,512]{1,0:T(8,128)(2,1)} fusion(bf16[1024,2048]{1,0:T(8,128)(2,1)} %get-tuple-element.228, bf16[1,1,1024,512]{2,3,1,0:T(8,128)(2,1)} %copy.341, f32[1024]{0:T(1024)S(1)} %fusion.80), kind=kOutput, calls=%fused_computation.39 | convolution fusion | flops 2151153664 | bytes 7344128 | tf_op jit(solution)/shard_map/dot_general | solution.py:596
  247.2 3.4 fusion.49
  252.1 3.1 convert_element_type.150
  257.6 4.0 convert_element_type.154
  261.6 3.5 copy.386
  265.1 2.3 copy.366
  267.3 2.3 pad_maximum_fusion.3
  269.7 2.9 gather_fusion.3
  278.4 6.0 %reshape_reshape.7 = bf16[64,16,16,32]{3,2,1,0:T(8,128)(2,1)} reshape(bf16[32,2,4,4,512]{4,3,2,1,0:T(4,128)(2,1)} %copy.344) | data formatting | bytes 2097152 | tf_op jit(solution)/shard_map/reshape;reshape | solution.py:612
  284.4 11.9 %multiply_reduce_fusion = (f32[64,16,16]{2,1,0:T(8,128)S(1)}, f32[64,16,16,16]{2,3,1,0:T(8,128)}) fusion(f32[64,16,16,16]{2,3,1,0:T(8,128)} %get-tuple-element.249, f32[64,16,16]{2,1,0:T(8,128)S(1)} %copy-done.30, bf16[64,16,16,32]{3,1,2,0:T(8,128)(2,1)} %copy.335, bf16[64,16,16,32]{3,2,1,0:T(8,128)(2,1)} %reshape_reshape.7), kind=kOutput, calls=%fused_computation.16 | convolution fusion | flops 17547264 | bytes 4325376 | tf_op jit(solution)/shard_map/wqhd,wkhd->whqk/dot_general | solution.py:614
  296.3 7.6 %convert_reduce_fusion = (f32[16,16,16]{1,2,0:T(8,128)S(1)}, bf16[64,16,16,16]{2,3,1,0:T(8,128)(2,1)S(1)}) fusion(f32[64,16,16,16]{2,3,1,0:T(8,128)} %get-tuple-element.254, f32[64,16,16]{2,1,0:T(8,128)S(1)} %get-tuple-element.253, f32[64,16,16,16]{2,3,1,0:T(8,128)} %get-tuple-element.249, f32[64,16,16]{2,1,0:T(8,128)S(1)} %copy-done.30), kind=kLoop, calls=%fused_computation.11 | loop fusion | flops 1568768 | bytes 2768896 | tf_op jit(solution)/shard_map/reduce_sum | solution.py:624
  306.1 4.2 fusion.9
  310.3 8.9 %convert_bitcast_fusion = bf16[64,16,16,32]{3,1,2,0:T(8,128)(2,1)} fusion(bf16[64,16,16,32]{3,2,1,0:T(8,128)(2,1)} %reshape_reshape.7, f32[64,16,16,16]{2,3,1,0:T(8,128)} %get-tuple-element.249, f32[64,16,16]{2,1,0:T(8,128)S(1)} %copy-done.30), kind=kOutput, calls=%fused_computation.41 | convolution fusion | flops 17825792 | bytes 3211264 | tf_op jit(solution)/shard_map/whqk,wqhd->wkhd/dot_general | solution.py:617
  319.2 3.0 copy.349
  322.2 6.6 %concatenate.48 = bf16[32,2,4,4,512]{4,3,2,1,0:T(4,128)(2,1)} reshape(bf16[64,16,16,32]{3,2,1,0:T(8,128)(2,1)} %copy.349) | data formatting | bytes 2097152 | tf_op jit(solution)/shard_map/concatenate | solution.py:637
  328.9 5.2 %copy.351 = bf16[64,16,16,32]{3,2,1,0:T(8,128)(2,1)} copy(bf16[64,16,16,32]{3,1,2,0:T(8,128)(2,1)} %fusion.9) | data formatting | bytes 2097152 | tf_op jit(solution)/shard_map/mul | solution.py:634
  334.1 6.6 %concatenate.49 = bf16[32,2,4,4,512]{4,3,2,1,0:T(4,128)(2,1)} reshape(bf16[64,16,16,32]{3,2,1,0:T(8,128)(2,1)} %copy.351) | data formatting | bytes 2097152 | tf_op jit(solution)/shard_map/concatenate | solution.py:637
  340.8 5.2 %copy.353 = bf16[64,16,16,32]{3,2,1,0:T(8,128)(2,1)} copy(bf16[64,16,16,32]{3,1,2,0:T(8,128)(2,1)} %convert_bitcast_fusion) | data formatting | bytes 2097152 | tf_op jit(solution)/shard_map/whqk,wqhd->wkhd/transpose | solution.py:617
  346.0 6.7 %concatenate.50 = bf16[32,2,4,4,512]{4,3,2,1,0:T(4,128)(2,1)} reshape(bf16[64,16,16,32]{3,2,1,0:T(8,128)(2,1)} %copy.353) | data formatting | bytes 2097152 | tf_op jit(solution)/shard_map/concatenate | solution.py:637
  352.6 3.9 maximum_bitcast_fusion
  358.8 3.4 copy.355
  364.1 18.3 %scatter_fusion.2 = bf16[136,8,1536]{2,1,0:T(8,128)(2,1)} fusion(bf16[136,8,1536]{2,1,0:T(8,128)(2,1)} %broadcast_in_dim.67, s32[128]{0:T(128)S(1)} %copy-done.58, bf16[128,8,1536]{2,1,0:T(8,128)(2,1)} %bitcast.226), kind=kCustom, calls=%fused_computation.6 | custom fusion | bytes 9437696 | tf_op jit(solution)/shard_map/scatter | solution.py:109
  382.5 3.8 slice.148
  388.1 4.3 collective-permute-done.3
  392.4 2.5 scatter_fusion.3
  394.9 5.4 %fusion.22 = bf16[512,1536]{1,0:T(8,128)(2,1)} fusion(bf16[128,8,1536]{2,1,0:T(8,128)(2,1)} %scatter_fusion.3, bf16[1,1,1024,512]{2,3,1,0:T(8,128)(2,1)} %copy-done.11, f32[512]{0:T(512)S(1)} %bitcast.260, f32[512]{0:T(512)S(1)} %bitcast.241, f32[1024]{0:T(1024)S(1)} %copy-done.42, f32[1024]{0:T(1024)S(1)} %copy-done.36), kind=kOutput, calls=%fused_computation.66 | convolution fusion | flops 1615331328 | bytes 5779456 | tf_op jit(solution)/shard_map/dot_general | solution.py:650
  400.3 3.1 fusion.107
  404.0 4.0 convert_element_type.144
  407.9 2.8 copy.388
  410.8 2.9 copy.356
  413.7 2.4 fusion.39
  417.5 2.4 fusion.35
  421.4 46.7 %scatter_grads.1 = (f32[16,512]{1,0:T(8,128)S(1)}, f32[64,384]{1,0:T(8,128)S(1)}, f32[64,128]{1,0:T(8,128)S(1)}, f32[64,512]{1,0:T(8,128)S(1)}, f32[256,128]{1,0:T(8,128)S(1)}) custom-call(f32[16,512]{1,0:T(8,128)S(1)} %reshape.858.refs_0_, bf16[4,2,2,4,32,384]{5,4,3,2,1,0:T(8,128)(2,1)S(1)} %bitcast.213, bf16[4,2,2,4,32,128]{5,4,3,2,1,0:T(8,128)(2,1)S(1)} %bitcast.214, ...), custom_call_target="tpu_custom_call" | custom-call | tf_op jit(solution)/shard_map/scatter_grads/pallas_call | solution.py:466
  468.5 3.0 copy.367
  (249 shorter events, 53.2 us)
Async XLA Ops:
  0.7 2.2 copy-start.37
  0.7 2.2 copy-start.63
  0.7 2.7 copy-start.5
  0.7 2.7 copy-start.7
  0.7 2.7 copy-start.3
  0.7 2.7 copy-start.1
  2.5 50.2 %copy-start.35 = (f32[1024]{0:T(1024)}, f32[1024]{0:T(1024)S(1)}, u32[]{:S(2)}) copy-start(f32[1024]{0:T(1024)S(1)} %broadcast_multiply_fusion.1) | copy-start | bytes 12292
  2.8 49.9 %copy-start.43 = (f32[1024]{0:T(1024)}, f32[1024]{0:T(1024)S(1)}, u32[]{:S(2)}) copy-start(f32[1024]{0:T(1024)S(1)} %fusion.38) | copy-start | bytes 12292
  2.9 49.9 %copy-start.41 = (f32[1024]{0:T(1024)}, f32[1024]{0:T(1024)S(1)}, u32[]{:S(2)}) copy-start(f32[1024]{0:T(1024)S(1)} %fusion.81) | copy-start | bytes 12292
  2.9 49.9 %copy-start.49 = (f32[1,512]{1,0:T(1,128)}, f32[1,512]{1,0:T(1,128)S(1)}, u32[]{:S(2)}) copy-start(f32[1,512]{1,0:T(1,128)S(1)} %get-tuple-element.243) | copy-start | bytes 6148
  2.9 55.9 %copy-start.59 = (f32[1,512]{1,0:T(1,128)}, f32[1,512]{1,0:T(1,128)S(1)}, u32[]{:S(2)}) copy-start(f32[1,512]{1,0:T(1,128)S(1)} %get-tuple-element.242) | copy-start | bytes 6148
  3.3 181.9 %copy-start.55 = (s32[8]{0:T(128)}, s32[8]{0:T(128)S(1)}, u32[]{:S(2)}) copy-start(s32[8]{0:T(128)S(1)} %fusion.84) | copy-start | bytes 100
  53.9 11.9 %copy-start.51 = (f32[49,16]{0,1:T(8,128)S(1)}, f32[49,16]{0,1:T(8,128)}, u32[]{:S(2)}) copy-start(f32[49,16]{0,1:T(8,128)} %param.39) | copy-start | bytes 9412
  61.2 9.2 %collective-permute-start = (bf16[8,8,1536]{2,1,0:T(8,128)(2,1)S(1)}, bf16[8,8,1536]{2,1,0:T(8,128)(2,1)S(1)}, u32[]{:S(2)}, u32[]{:S(2)}) collective-permute-start(bf16[8,8,1536]{2,1,0:T(8,128)(2,1)S(1)} %gather_fusion), channel_id=1, source_target_pairs={{8,0},{16,8},{24,16},{0,24},{9,1},{17,9},{25,17},{1,25},{10,2},{18... | collective-permute-start | bytes 589832 | tf_op jit(solution)/shard_map/ppermute | solution.py:32
  70.4 94.4 %copy-start.57 = (s32[128]{0:T(128)}, s32[128]{0:T(128)S(1)}, u32[]{:S(2)}) copy-start(s32[128]{0:T(128)S(1)} %fusion.83) | copy-start | bytes 1540
  144.7 5.7 %copy-start.29 = (f32[64,16,16]{2,1,0:T(8,128)}, f32[64,16,16]{2,1,0:T(8,128)S(1)}, u32[]{:S(2)}) copy-start(f32[64,16,16]{2,1,0:T(8,128)S(1)} %get-tuple-element.248) | copy-start | bytes 196612
  181.5 3.7 collective-permute-start.1
  189.6 30.9 %copy-start.16 = (f32[1024,512]{0,1:T(8,128)}, f32[1024,512]{0,1:T(8,128)S(1)}, u32[]{:S(2)}) copy-start(f32[1024,512]{0,1:T(8,128)S(1)} %get-tuple-element.251) | copy-start | bytes 6291460
  190.0 22.9 %copy-start.22 = (bf16[1,1,1024,512]{2,3,1,0:T(8,128)(2,1)S(1)}, bf16[1,1,1024,512]{2,3,1,0:T(8,128)(2,1)}, u32[]{:S(2)}) copy-start(bf16[1,1,1024,512]{2,3,1,0:T(8,128)(2,1)} %copy.341) | copy-start | bytes 3145732
  190.0 22.9 %copy-start.64 = (bf16[4,2,2,128,512]{4,3,2,1,0:T(8,128)(2,1)S(1)}, bf16[4,2,2,128,512]{4,3,2,1,0:T(8,128)(2,1)}, u32[]{:S(2)}) copy-start(bf16[4,2,2,128,512]{4,3,2,1,0:T(8,128)(2,1)} %get-tuple-element.32) | copy-start | bytes 6291460
  228.0 3.1 copy-start.17
  231.1 2.4 copy-start.18
  233.5 1.9 copy-start.23
  240.4 26.9 %collective-permute-start.2 = (bf16[8,8,512]{2,1,0:T(8,128)(2,1)S(1)}, bf16[8,8,512]{2,1,0:T(8,128)(2,1)S(1)}, u32[]{:S(2)}, u32[]{:S(2)}) collective-permute-start(bf16[8,8,512]{2,1,0:T(8,128)(2,1)S(1)} %gather_fusion.2), channel_id=1, source_target_pairs={{8,0},{16,8},{24,16},{0,24},{9,1},{17,9},{25,17},{1,25},{10,2},{18... | collective-permute-start | bytes 196616 | tf_op jit(solution)/shard_map/ppermute | solution.py:32
  240.8 6.4 %copy-start.65 = (bf16[4,2,2,128,512]{4,3,2,1,0:T(8,128)(2,1)S(1)}, bf16[4,2,2,128,512]{4,3,2,1,0:T(8,128)(2,1)}, u32[]{:S(2)}) copy-start(bf16[4,2,2,128,512]{4,3,2,1,0:T(8,128)(2,1)} %get-tuple-element.32) | copy-start | bytes 6291460
  240.8 6.4 %copy-start.66 = (bf16[1024,2048]{1,0:T(8,128)(2,1)S(1)}, bf16[1024,2048]{1,0:T(8,128)(2,1)}, u32[]{:S(2)}) copy-start(bf16[1024,2048]{1,0:T(8,128)(2,1)} %get-tuple-element.228) | copy-start | bytes 12582916
  247.2 3.4 copy-start.26
  247.2 3.4 copy-start.28
  276.6 7.8 %copy-start.30 = (f32[64,16,16]{2,1,0:T(8,128)S(1)}, f32[64,16,16]{2,1,0:T(8,128)}, u32[]{:S(2)}) copy-start(f32[64,16,16]{2,1,0:T(8,128)} %copy-done.29) | copy-start | bytes 196612
  296.3 7.6 %copy-start.20 = (bf16[64,16,16,32]{3,1,2,0:T(8,128)(2,1)S(1)}, bf16[64,16,16,32]{3,1,2,0:T(8,128)(2,1)}, u32[]{:S(2)}) copy-start(bf16[64,16,16,32]{3,1,2,0:T(8,128)(2,1)} %copy.333) | copy-start | bytes 3145732
  303.9 2.2 copy-start.19
  358.8 5.3 %copy-start.58 = (s32[128]{0:T(128)S(1)}, s32[128]{0:T(128)}, u32[]{:S(2)}) copy-start(s32[128]{0:T(128)} %copy-done.57) | copy-start | bytes 1540
  382.5 5.2 %copy-start.62 = (s32[256]{0:T(256)S(1)}, s32[256]{0:T(256)}, u32[]{:S(2)}) copy-start(s32[256]{0:T(256)} %copy-done.61) | copy-start | bytes 3076
  382.5 9.9 %copy-start.56 = (s32[8]{0:T(128)S(1)}, s32[8]{0:T(128)}, u32[]{:S(2)}) copy-start(s32[8]{0:T(128)} %copy-done.55) | copy-start | bytes 100
  382.5 12.4 %copy-start.36 = (f32[1024]{0:T(1024)S(1)}, f32[1024]{0:T(1024)}, u32[]{:S(2)}) copy-start(f32[1024]{0:T(1024)} %copy-done.35) | copy-start | bytes 12292
  382.5 12.4 %copy-start.42 = (f32[1024]{0:T(1024)S(1)}, f32[1024]{0:T(1024)}, u32[]{:S(2)}) copy-start(f32[1024]{0:T(1024)} %copy-done.41) | copy-start | bytes 12292
  382.5 12.4 %copy-start.50 = (f32[1,512]{1,0:T(1,128)S(1)}, f32[1,512]{1,0:T(1,128)}, u32[]{:S(2)}) copy-start(f32[1,512]{1,0:T(1,128)} %copy-done.49) | copy-start | bytes 6148
  382.5 12.4 %copy-start.60 = (f32[1,512]{1,0:T(1,128)S(1)}, f32[1,512]{1,0:T(1,128)}, u32[]{:S(2)}) copy-start(f32[1,512]{1,0:T(1,128)} %copy-done.59) | copy-start | bytes 6148
  387.3 5.1 %collective-permute-start.3 = (bf16[8,8,1536]{2,1,0:T(8,128)(2,1)S(1)}, bf16[8,8,1536]{2,1,0:T(8,128)(2,1)S(1)}, u32[]{:S(2)}, u32[]{:S(2)}) collective-permute-start(bf16[8,8,1536]{2,1,0:T(8,128)(2,1)S(1)} %slice.149), channel_id=1, source_target_pairs={{24,0},{0,8},{8,16},{16,24},{25,1},{1,9},{9,17},{17,25},{26,2},{2,... | collective-permute-start | bytes 589832 | tf_op jit(solution)/shard_map/ppermute | solution.py:32
  394.9 5.5 %copy-start.10 = (bf16[4,2,2,32,1536]{4,3,2,1,0:T(8,128)(2,1)S(1)}, bf16[4,2,2,32,1536]{4,3,2,1,0:T(8,128)(2,1)}, u32[]{:S(2)}) copy-start(bf16[4,2,2,32,1536]{4,3,2,1,0:T(8,128)(2,1)} %copy-done.9) | copy-start | bytes 4718596
  394.9 5.4 %copy-start.21 = (bf16[128,8,1536]{2,1,0:T(8,128)(2,1)S(1)}, bf16[128,8,1536]{2,1,0:T(8,128)(2,1)}, u32[]{:S(2)}) copy-start(bf16[128,8,1536]{2,1,0:T(8,128)(2,1)} %scatter_fusion.3) | copy-start | bytes 9437188
  410.8 5.4 %copy-start.44 = (f32[1024]{0:T(1024)S(1)}, f32[1024]{0:T(1024)}, u32[]{:S(2)}) copy-start(f32[1024]{0:T(1024)} %copy-done.43) | copy-start | bytes 12292
  413.7 2.5 copy-start.12
  413.7 2.9 copy-start.13
  413.7 3.8 copy-start.15
  413.7 3.8 copy-start.24
  468.1 3.4 copy-start.38
  468.1 3.4 copy-start.45
  468.1 3.4 copy-start.46
  468.2 4.0 copy-start.2
  468.2 4.0 copy-start.31
  468.2 4.0 copy-start.32
  468.2 4.8 %copy-start.4 = (f32[64,512]{1,0:T(8,128)S(1)}, f32[64,512]{1,0:T(8,128)}, u32[]{:S(2)}) copy-start(f32[64,512]{1,0:T(8,128)} %refs_2_.1) | copy-start | bytes 393220
  468.2 4.8 %copy-start.33 = (f32[64,512]{1,0:T(8,128)S(1)}, f32[64,512]{1,0:T(8,128)}, u32[]{:S(2)}) copy-start(f32[64,512]{1,0:T(8,128)} %param.30) | copy-start | bytes 393220
  468.2 4.8 %copy-start.34 = (f32[64,512]{1,0:T(8,128)S(1)}, f32[64,512]{1,0:T(8,128)}, u32[]{:S(2)}) copy-start(f32[64,512]{1,0:T(8,128)} %param.34) | copy-start | bytes 393220
  468.2 5.6 %copy-start.52 = (f32[49,16]{0,1:T(8,128)S(1)}, f32[49,16]{0,1:T(8,128)}, u32[]{:S(2)}) copy-start(f32[49,16]{0,1:T(8,128)} %param.39) | copy-start | bytes 9412
  468.2 5.6 %copy-start.53 = (f32[49,16]{0,1:T(8,128)S(1)}, f32[49,16]{0,1:T(8,128)}, u32[]{:S(2)}) copy-start(f32[49,16]{0,1:T(8,128)} %param.40) | copy-start | bytes 9412
  468.2 5.6 %copy-start.54 = (f32[49,16]{0,1:T(8,128)S(1)}, f32[49,16]{0,1:T(8,128)}, u32[]{:S(2)}) copy-start(f32[49,16]{0,1:T(8,128)} %param.41) | copy-start | bytes 9412
  468.3 6.2 %copy-start.6 = (f32[64,384]{1,0:T(8,128)S(1)}, f32[64,384]{1,0:T(8,128)}, u32[]{:S(2)}) copy-start(f32[64,384]{1,0:T(8,128)} %refs_0_.1) | copy-start | bytes 294916
  468.3 6.2 %copy-start.39 = (f32[64,384]{1,0:T(8,128)S(1)}, f32[64,384]{1,0:T(8,128)}, u32[]{:S(2)}) copy-start(f32[64,384]{1,0:T(8,128)} %param.28) | copy-start | bytes 294916
  468.3 6.2 %copy-start.40 = (f32[64,384]{1,0:T(8,128)S(1)}, f32[64,384]{1,0:T(8,128)}, u32[]{:S(2)}) copy-start(f32[64,384]{1,0:T(8,128)} %param.32) | copy-start | bytes 294916
  468.5 6.7 %copy-start.8 = (f32[64,128]{1,0:T(8,128)S(1)}, f32[64,128]{1,0:T(8,128)}, u32[]{:S(2)}) copy-start(f32[64,128]{1,0:T(8,128)} %refs_1_.1) | copy-start | bytes 98308
  468.5 6.7 %copy-start.47 = (f32[64,128]{1,0:T(8,128)S(1)}, f32[64,128]{1,0:T(8,128)}, u32[]{:S(2)}) copy-start(f32[64,128]{1,0:T(8,128)} %param.29) | copy-start | bytes 98308
  468.5 6.7 %copy-start.48 = (f32[64,128]{1,0:T(8,128)S(1)}, f32[64,128]{1,0:T(8,128)}, u32[]{:S(2)}) copy-start(f32[64,128]{1,0:T(8,128)} %param.33) | copy-start | bytes 98308
  (7 other events, 8.5 us)

commit v2 on v1

--- a/solution.py
+++ b/solution.py
@@ -1,5 +1,7 @@
 import functools
 import itertools
+import math
+import typing
 
 import jax
 import jax.numpy as jnp
@@ -13,6 +15,8 @@
 WIN = 4
 STEP = 10
 RELS = 49
+SLAB, CLIP = "slab", "clip"
+SHORT = 64
 
 
 HIGHEST = lax.Precision.HIGHEST
@@ -147,13 +151,14 @@
 
 class Place:
     def __init__(self, clip_size):
-        self.slab, self.clip = lax.axis_index("slab"), lax.axis_index("clip")
+        self.slab, self.clip = lax.axis_index(SLAB), lax.axis_index(CLIP)
         self.x, self.core = self.slab // 2, self.slab % 2
         self.z, self.y = self.clip // 2, self.clip % 2
         self.depth = clip_size // 2
         self.over_core = (self.x * 2 + 1 - self.core, self.clip)
         self.over_x = ((1 - self.x) * 2 + self.core, self.clip)
         self.over_y = (self.slab, self.z * 2 + 1 - self.y)
+        self.over_diagonal = ((1 - self.x) * 2 + 1 - self.core, self.clip)
         self.x_slab = (1 - self.x) * 2 + self.core
         self.core_slab = self.x * 2 + 1 - self.core
 
@@ -165,7 +170,7 @@
 
     def greet(self):
         barrier = pltpu.get_barrier_semaphore()
-        partners = [self.over_core, self.over_x, self.over_y]
+        partners = [self.over_core, self.over_x, self.over_y, self.over_diagonal]
         partners += [self.over_z(step) for step in range(1, self.depth)]
         for partner in partners:
             pl.semaphore_signal(barrier, inc=1, device_id=partner, device_id_type=MESH)
@@ -240,10 +245,6 @@
 
     def end(self):
         wait_all(self.over_core)
-
-
-def gather_copies(place, clip_size):
-    return 2 * (place - 1) + 9
 
 
 def add_into(held, index, arrived, arrived_index):
@@ -362,76 +363,6 @@
         return total
 
 
-def gather_kernel(clip_size, *refs):
-    masters, wholes = refs[:4], refs[4:8]
-    place, links = Place(clip_size), Links(*refs[8:])
-    place.greet()
-    flows = [
-        Gather(place, links, whole, master.shape[1]) for master, whole in zip(masters, wholes)
-    ]
-    for stage in ("begin", "second", "third", "fourth", "end"):
-        for position, flow in enumerate(flows):
-            if stage == "begin":
-                flow.begin(masters[position])
-            else:
-                getattr(flow, stage)()
-    links.drain()
-
-
-def gather_all(masters, clip_size):
-    vmem = pl.BlockSpec(memory_space=pltpu.VMEM)
-    depth = clip_size // 2
-    shapes = [
-        jax.ShapeDtypeStruct((depth, 2, 2, m.shape[0] // 2, 4 * m.shape[1]), jnp.bfloat16)
-        for m in masters
-    ]
-    copies = 4 * (2 * (depth - 1) + 9)
-    wholes = pl.pallas_call(
-        functools.partial(gather_kernel, clip_size),
-        out_shape=shapes,
-        in_specs=[vmem] * 4,
-        out_specs=[vmem] * 4,
-        scratch_shapes=[pltpu.SemaphoreType.DMA((copies,)), pltpu.SemaphoreType.DMA((copies,))],
-        compiler_params=pltpu.CompilerParams(
-            collective_id=0, has_side_effects=True, vmem_limit_bytes=48 << 20
-        ),
-        name="gather_weights",
-    )(*masters)
-    return [w.reshape(-1, w.shape[-1]) for w in wholes]
-
-
-def scatter_kernel(clip_size, shapes, *refs):
-    small_in, helds_in = refs[0], refs[1:5]
-    small_out, outs = refs[5], refs[6:10]
-    rest = list(refs[10:])
-    place = Place(clip_size)
-    links = Links(rest.pop(0), rest.pop(0))
-    place.greet()
-    small = Small(place, links, rest.pop(0), rest.pop(0), rest.pop(0))
-    small.held[0] = small_in[...]
-    flows = []
-    loads = rest.pop(0)
-    for position, source in enumerate(helds_in):
-        held = rest.pop(0)
-        load = pltpu.make_async_copy(source, held, loads.at[position])
-        load.start()
-        flows.append(Scatter(place, links, held, *[rest.pop(0) for _ in range(6)]))
-        flows[-1].load = load
-    for flow in flows:
-        flow.load.wait()
-    flows = [small] + flows
-    for stage in ("begin", "second", "third", "fourth"):
-        for flow in flows:
-            getattr(flow, stage)()
-    small_out[...] = small.end()
-    for flow, out in zip(flows[1:], outs):
-        first, last = flow.end()
-        rows = first.shape[0]
-        out[:rows, :] = first
-        out[rows:, :] = last
-    links.drain()
-
-
 def scatter_buffers(shape):
     slabs, _, _, depth, rows, columns = shape
     return [
@@ -444,37 +375,663 @@
     ]
 
 
-def scatter_all(small, grads, clip_size):
-    vmem = pl.BlockSpec(memory_space=pltpu.VMEM)
+def norm_parts(values):
+    center = values - jnp.mean(values, -1, keepdims=True)
+    inverse = lax.rsqrt(jnp.mean(center * center, -1, keepdims=True) + norm_epsilon)
+    return center * inverse, inverse
+
+
+def norm_back(normed, inverse, grad):
+    return inverse * (
+        grad
+        - jnp.mean(grad, -1, keepdims=True)
+        - normed * jnp.mean(grad * normed, -1, keepdims=True)
+    )
+
+
+def gelu_parts(values):
+    below = 0.5 + 0.5 * lax.erf(values * (0.5**0.5))
+    density = jnp.exp(-0.5 * values * values) * ((0.5 / math.pi) ** 0.5)
+    return values * below, below + values * density
+
+
+def mm(left, right):
+    return jnp.dot(left, right, preferred_element_type=jnp.float32)
+
+
+def mm_nt(left, right):
+    return lax.dot_general(
+        left, right, (((1,), (1,)), ((), ())), preferred_element_type=jnp.float32
+    )
+
+
+def mm_tn(left, right):
+    return lax.dot_general(
+        left, right, (((0,), (0,)), ((), ())), preferred_element_type=jnp.float32
+    )
+
+
+def span(index, size):
+    return pl.ds(pl.multiple_of(index * size, size), size)
+
+
+def blocks(ref, index, count):
+    return jnp.concatenate([ref[index + k] for k in range(count)], 0)
+
+
+def rows_of(ref, index, size):
+    value = ref[span(index, size // ref.shape[1])]
+    return value.reshape(size, value.shape[-1])
+
+
+def put_rows(ref, index, value):
+    count = value.shape[0] // ref.shape[1]
+    ref[span(index, count)] = value.reshape(count, ref.shape[1], value.shape[-1])
+
+
+def flat(ref, columns=slice(None)):
+    block = ref[:, :, :, :, columns]
+    return block.reshape(-1, block.shape[-1])
+
+
+class Held(typing.NamedTuple):
+    xb: typing.Any
+    eb: typing.Any
+    et: typing.Any
+    attn_in: typing.Any
+    attn_in_t: typing.Any
+    own: typing.Any
+    lent: typing.Any
+    borrowed: typing.Any
+    probs: typing.Any
+    att_win: typing.Any
+    att_out: typing.Any
+    att_back: typing.Any
+    att_rows: typing.Any
+    att_t: typing.Any
+    mid: typing.Any
+    mlp_in: typing.Any
+    mlp_in_t: typing.Any
+    act: typing.Any
+    slope: typing.Any
+    mid_grad: typing.Any
+    mid_low: typing.Any
+    dwin_own: typing.Any
+    dlent: typing.Any
+    dborrowed: typing.Any
+    qg_win: typing.Any
+    qg_out: typing.Any
+    qg_back: typing.Any
+    qg_rows: typing.Any
+    bias: typing.Any
+    bias_grad: typing.Any
+    up_sum: typing.Any
+    att_sum: typing.Any
+    out_low: typing.Any
+    load_sems: typing.Any
+    whole_qkv: typing.Any
+    whole_proj: typing.Any
+    whole_up: typing.Any
+    whole_down: typing.Any
+
+
+def block_kernel(slabs, clips, *refs):
+    refs = list(refs)
+    tokens, y_grad, units, vectors, table = refs[:5]
+    masters = refs[5:9]
+    block_out, x_grad, small_out = refs[9:12]
+    owned = refs[12:16]
+    rest = refs[16:]
+    place = Place(clips)
+    links = Links(rest.pop(0), rest.pop(0))
+    s = Held(*rest[: len(Held._fields)])
+    rest = rest[len(Held._fields) :]
+    small = Small(place, links, rest.pop(0), rest.pop(0), rest.pop(0))
+    flows = [Scatter(place, links, *[rest.pop(0) for _ in range(7)]) for _ in masters]
+    qkv_flow, proj_flow, up_flow, down_flow = flows
+    xb, eb, own, bias = s.xb, s.eb, s.own, s.bias
+    tok, width = xb.shape
+    unit = SHORT // slabs * BINS
+    unit_count = tok // unit
+    half = WIN // 2 * BINS
+    per_unit = unit // half
+    group = WIN * BINS
+    head = width // HEADS
+    pack = 128 // head
+    tiles = width // 128
+    score_scale = head**-0.5
+    grad_scale = float(tok * slabs * clips) ** -0.5
+    slots = s.lent.shape[0]
+
+    loads = [
+        pltpu.make_async_copy(tokens, xb, s.load_sems.at[0]),
+        pltpu.make_async_copy(y_grad, eb, s.load_sems.at[1]),
+    ]
+    for load in loads:
+        load.start()
+    place.greet()
+    gathers = [
+        Gather(place, links, whole, master.shape[1])
+        for whole, master in zip(
+            (s.whole_qkv, s.whole_proj, s.whole_up, s.whole_down), masters
+        )
+    ]
+    qkv_copy, proj_copy, up_copy, down_copy = gathers
+    qkv_copy.begin(masters[0])
+
+    heads = [units[HEADS_AT, i] for i in range(slots)]
+    tails = [units[TAILS_AT, i] for i in range(slots)]
+    used = units[USED_AT, 0]
+
+    heads_of = lax.broadcasted_iota(jnp.int32, (HEADS, width), 1) // head
+    spread = (heads_of == lax.broadcasted_iota(jnp.int32, (HEADS, width), 0)).astype(jnp.float32)
+    by_offset = jnp.dot(table[...], spread, precision=HIGHEST)
+    key = lax.broadcasted_iota(jnp.int32, (group, width), 0)
+    query = lax.broadcasted_iota(jnp.int32, (group, width), 1) % group
+    key_row, key_bin, query_row, query_bin = key // BINS, key % BINS, query // BINS, query % BINS
+    key_place, query_place = (key_bin - WIN // 2) % BINS, (query_bin - WIN // 2) % BINS
+    key_class = key_place // WIN + jnp.where(key_place >= WIN + WIN // 2, 1, 0)
+    query_class = query_place // WIN + jnp.where(query_place >= WIN + WIN // 2, 1, 0)
+    same = key_class == query_class
+    offset = (query_row - key_row + WIN - 1) * (2 * WIN - 1) + query_place - key_place + WIN - 1
+    offset = jnp.where(same, offset, -1)
+    total = jnp.zeros((group, width), jnp.float32)
+    for r in range(RELS):
+        total = jnp.where(offset == r, by_offset[r : r + 1, :], total)
+    total = jnp.where(same, total, masked_score)
+    bias[0] = total
+    bias[1] = jnp.where(key_row // (WIN // 2) == query_row // (WIN // 2), total, masked_score)
+    lane = lax.broadcasted_iota(jnp.int32, (group, 128), 1) // head
+    picks = [(lane == h).astype(jnp.bfloat16) for h in range(pack)]
+
+    def stacked(block):
+        return jnp.concatenate([block * pick for pick in picks], 0)
+
+    def folded(block):
+        result = block[(pack - 1) * group :]
+        for h in range(pack - 2, -1, -1):
+            result = jnp.where(lane == h, block[h * group : (h + 1) * group], result)
+        return result
+
+    loads[0].wait()
+    chunk = 256
+
+    @pl.loop(0, tok // chunk)
+    def _(i):
+        normed, _ = norm_parts(xb[span(i, chunk), :].astype(jnp.float32))
+        low = (normed * vectors[0:1, :] + vectors[1:2, :]).astype(jnp.bfloat16)
+        put_rows(s.attn_in, i, low)
+        s.attn_in_t[:, span(i, chunk)] = low.T
+
+    qkv_copy.second()
+    proj_copy.begin(masters[1])
+    up_copy.begin(masters[2])
+
+    loads[1].wait()
+
+    @pl.loop(0, tok // chunk)
+    def _(i):
+        live = lax.broadcasted_iota(jnp.int32, (chunk, width), 0) + i * chunk < used
+        low = jnp.where(live, eb[span(i, chunk), :].astype(jnp.float32), 0.0)
+        low = low.astype(jnp.bfloat16)
+        eb[span(i, chunk), :] = low
+        s.et[:, span(i, chunk)] = low.T
+
+    qkv_copy.third()
+    down_copy.begin(masters[3])
+    proj_copy.second()
+    qkv_copy.fourth()
+    qkv_copy.end()
+    up_copy.second()
+    whole_qkv, whole_proj = s.whole_qkv, s.whole_proj
+    whole_up, whole_down = s.whole_up, s.whole_down
+
+    qkv_bias = jnp.concatenate(
+        [vectors[2:3, :], jnp.zeros((1, width), jnp.float32), vectors[3:4, :]], 1
+    )
+    head_in = jnp.concatenate(
+        [s.attn_in[heads[i]] for i in range(slots)], 0
+    )
+    put_rows(s.lent, 0, (mm(head_in, flat(whole_qkv)) + qkv_bias).astype(jnp.bfloat16))
+    before = (lax.rem(place.slab + slabs - 1, slabs), place.clip)
+    after = (lax.rem(place.slab + 1, slabs), place.clip)
+    lend = links.send(s.lent, s.borrowed, before)
+
+    @pl.loop(0, tok // chunk)
+    def _(i):
+        rows = mm(rows_of(s.attn_in, i, chunk), flat(whole_qkv)) + qkv_bias
+        put_rows(own, i, rows.astype(jnp.bfloat16))
+
+    groups_unit = unit // group
+
+    def window(ref, u, j):
+        begin = units[BEGIN_AT, u] + 2 * j
+        if j < groups_unit - 1:
+            return blocks(ref, begin, 2)
+        return jnp.concatenate([ref[begin], ref[units[SECOND_AT, u]]], 0)
+
+    def forward(u, j):
+        rows = window(own, u, j)
+        wrap = units[WRAP_AT, u] if j == groups_unit - 1 else 0
+        offsets = bias[wrap]
+        place_at = span(u * groups_unit + j, group)
+        for t in range(tiles):
+            cols = slice(128 * t, 128 * (t + 1))
+            queries = stacked(rows[:, cols])
+            keys = rows[:, width + 128 * t : width + 128 * (t + 1)]
+            values = rows[:, 2 * width + 128 * t : 2 * width + 128 * (t + 1)]
+            scores = mm_nt(keys, queries) * score_scale + offsets[:, cols]
+            weights = jnp.exp(scores - jnp.max(scores, 0, keepdims=True))
+            weights = weights / jnp.sum(weights, 0, keepdims=True)
+            s.probs[place_at, cols] = weights
+            mixed = folded(mm_tn(weights.astype(jnp.bfloat16), values))
+            mixed = mixed.astype(jnp.bfloat16).reshape(2, half, 128)
+            s.att_win[span(u * groups_unit + j, 2), :, cols] = mixed
+
+    def sweep(step, exchange, give_back, first, second, third):
+        @pl.loop(0, unit_count // 2)
+        def _(u):
+            for j in range(groups_unit - 1):
+                step(u, j)
+
+        first()
+        exchange()
+
+        @pl.loop(0, unit_count // 2)
+        def _(u):
+            step(2 * u, groups_unit - 1)
+            step(2 * u + 1, groups_unit - 1)
+
+        handle = give_back()
+        second()
+
+        @pl.loop(unit_count // 2, 3 * unit_count // 4)
+        def _(u):
+            for j in range(groups_unit - 1):
+                step(u, j)
+
+        third()
+
+        @pl.loop(3 * unit_count // 4, unit_count)
+        def _(u):
+            for j in range(groups_unit - 1):
+                step(u, j)
+
+        handle()
+
+    def give_back_from(ref, out, arrived):
+        def send():
+            for slot in range(slots):
+                out[slot] = ref[tails[slot]]
+            return take_lent(links.send(out, arrived, after), arrived, ref)
+
+        return send
+
+    def from_windows(ref, target, target_t=None):
+        @pl.loop(0, unit_count)
+        def _(u):
+            front = ref[units[FRONT_AT, u]]
+            back = blocks(ref, units[BACK_AT, u], per_unit - 1)
+            rows = jnp.concatenate([front, back], 0)
+            target[span(u, unit), :] = rows
+            if target_t is not None:
+                target_t[:, span(u, unit)] = rows.T
+
+    def take_lent(copy, arrived, ref):
+        def take():
+            copy.wait_recv()
+            ref[tok // half :] = arrived[...]
+
+        return take
+
+    def first():
+        proj_copy.third()
+        up_copy.third()
+
+    def second():
+        down_copy.second()
+        proj_copy.fourth()
+
+    def third():
+        up_copy.fourth()
+        down_copy.third()
+
+    sweep(
+        forward,
+        take_lent(lend, s.borrowed, own),
+        give_back_from(s.att_win, s.att_out, s.att_back),
+        first,
+        second,
+        third,
+    )
+    from_windows(s.att_win, s.att_rows, s.att_t)
+
+    proj_copy.end()
+    mid, mlp_in = s.mid, s.mlp_in
+
+    @pl.loop(0, tok // chunk)
+    def _(i):
+        rows = mm(s.att_rows[span(i, chunk), :], flat(whole_proj))
+        rows = xb[span(i, chunk), :].astype(jnp.float32) + rows + vectors[4:5, :]
+        mid[span(i, chunk), :] = rows
+        normed, _ = norm_parts(rows)
+        low = (normed * vectors[5:6, :] + vectors[6:7, :]).astype(jnp.bfloat16)
+        mlp_in[span(i, chunk), :] = low
+        s.mlp_in_t[:, span(i, chunk)] = low.T
+
+    up_copy.end()
+    down_copy.fourth()
+    act, slope = s.act, s.slope
+    wide = act.shape[1] // width
+
+    @pl.loop(0, wide)
+    def _(c):
+        cols = span(c, width)
+
+        @pl.loop(0, tok // chunk)
+        def _(i):
+            pre = mm(mlp_in[span(i, chunk), :], flat(whole_up, cols))
+            value, derivative = gelu_parts(pre + vectors[pl.ds(8 + c, 1), :])
+            act[span(i, chunk), cols] = value.astype(jnp.bfloat16)
+            slope[span(i, chunk), cols] = derivative.astype(jnp.bfloat16)
+
+    out_low = s.out_low
+    down_copy.end()
+
+    @pl.loop(0, tok // chunk)
+    def _(i):
+        rows = mid[span(i, chunk), :] + mm(act[span(i, chunk), :], flat(whole_down))
+        live = lax.broadcasted_iota(jnp.int32, (chunk, width), 0) + i * chunk < used
+        rows = jnp.where(live, rows + vectors[7:8, :], 0.0)
+        out_low[span(i, chunk), :] = rows.astype(jnp.bfloat16)
+
+    store_out = pltpu.make_async_copy(out_low, block_out, s.load_sems.at[0])
+    store_out.start()
+
+    down = down_flow.held
+
+    @pl.loop(0, clips)
+    def _(c):
+        size = act.shape[1] // clips
+        part = (mm(s.et[...], act[:, span(c, size)]) * grad_scale).astype(jnp.bfloat16)
+        part = part.reshape(slabs, 2, -1, size)
+        for h in range(2):
+            down[:, c % 2, h, c // 2] = part[:, h]
+
+    down_flow.begin()
+
+    @pl.loop(0, wide)
+    def _(c):
+        cols = span(c, width)
+        weights = whole_down.reshape(wide, width, width)[c]
+
+        def step(i, sums):
+            grad = mm_nt(eb[span(i, chunk), :], weights)
+            low = grad * slope[span(i, chunk), cols].astype(jnp.float32)
+            low = low.astype(jnp.bfloat16)
+            slope[span(i, chunk), cols] = low
+            return sums + jnp.sum(low.astype(jnp.float32), 0, keepdims=True)
+
+        sums = lax.fori_loop(0, tok // chunk, step, jnp.zeros((1, width), jnp.float32))
+        s.up_sum[pl.ds(c, 1), :] = sums
+
+    up = up_flow.held
+
+    def keep(target, slab, part):
+        part = (part * grad_scale).astype(jnp.bfloat16)
+        part = part.reshape(clips // 2, 2, 2, -1, part.shape[-1])
+        for y in range(2):
+            for h in range(2):
+                target[slab, y, h] = part[:, y, h]
+
+    @pl.loop(0, slabs)
+    def _(i):
+        keep(up, i, mm(s.mlp_in_t[...], slope[:, span(i, act.shape[1] // slabs)]))
+
+    up_flow.begin()
+    down_flow.second()
+
+    mid_grad, mid_low = s.mid_grad, s.mid_low
+
+    def mid_step(i, sums):
+        grad = mm_nt(slope[span(i, chunk), :], flat(whole_up))
+        normed, inverse = norm_parts(mid[span(i, chunk), :])
+        out_grad = eb[span(i, chunk), :].astype(jnp.float32)
+        rows = out_grad + norm_back(normed, inverse, grad * vectors[5:6, :])
+        low = rows.astype(jnp.bfloat16)
+        mid_grad[span(i, chunk), :] = rows
+        put_rows(mid_low, i, low)
+        return tuple(
+            old + jnp.sum(new, 0, keepdims=True)
+            for old, new in zip(sums, (low.astype(jnp.float32), grad * normed, grad, out_grad))
+        )
+
+    zero = jnp.zeros((1, width), jnp.float32)
+    mid_sums = lax.fori_loop(0, tok // chunk, mid_step, (zero,) * 4)
+    for row, value in zip((4, 5, 6, 7), mid_sums):
+        small.held[0, row : row + 1, :] = value * grad_scale
+    small.held[0, 8:12, :] = s.up_sum[...] * grad_scale
+    up_flow.second()
+
+    proj_columns = flat(whole_proj)
+    head_low = jnp.concatenate(
+        [mid_low[heads[i]] for i in range(slots)], 0
+    )
+    put_rows(s.dlent, 0, mm_nt(head_low, proj_columns).astype(jnp.bfloat16))
+    lend_back = links.send(s.dlent, s.dborrowed, before)
+    dwin_own = s.dwin_own
+
+    @pl.loop(0, tok // chunk)
+    def _(i):
+        rows = mm_nt(rows_of(mid_low, i, chunk), flat(whole_proj))
+        put_rows(dwin_own, i, rows.astype(jnp.bfloat16))
+
+    grad = mm(s.att_t[...], mid_low[...].reshape(tok, width))
+    for i in range(slabs):
+        keep(proj_flow.held, i, grad[:, i * (width // slabs) : (i + 1) * (width // slabs)])
+    proj_flow.begin()
+    down_flow.third()
+
+    bias_grad, qg_win = s.bias_grad, s.qg_win
+    bias_grad[...] = jnp.zeros_like(bias_grad)
+
+    def backward(u, j):
+        rows = window(own, u, j)
+        grads = window(dwin_own, u, j)
+        place_at = span(u * groups_unit + j, group)
+        for t in range(tiles):
+            cols = slice(128 * t, 128 * (t + 1))
+            queries = stacked(rows[:, cols])
+            keys = rows[:, width + 128 * t : width + 128 * (t + 1)]
+            values = rows[:, 2 * width + 128 * t : 2 * width + 128 * (t + 1)]
+            mixed = stacked(grads[:, cols])
+            weights = s.probs[place_at, cols]
+            prob_grad = mm_nt(values, mixed)
+            value_grad = mm(weights.astype(jnp.bfloat16), mixed)
+            inner = jnp.sum(weights * prob_grad, 0, keepdims=True)
+            score = (weights * (prob_grad - inner)).astype(jnp.bfloat16)
+            bias_grad[:, cols] += score.astype(jnp.float32)
+            key_grad = mm(score, queries) * score_scale
+            query_grad = folded(mm_tn(score, keys)) * score_scale
+            for k, value in enumerate((query_grad, key_grad, value_grad)):
+                at = slice(k * width + 128 * t, k * width + 128 * (t + 1))
+                value = value.astype(jnp.bfloat16).reshape(2, half, 128)
+                qg_win[span(u * groups_unit + j, 2), :, at] = value
+
+    def second_back():
+        proj_flow.second()
+
+    sweep(
+        backward,
+        take_lent(lend_back, s.dborrowed, dwin_own),
+        give_back_from(qg_win, s.qg_out, s.qg_back),
+        up_flow.third,
+        second_back,
+        down_flow.fourth,
+    )
+    qg_rows = s.qg_rows
+    from_windows(qg_win, qg_rows)
+
+    pair = 2
+    for i in range(slabs // pair):
+        size = 3 * width // slabs
+        grad = mm(s.attn_in_t[...], qg_rows[:, i * pair * size : (i + 1) * pair * size])
+        for k in range(pair):
+            keep(qkv_flow.held, i * pair + k, grad[:, k * size : (k + 1) * size])
+    qkv_flow.begin()
+    proj_flow.third()
+    up_flow.fourth()
+
+    def in_step(i, sums):
+        rows = qg_rows[span(i, chunk), :]
+        grad = mm_nt(rows, flat(whole_qkv))
+        normed, inverse = norm_parts(xb[span(i, chunk), :].astype(jnp.float32))
+        mid[span(i, chunk), :] = mid_grad[span(i, chunk), :] + norm_back(
+            normed, inverse, grad * vectors[0:1, :]
+        )
+        query_part = rows[:, :width].astype(jnp.float32)
+        value_part = rows[:, 2 * width :].astype(jnp.float32)
+        return tuple(
+            old + jnp.sum(new, 0, keepdims=True)
+            for old, new in zip(sums, (grad * normed, grad, query_part, value_part))
+        )
+
+    in_sums = lax.fori_loop(0, tok // chunk, in_step, (zero,) * 4)
+    store_grad = pltpu.make_async_copy(mid, x_grad, s.load_sems.at[1])
+    store_grad.start()
+    for row, value in zip((0, 1, 2, 3), in_sums):
+        small.held[0, row : row + 1, :] = value * grad_scale
+
+    by_head = bias_grad[...]
+    for r in range(RELS):
+        picked = jnp.sum(jnp.where(offset == r, by_head, 0.0), 0, keepdims=True)
+        s.att_sum[r : r + 1, :] = picked
+    s.att_sum[RELS:, :] = jnp.zeros((128 - RELS, width), jnp.float32)
+    sums = lax.dot_general(
+        spread, s.att_sum[...], (((1,), (1,)), ((), ())), precision=HIGHEST
+    ) * grad_scale
+    for i in range(width // 128):
+        small.held[0, 12:16, 128 * i : 128 * (i + 1)] = sums[4 * i : 4 * i + 4, :]
+
+    qkv_flow.second()
+    small.begin()
+    proj_flow.fourth()
+    small.second()
+    qkv_flow.third()
+    small.third()
+    qkv_flow.fourth()
+    small.fourth()
+    for flow, out in zip(flows, owned):
+        first, last = flow.end()
+        if flow is down_flow:
+            out[...] = jnp.concatenate([first, last], 0).T
+        else:
+            rows = first.shape[0]
+            out[:rows, :] = first
+            out[rows:, :] = last
+    small_out[...] = small.end()
+    store_out.wait()
+    store_grad.wait()
+    links.drain()
+
+
+BEGIN_AT, SECOND_AT, FRONT_AT, BACK_AT, WRAP_AT, HEADS_AT, TAILS_AT, USED_AT = range(8)
+
+
+def unit_table(lengths, slab_size, tok):
+    unit, half = SHORT // slab_size * BINS, WIN // 2 * BINS
+    count, size = tok // unit, unit // half
+    at = jnp.arange(count, dtype=jnp.int32)
+    segment = lengths // slab_size * BINS // unit
+    ends = jnp.cumsum(segment)
+    starts = ends - segment
+    slots = jnp.arange(1, lengths.shape[0] + 1, dtype=jnp.int32)
+    here = (starts[:, None] <= at) & (at < ends[:, None])
+    inside = jnp.sum(here, 0)
+    last = jnp.sum(jnp.where(here & (ends[:, None] == at + 1), slots[:, None], 0), 0)
+    first = jnp.sum(jnp.where(here & (starts[:, None] == at), slots[:, None], 0), 0)
+    begin = at * size + inside
+    front = jnp.maximum(at * size - inside, 0)
+    blocks_own = tok // half
+    pad = (0, count - lengths.shape[0])
+    return jnp.stack([
+        begin,
+        jnp.where(last > 0, blocks_own + last - 1, begin + size - 1),
+        jnp.where(first > 0, blocks_own + first - 1, front),
+        at * size - inside + 1,
+        ((last > 0) & (lax.axis_index(SLAB) == slab_size - 1)).astype(jnp.int32),
+        jnp.pad(jnp.minimum(starts, count - 1) * size, pad),
+        jnp.pad(jnp.maximum(ends * size - 1, 0), pad),
+        jnp.full((count,), ends[-1] * unit),
+    ]).astype(jnp.int32)
+
+
+def block_call(tokens, y_grad, clip_rows, vectors, table, masters, slab_size, clip_size):
+    vmem, smem, anywhere = (
+        pl.BlockSpec(memory_space=pltpu.VMEM),
+        pl.BlockSpec(memory_space=pltpu.SMEM),
+        pl.BlockSpec(memory_space=pl.ANY),
+    )
     depth = clip_size // 2
+    tok, width = tokens.shape
+    hidden = masters[2].shape[1] * slab_size
+    slots = clip_rows.shape[1]
+    half = WIN // 2 * BINS
+    low, full = jnp.bfloat16, jnp.float32
     helds = []
-    for grad in grads:
-        rows, columns = grad.shape[0] // clip_size // 2, grad.shape[1] // 4
-        held = grad.reshape(depth, 2, 2, rows, 4, columns).transpose(4, 1, 2, 0, 3, 5)
-        helds.append(held.astype(jnp.bfloat16))
-    copies = 4 * (2 + 4 + 2 + 2 * (depth - 1)) + 3 + depth - 1
-    scratch = [
-        pltpu.SemaphoreType.DMA((copies,)),
-        pltpu.SemaphoreType.DMA((copies,)),
-        pltpu.VMEM((3,) + small.shape, jnp.float32),
-        pltpu.VMEM((3,) + small.shape, jnp.float32),
-        pltpu.VMEM((depth,) + small.shape, jnp.float32),
-        pltpu.SemaphoreType.DMA((4,)),
+    for position, master in enumerate(masters):
+        rows, columns = master.shape if position < 3 else master.shape[::-1]
+        helds.append((slab_size, 2, 2, depth, rows // 2, columns))
+    def buffer(*sizes):
+        kind = full if sizes[-1] is full else low
+        return pltpu.VMEM(sizes[:-1] if sizes[-1] is full else sizes, kind)
+
+    def whole(master):
+        return buffer(depth, 2, 2, master.shape[0] // 2, slab_size * master.shape[1])
+
+    held = Held(
+        xb=buffer(tok, width), eb=buffer(tok, width), et=buffer(width, tok),
+        attn_in=buffer(tok // half, half, width), attn_in_t=buffer(width, tok),
+        own=buffer(tok // half + slots, half, 3 * width), lent=buffer(slots, half, 3 * width),
+        borrowed=buffer(slots, half, 3 * width),
+        probs=buffer(tok, width, full), att_win=buffer(tok // half + slots, half, width),
+        att_out=buffer(slots, half, width), att_back=buffer(slots, half, width), att_rows=buffer(tok, width), att_t=buffer(width, tok),
+        mid=buffer(tok, width, full), mlp_in=buffer(tok, width), mlp_in_t=buffer(width, tok),
+        act=buffer(tok, hidden), slope=buffer(tok, hidden), mid_grad=buffer(tok, width, full),
+        mid_low=buffer(tok // half, half, width), dwin_own=buffer(tok // half + slots, half, width), dlent=buffer(slots, half, width),
+        dborrowed=buffer(slots, half, width), qg_win=buffer(tok // half + slots, half, 3 * width),
+        qg_out=buffer(slots, half, 3 * width), qg_back=buffer(slots, half, 3 * width), qg_rows=buffer(tok, 3 * width),
+        bias=buffer(2, WIN * BINS, width, full), bias_grad=buffer(WIN * BINS, width, full),
+        up_sum=buffer(hidden // width, width, full), att_sum=buffer(128, width, full),
+        out_low=buffer(tok, width),
+        load_sems=pltpu.SemaphoreType.DMA((2,)),
+        whole_qkv=whole(masters[0]), whole_proj=whole(masters[1]),
+        whole_up=whole(masters[2]), whole_down=whole(masters[3]),
+    )
+    copies = 4 * (2 * (depth - 1) + 9) + 4 * (2 + 4 + 2 + 2 * (depth - 1)) + 3 + depth - 1 + 4
+    scratch = [pltpu.SemaphoreType.DMA((copies,)), pltpu.SemaphoreType.DMA((copies,)), *held]
+    small = (16, width)
+    scratch += [
+        pltpu.VMEM((3,) + small, full), pltpu.VMEM((3,) + small, full), pltpu.VMEM((depth,) + small, full)
     ]
-    for held in helds:
-        scratch += [pltpu.VMEM(held.shape, held.dtype)] + scatter_buffers(held.shape)
+    for sizes in helds:
+        scratch += [pltpu.VMEM(sizes, low)] + scatter_buffers(sizes)
     return pl.pallas_call(
-        functools.partial(scatter_kernel, clip_size, [h.shape for h in helds]),
-        out_shape=[jax.ShapeDtypeStruct(small.shape, jnp.float32)]
-        + [jax.ShapeDtypeStruct((2 * h.shape[4], h.shape[5]), jnp.float32) for h in helds],
-        in_specs=[vmem] + [pl.BlockSpec(memory_space=pl.ANY)] * 4,
-        out_specs=[vmem] * 5,
+        functools.partial(block_kernel, slab_size, clip_size),
+        out_shape=[
+            jax.ShapeDtypeStruct((tok, width), low),
+            jax.ShapeDtypeStruct((tok, width), full),
+            jax.ShapeDtypeStruct(small, full),
+        ]
+        + [jax.ShapeDtypeStruct(m.shape, full) for m in masters],
+        in_specs=[anywhere, anywhere, smem] + [vmem] * 6,
+        out_specs=[anywhere, anywhere] + [vmem] * 5,
         scratch_shapes=scratch,
         compiler_params=pltpu.CompilerParams(
-            collective_id=1, has_side_effects=True, vmem_limit_bytes=48 << 20
+            collective_id=0, has_side_effects=True, vmem_limit_bytes=62 << 20
         ),
-        name="scatter_grads",
-    )(small, *helds)
+        name="block",
+    )(tokens, y_grad, unit_table(clip_rows[0], slab_size, tok), vectors, table, *masters)
 
 
 def shards(
@@ -500,15 +1057,34 @@
     table_m,
     table_v,
 ):
+    slab_size, clip_size = lax.axis_size(SLAB), lax.axis_size(CLIP)
+    masters = (qkv_weight, proj_weight, up_weight, down_weight)
+    hidden = up_weight.shape[1] * slab_size
+    aligned = slab_size == 4 and clip_size % 2 == 0 and all(m.shape[0] % 32 == 0 for m in masters)
+    if aligned and hidden // (clip_size // 2) == tokens.shape[-1]:
+        block_out, x_grad, small, *owned = block_call(
+            tokens[0, 0], y_grad[0, 0], clip_rows, vectors, table, masters, slab_size, clip_size
+        )
+        results = [block_out[None, None], x_grad[None, None]]
+        moments = ((qkv_m, qkv_v), (proj_m, proj_v), (up_m, up_v), (down_m, down_v))
+        for master, (first, second), grad in zip(masters, moments, owned):
+            results += adamw(master, first, second, grad, rate_matrix, weight_decay)
+        rows = vectors.shape[0]
+        results += adamw(vectors, vectors_m, vectors_v, small[:rows], rate_vector, 0.0)
+        by_head = small[rows : rows + 4].reshape(4, -1, 128).transpose(1, 0, 2).reshape(-1, 128)
+        results += adamw(
+            table, table_m, table_v, by_head[: table.shape[1], :RELS].T, rate_vector, 0.0
+        )
+        return tuple(results)
     lengths = clip_rows[0]
-    slab_count = lax.axis_size("slab")
+    slab_count = lax.axis_size(SLAB)
     inputs = tokens[0, 0].astype(jnp.float32)
     tok_count, width = inputs.shape
     rows_dev = tok_count // BINS
     head_dim = width // HEADS
     score_scale = head_dim ** (-0.5)
     source, time_wraps, seg_starts = window_rows(
-        lengths, lax.axis_index("slab"), slab_count, rows_dev
+        lengths, lax.axis_index(SLAB), slab_count, rows_dev
     )
     total_rows = rows_dev + 2 * lengths.shape[0]
     head_rows = jnp.minimum(
@@ -525,24 +1101,18 @@
     )
     used_rows = jnp.sum(lengths) // slab_count
     live_rows = (jnp.arange(tok_count) // BINS < used_rows).astype(jnp.float32)[:, None]
-    masters = (qkv_weight, proj_weight, up_weight, down_weight)
-    clip_size = lax.axis_size("clip")
-    aligned = slab_count == 4 and clip_size % 2 == 0 and all(m.shape[0] % 32 == 0 for m in masters)
-    if aligned:
-        copies = gather_all(masters, clip_size)
-    else:
-        part_copies = (
-            lax.all_gather(qkv_weight.astype(jnp.bfloat16), "clip", axis=0, tiled=True),
-            lax.all_gather(proj_weight.astype(jnp.bfloat16), "clip", axis=0, tiled=True),
-            lax.all_gather(up_weight.astype(jnp.bfloat16), "clip", axis=0, tiled=True),
-            lax.all_gather(down_weight.astype(jnp.bfloat16), "clip", axis=0, tiled=True),
-        )
-        copies = (
-            lax.all_gather(part_copies[0], "slab", axis=1, tiled=True),
-            lax.all_gather(part_copies[1], "slab", axis=1, tiled=True),
-            lax.all_gather(part_copies[2], "slab", axis=1, tiled=True),
-            lax.all_gather(part_copies[3], "slab", axis=1, tiled=True),
-        )
+    part_copies = (
+        lax.all_gather(qkv_weight.astype(jnp.bfloat16), CLIP, axis=0, tiled=True),
+        lax.all_gather(proj_weight.astype(jnp.bfloat16), CLIP, axis=0, tiled=True),
+        lax.all_gather(up_weight.astype(jnp.bfloat16), CLIP, axis=0, tiled=True),
+        lax.all_gather(down_weight.astype(jnp.bfloat16), CLIP, axis=0, tiled=True),
+    )
+    copies = (
+        lax.all_gather(part_copies[0], SLAB, axis=1, tiled=True),
+        lax.all_gather(part_copies[1], SLAB, axis=1, tiled=True),
+        lax.all_gather(part_copies[2], SLAB, axis=1, tiled=True),
+        lax.all_gather(part_copies[3], SLAB, axis=1, tiled=True),
+    )
     qkv_copy, proj_copy, up_copy, down_copy = copies
     attn_input = affine_norm(inputs, vectors[0], vectors[1]).astype(jnp.bfloat16)
     bias_row = jnp.concatenate([vectors[2], jnp.zeros_like(vectors[2]), vectors[3]])
@@ -550,7 +1120,7 @@
         jnp.dot(attn_input, qkv_copy, preferred_element_type=jnp.float32) + bias_row
     ).astype(jnp.bfloat16)
     qkv_grid = qkv_rows.reshape(rows_dev, BINS, 3 * width)
-    borrowed = from_behind(qkv_grid[head_rows], "slab", -1)
+    borrowed = from_behind(qkv_grid[head_rows], SLAB, -1)
     qkv_windows = to_windows(jnp.concatenate([qkv_grid, borrowed], 0), source)
     query_win = qkv_windows[:, :, :width].reshape(windows_count, WIN * WIN, HEADS, head_dim)
     key_win = qkv_windows[:, :, width : 2 * width].reshape(
@@ -575,7 +1145,7 @@
     )
     attended = attended.astype(jnp.bfloat16).reshape(windows_count, WIN * WIN, width)
     spread_out = from_windows(attended, source, total_rows)
-    returned = from_behind(spread_out[rows_dev:], "slab", 1)
+    returned = from_behind(spread_out[rows_dev:], SLAB, 1)
     attended_rows = spread_out[:rows_dev].at[head_rows].add(returned).reshape(tok_count, width)
     residual = (
         inputs + jnp.dot(attended_rows, proj_copy, preferred_element_type=jnp.float32) + vectors[4]
@@ -607,7 +1177,7 @@
         jnp.bfloat16
     )
     mixed_grid = mixed_grad.reshape(rows_dev, BINS, width)
-    sent_back = from_behind(mixed_grid[head_rows], "slab", -1)
+    sent_back = from_behind(mixed_grid[head_rows], SLAB, -1)
     grad_windows = to_windows(jnp.concatenate([mixed_grid, sent_back], 0), source)
     grad_windows = grad_windows.reshape(windows_count, WIN * WIN, HEADS, head_dim)
     probs = jnp.exp(scores_of(query_win, key_win) - top_score) / exp_sum
@@ -643,7 +1213,7 @@
         -1,
     ).astype(jnp.bfloat16)
     qkv_spread = from_windows(qkv_grad_win, source, total_rows)
-    given_back = from_behind(qkv_spread[rows_dev:], "slab", 1)
+    given_back = from_behind(qkv_spread[rows_dev:], SLAB, 1)
     qkv_grad_rows = (
         qkv_spread[:rows_dev].at[head_rows].add(given_back).reshape(tok_count, 3 * width)
     )
@@ -671,40 +1241,28 @@
         ],
         0,
     )
-    grad_scale = float(tok_count * slab_count * lax.axis_size("clip")) ** (-0.5)
-    if aligned:
-        size = vector_grad.size + table_grad.size
-        flat = jnp.concatenate([vector_grad.reshape(-1), table_grad.reshape(-1)]) * grad_scale
-        flat = jnp.pad(flat, (0, -size % (8 * width))).reshape(-1, width)
-        grads = [g * grad_scale for g in (qkv_w_grad, proj_grad, up_grad, down_grad)]
-        summed, *owned = scatter_all(flat, grads, clip_size)
-        summed = summed.reshape(-1)
-        small_sums = (
-            summed[: vector_grad.size].reshape(vector_grad.shape),
-            summed[vector_grad.size : size].reshape(table_grad.shape),
-        )
-    else:
-        part_sums = (
-            lax.psum_scatter(
-                (qkv_w_grad * grad_scale).astype(jnp.bfloat16), "slab", scatter_dimension=1, tiled=True
-            ).astype(jnp.float32),
-            lax.psum_scatter(
-                (proj_grad * grad_scale).astype(jnp.bfloat16), "slab", scatter_dimension=1, tiled=True
-            ).astype(jnp.float32),
-            lax.psum_scatter(
-                (up_grad * grad_scale).astype(jnp.bfloat16), "slab", scatter_dimension=1, tiled=True
-            ).astype(jnp.float32),
-            lax.psum_scatter(
-                (down_grad * grad_scale).astype(jnp.bfloat16), "slab", scatter_dimension=1, tiled=True
-            ).astype(jnp.float32),
-        )
-        owned = (
-            lax.psum_scatter(part_sums[0], "clip", scatter_dimension=0, tiled=True),
-            lax.psum_scatter(part_sums[1], "clip", scatter_dimension=0, tiled=True),
-            lax.psum_scatter(part_sums[2], "clip", scatter_dimension=0, tiled=True),
-            lax.psum_scatter(part_sums[3], "clip", scatter_dimension=0, tiled=True),
-        )
-        small_sums = lax.psum((vector_grad * grad_scale, table_grad * grad_scale), ("slab", "clip"))
+    grad_scale = float(tok_count * slab_count * lax.axis_size(CLIP)) ** (-0.5)
+    part_sums = (
+        lax.psum_scatter(
+            (qkv_w_grad * grad_scale).astype(jnp.bfloat16), SLAB, scatter_dimension=1, tiled=True
+        ).astype(jnp.float32),
+        lax.psum_scatter(
+            (proj_grad * grad_scale).astype(jnp.bfloat16), SLAB, scatter_dimension=1, tiled=True
+        ).astype(jnp.float32),
+        lax.psum_scatter(
+            (up_grad * grad_scale).astype(jnp.bfloat16), SLAB, scatter_dimension=1, tiled=True
+        ).astype(jnp.float32),
+        lax.psum_scatter(
+            (down_grad * grad_scale).astype(jnp.bfloat16), SLAB, scatter_dimension=1, tiled=True
+        ).astype(jnp.float32),
+    )
+    owned = (
+        lax.psum_scatter(part_sums[0], CLIP, scatter_dimension=0, tiled=True),
+        lax.psum_scatter(part_sums[1], CLIP, scatter_dimension=0, tiled=True),
+        lax.psum_scatter(part_sums[2], CLIP, scatter_dimension=0, tiled=True),
+        lax.psum_scatter(part_sums[3], CLIP, scatter_dimension=0, tiled=True),
+    )
+    small_sums = lax.psum((vector_grad * grad_scale, table_grad * grad_scale), (SLAB, CLIP))
     qkv_new, qkv_m_new, qkv_v_new = adamw(
         qkv_weight, qkv_m, qkv_v, owned[0], rate_matrix, weight_decay
     )
@@ -751,21 +1309,21 @@
         shards,
         mesh=mesh,
         in_specs=(
-            P("clip", "slab", None, None),
-            P("clip", "slab", None, None),
-            P("clip", None),
-            P("clip", "slab"),
-            P("clip", "slab"),
-            P("clip", "slab"),
-            P("clip", "slab"),
-            P("clip", "slab"),
-            P("clip", "slab"),
-            P("clip", "slab"),
-            P("clip", "slab"),
-            P("clip", "slab"),
-            P("clip", "slab"),
-            P("clip", "slab"),
-            P("clip", "slab"),
+            P(CLIP, SLAB, None, None),
+            P(CLIP, SLAB, None, None),
+            P(CLIP, None),
+            P(CLIP, SLAB),
+            P(CLIP, SLAB),
+            P(CLIP, SLAB),
+            P(CLIP, SLAB),
+            P(CLIP, SLAB),
+            P(CLIP, SLAB),
+            P(CLIP, SLAB),
+            P(CLIP, SLAB),
+            P(CLIP, SLAB),
+            P(CLIP, SLAB),
+            P(CLIP, SLAB),
+            P(CLIP, SLAB),
             P(),
             P(),
             P(),
@@ -774,20 +1332,20 @@
             P(),
         ),
         out_specs=(
-            P("clip", "slab", None, None),
-            P("clip", "slab", None, None),
-            P("clip", "slab"),
-            P("clip", "slab"),
-            P("clip", "slab"),
-            P("clip", "slab"),
-            P("clip", "slab"),
-            P("clip", "slab"),
-            P("clip", "slab"),
-            P("clip", "slab"),
-            P("clip", "slab"),
-            P("clip", "slab"),
-            P("clip", "slab"),
-            P("clip", "slab"),
+            P(CLIP, SLAB, None, None),
+            P(CLIP, SLAB, None, None),
+            P(CLIP, SLAB),
+            P(CLIP, SLAB),
+            P(CLIP, SLAB),
+            P(CLIP, SLAB),
+            P(CLIP, SLAB),
+            P(CLIP, SLAB),
+            P(CLIP, SLAB),
+            P(CLIP, SLAB),
+            P(CLIP, SLAB),
+            P(CLIP, SLAB),
+            P(CLIP, SLAB),
+            P(CLIP, SLAB),
             P(),
             P(),
             P(),

time: 483 us -> 160 us (0.33); the launches traced: 476 us -> 160 us
  local copies, waits for them, and re-layouts: 216 us -> 5.82 us
  matrix products: 111 us -> 0 us
  Pallas kernels: 96 us -> 143 us
  other arithmetic: 41.1 us -> 9.58 us
  waiting for transfers between devices: 5.73 us -> 0 us
    dot_general x19 -> x0, matrix products: 99.3 us -> none  [the longest x1 22.9 us: shards(): jnp.dot(mlp_input, up_copy, preferred_element_type=jnp.float32)]
    pallas_call x2 -> x1, Pallas kernels: 96 us -> 143 us  [block_call(): pl.pallas_call(functools.partial(block_kernel, slab_size, clip_size), out...]
    scatter x2 -> x0, local copies, waits for them, and re-layouts: 34.2 us -> none  [from_windows(): blank.at[source.reshape(-1)]]
    reshape x11 -> x1, local copies, waits for them, and re-layouts: 29.8 us -> 0.02 us  [shards(): small[rows:rows + 4].reshape(4, -1, 128).transpose(1, 0, 2).reshape(-1, 128)]
    slice x20 -> x2, local copies, waits for them, and re-layouts: 29.2 us -> 1.4 us  [the longest x1 0.82 us: shards(): small[rows:rows + 4].reshape(4, -1, 128).transpose(1, 0, 2).reshape(-1, 128)]
    concatenate x8 -> x0, local copies, waits for them, and re-layouts: 27.3 us -> none  [the longest x3 19.9 us: shards(): jnp.concatenate([query_grad.reshape(windows_count, WIN * WIN, width), key...]
    convert_element_type x9 -> x0, local copies, waits for them, and re-layouts: 22.7 us -> none  [the longest x8 19.7 us: scatter_all(): helds.append(held.astype(jnp.bfloat16))]
    reduce_sum x13 -> x1, other arithmetic: 18.7 us -> 0.09 us  [unit_table(): jnp.sum(jnp.where(here & (starts[:, None] == at), slots[:, None], 0), 0)]
  transfers between devices with their start and end apart: 4 -> 0, of which waited for: 2 -> 0; matrix products, arithmetic and copies ran while one was open for 7% -> 0% of each run, Pallas kernels for 0% -> 0%
where the time goes in v2:
time: 160 us
  Pallas kernels  143 us (89%)
  other arithmetic  9.58 us (6%)
  local copies, waits for them, and re-layouts  5.82 us (4%)
    pallas_call x1, Pallas kernels, block_call(): pl.pallas_call(functools.partial(block_kernel, slab_size, clip_size), out...  143 us
    sub x6, other arithmetic, adamw(): return (weight - rate * (update + decay * weight), first, second)  7.72 us
    unnamed x45, local copies, waits for them, and re-layouts  3.78 us

profile of v2, /device:TPU:0, one launch (start us, length us, event | category | flops | bytes accessed | tf_op | source)
XLA Modules:
  0.0 159.7 jit_solution(8931670768526052486)
XLA Ops:
  0.7 0.0 copy-start.18
  0.7 0.0 copy-start.5
  0.7 0.0 copy-start.2
  0.7 0.0 copy-start.6
  0.7 0.0 copy-start.4
  0.7 0.0 copy-start.20
  0.7 0.0 copy-start.19
  0.7 0.0 copy-start.15
  0.8 0.0 copy-start.14
  0.8 0.0 copy-start.8
  0.8 0.0 copy-start.17
  0.8 0.0 copy-start.13
  0.8 0.0 copy-start.7
  0.8 0.0 copy-start.16
  0.8 0.0 copy-start.12
  0.8 0.9 and_select_fusion.2
  1.7 0.2 broadcast_in_dim.40
  1.9 0.6 slice.13
  3.2 0.7 minimum_multiply_fusion
  3.8 0.1 select_reduce_fusion
  4.0 0.6 stack.16.refs_2_
  4.6 1.4 copy.43.refs_4_
  6.0 0.0 copy-start.3
  6.0 0.0 copy-start.9
  6.0 0.0 copy-start.10
  6.0 142.8 %block.1 = (bf16[1024,512]{1,0:T(8,128)(2,1)}, f32[1024,512]{1,0:T(8,128)}, f32[16,512]{1,0:T(8,128)}, f32[64,384]{1,0:T(8,128)}, f32[64,128]{1,0:T(8,128)}, /*index=5*/f32[64,512]{1,0:T(8,128)}, f32[256,128]{1,0:T(8,128)}) custom-call(bf16[1024,512]{1,0:T(8,128)(2,1)} %bitcast.65, bf16[1024,512]{1,0:T(8,128)(2,1)} %bitcast.66, s32[8,8]{1,0:T(8,128)} %stack.16.refs_2_, ...), custom_call_target="tpu_custom_call" | custom-call | tf_op jit(solution)/shard_map/block/pallas_call | solution.py:1019
  148.8 0.0 copy-start.11
  148.8 0.0 copy-start.1
  148.8 0.8 slice.15
  149.6 0.0 copy-done.18
  149.6 0.0 copy-done.20
  149.6 0.0 copy-done.19
  149.6 0.6 multiply_subtract_fusion.5
  150.3 0.0 copy-done.5
  150.3 0.0 copy-done.15
  150.3 0.0 copy-done.14
  150.3 1.4 multiply_subtract_fusion.3
  151.7 0.0 copy-done.6
  151.7 0.0 copy-done.17
  151.7 0.0 copy-done.16
  151.7 1.4 multiply_subtract_fusion.4
  153.1 0.0 copy-done.4
  153.1 0.0 copy-done.13
  153.1 0.0 copy-done.12
  153.1 1.6 %multiply_subtract_fusion.2 = (f32[64,384]{1,0:T(8,128)}, f32[64,384]{1,0:T(8,128)}, f32[64,384]{1,0:T(8,128)}) fusion(f32[64,384]{1,0:T(8,128)S(1)} %copy-done.4, f32[64,384]{1,0:T(8,128)} %get-tuple-element.29, f32[64,384]{1,0:T(8,128)S(1)} %copy-done.12, f32[64,384]{1,0:T(8,128)S(1)} %copy-done.13), kind=kLoop, calls=%fused_computation.11 | loop fusion | flops 344064 | bytes 688128 | tf_op jit(solution)/shard_map/sub | solution.py:122
  154.8 0.0 copy-start
  154.8 0.0 copy-done.2
  154.8 0.0 copy-done.8
  154.8 0.0 copy-done.7
  154.8 1.8 %multiply_subtract_fusion.1 = (f32[64,512]{1,0:T(8,128)}, f32[64,512]{1,0:T(8,128)}, f32[64,512]{1,0:T(8,128)}) fusion(f32[64,512]{1,0:T(8,128)S(1)} %copy-done.2, f32[64,512]{1,0:T(8,128)} %get-tuple-element.31, f32[64,512]{1,0:T(8,128)S(1)} %copy-done.7, f32[64,512]{1,0:T(8,128)S(1)} %copy-done.8), kind=kLoop, calls=%fused_computation.9 | loop fusion | flops 458752 | bytes 917504 | tf_op jit(solution)/shard_map/sub | solution.py:122
  156.6 0.0 copy-done.3
  156.6 0.0 copy-done.9
  156.6 0.0 copy-done.10
  156.6 0.0 copy-done.11
  156.6 0.8 multiply_subtract_fusion
  157.4 0.0 copy-done.1
  157.4 1.0 copy.47
  158.4 0.0 copy-done
  158.4 1.3 copy.48
  (8 shorter events, 0.1 us)
Async XLA Ops:
  0.7 149.0 %copy-start.18 = (f32[49,16]{0,1:T(8,128)S(1)}, f32[49,16]{0,1:T(8,128)}, u32[]{:S(2)}) copy-start(f32[49,16]{0,1:T(8,128)} %param.39) | copy-start | bytes 9412
  0.7 149.6 %copy-start.5 = (f32[12,512]{1,0:T(8,128)S(1)}, f32[12,512]{1,0:T(8,128)}, u32[]{:S(2)}) copy-start(f32[12,512]{1,0:T(8,128)} %refs_3_.1) | copy-start | bytes 73732
  0.7 154.1 %copy-start.2 = (f32[64,512]{1,0:T(8,128)S(1)}, f32[64,512]{1,0:T(8,128)}, u32[]{:S(2)}) copy-start(f32[64,512]{1,0:T(8,128)} %refs_7_.1) | copy-start | bytes 393220
  0.7 151.0 %copy-start.6 = (f32[64,128]{1,0:T(8,128)S(1)}, f32[64,128]{1,0:T(8,128)}, u32[]{:S(2)}) copy-start(f32[64,128]{1,0:T(8,128)} %refs_6_.1) | copy-start | bytes 98308
  0.7 152.4 %copy-start.4 = (f32[64,384]{1,0:T(8,128)S(1)}, f32[64,384]{1,0:T(8,128)}, u32[]{:S(2)}) copy-start(f32[64,384]{1,0:T(8,128)} %refs_5_.1) | copy-start | bytes 294916
  0.7 148.9 %copy-start.20 = (f32[49,16]{0,1:T(8,128)S(1)}, f32[49,16]{0,1:T(8,128)}, u32[]{:S(2)}) copy-start(f32[49,16]{0,1:T(8,128)} %param.41) | copy-start | bytes 9412
  0.7 148.9 %copy-start.19 = (f32[49,16]{0,1:T(8,128)S(1)}, f32[49,16]{0,1:T(8,128)}, u32[]{:S(2)}) copy-start(f32[49,16]{0,1:T(8,128)} %param.40) | copy-start | bytes 9412
  0.7 149.5 %copy-start.15 = (f32[12,512]{1,0:T(8,128)S(1)}, f32[12,512]{1,0:T(8,128)}, u32[]{:S(2)}) copy-start(f32[12,512]{1,0:T(8,128)} %param.38) | copy-start | bytes 73732
  0.8 149.5 %copy-start.14 = (f32[12,512]{1,0:T(8,128)S(1)}, f32[12,512]{1,0:T(8,128)}, u32[]{:S(2)}) copy-start(f32[12,512]{1,0:T(8,128)} %param.37) | copy-start | bytes 73732
  0.8 154.0 %copy-start.8 = (f32[64,512]{1,0:T(8,128)S(1)}, f32[64,512]{1,0:T(8,128)}, u32[]{:S(2)}) copy-start(f32[64,512]{1,0:T(8,128)} %param.34) | copy-start | bytes 393220
  0.8 150.9 %copy-start.17 = (f32[64,128]{1,0:T(8,128)S(1)}, f32[64,128]{1,0:T(8,128)}, u32[]{:S(2)}) copy-start(f32[64,128]{1,0:T(8,128)} %param.33) | copy-start | bytes 98308
  0.8 152.3 %copy-start.13 = (f32[64,384]{1,0:T(8,128)S(1)}, f32[64,384]{1,0:T(8,128)}, u32[]{:S(2)}) copy-start(f32[64,384]{1,0:T(8,128)} %param.32) | copy-start | bytes 294916
  0.8 154.0 %copy-start.7 = (f32[64,512]{1,0:T(8,128)S(1)}, f32[64,512]{1,0:T(8,128)}, u32[]{:S(2)}) copy-start(f32[64,512]{1,0:T(8,128)} %param.30) | copy-start | bytes 393220
  0.8 150.9 %copy-start.16 = (f32[64,128]{1,0:T(8,128)S(1)}, f32[64,128]{1,0:T(8,128)}, u32[]{:S(2)}) copy-start(f32[64,128]{1,0:T(8,128)} %param.29) | copy-start | bytes 98308
  0.8 152.3 %copy-start.12 = (f32[64,384]{1,0:T(8,128)S(1)}, f32[64,384]{1,0:T(8,128)}, u32[]{:S(2)}) copy-start(f32[64,384]{1,0:T(8,128)} %param.28) | copy-start | bytes 294916
  6.0 150.6 %copy-start.3 = (f32[256,128]{1,0:T(8,128)S(1)}, f32[256,128]{1,0:T(8,128)}, u32[]{:S(2)}) copy-start(f32[256,128]{1,0:T(8,128)} %refs_8_.1) | copy-start | bytes 393220
  6.0 150.6 %copy-start.9 = (f32[256,128]{1,0:T(8,128)S(1)}, f32[256,128]{1,0:T(8,128)}, u32[]{:S(2)}) copy-start(f32[256,128]{1,0:T(8,128)} %param.31) | copy-start | bytes 393220
  6.0 150.6 %copy-start.10 = (f32[256,128]{1,0:T(8,128)S(1)}, f32[256,128]{1,0:T(8,128)}, u32[]{:S(2)}) copy-start(f32[256,128]{1,0:T(8,128)} %param.35) | copy-start | bytes 393220
  148.8 7.9 %copy-start.11 = (f32[256,128]{1,0:T(8,128)S(1)}, f32[256,128]{1,0:T(8,128)}, u32[]{:S(2)}) copy-start(f32[256,128]{1,0:T(8,128)} %get-tuple-element.32) | copy-start | bytes 393220
  148.8 8.7 %copy-start.1 = (bf16[1024,512]{1,0:T(8,128)(2,1)S(1)}, bf16[1024,512]{1,0:T(8,128)(2,1)}, u32[]{:S(2)}) copy-start(bf16[1024,512]{1,0:T(8,128)(2,1)} %get-tuple-element.27) | copy-start | bytes 3145732
  154.8 3.7 %copy-start = (f32[1024,512]{1,0:T(8,128)S(1)}, f32[1024,512]{1,0:T(8,128)}, u32[]{:S(2)}) copy-start(f32[1024,512]{1,0:T(8,128)} %get-tuple-element.28) | copy-start | bytes 6291460

commit v3 on v2

--- a/solution.py
+++ b/solution.py
@@ -161,6 +161,8 @@
         self.over_diagonal = ((1 - self.x) * 2 + 1 - self.core, self.clip)
         self.x_slab = (1 - self.x) * 2 + self.core
         self.core_slab = self.x * 2 + 1 - self.core
+        self.partners = [self.over_core, self.over_x, self.over_y, self.over_diagonal]
+        self.partners += [self.over_z(step) for step in range(1, self.depth)]
 
     def z_at(self, step):
         return lax.rem(self.z + step, self.depth)
@@ -170,11 +172,11 @@
 
     def greet(self):
         barrier = pltpu.get_barrier_semaphore()
-        partners = [self.over_core, self.over_x, self.over_y, self.over_diagonal]
-        partners += [self.over_z(step) for step in range(1, self.depth)]
-        for partner in partners:
+        for partner in self.partners:
             pl.semaphore_signal(barrier, inc=1, device_id=partner, device_id_type=MESH)
-        pl.semaphore_wait(barrier, len(partners))
+
+    def meet(self):
+        pl.semaphore_wait(pltpu.get_barrier_semaphore(), len(self.partners))
 
 
 def wait_all(copies):
@@ -183,149 +185,128 @@
 
 
 class Gather:
-    def __init__(self, place, links, whole, width):
-        self.place, self.links, self.whole, self.width = place, links, whole, width
-
-    def columns(self, slab):
-        return pl.ds(pl.multiple_of(slab * self.width, 128), self.width)
-
-    def move(self, device, *index):
-        block = self.whole.at[index]
+    def __init__(self, place, links, whole, width, rows, columns):
+        self.place, self.links, self.whole = place, links, whole
+        self.width, self.rows, self.columns = width, rows, columns
+
+    def move(self, device, z, y, half, slab):
+        start, size = self.columns(slab)
+        lanes = pl.ds(pl.multiple_of(slab * self.width + start, 128), size)
+        block = self.whole.at[z, y, half, self.rows, lanes]
         return self.links.send(block, block, device)
 
-    def begin(self, master):
+    def first(self):
         place = self.place
-        rows = self.whole.shape[3]
-        for half in range(2):
-            self.whole[place.z, place.y, half, :, self.columns(place.slab)] = master[
-                half * rows : (half + 1) * rows, :
-            ].astype(jnp.bfloat16)
-        self.over_z = [
-            [
-                self.move(
-                    place.over_z(step), place.z, place.y, half, slice(None), self.columns(place.slab)
-                )
-                for step in range(1, place.depth)
-            ]
-            for half in range(2)
+        self.copies = [
+            self.move(place.over_z(step), place.z, place.y, EVERY, place.slab)
+            for step in range(1, place.depth)
         ]
 
     def second(self):
-        place, every = self.place, slice(None)
-        mine = self.columns(place.slab)
-        wait_all(self.over_z[0])
-        self.first_x = self.move(place.over_x, every, place.y, 0, every, mine)
-        wait_all(self.over_z[1])
-        self.first_y = self.move(place.over_y, every, place.y, 1, every, mine)
+        place = self.place
+        wait_all(self.copies)
+        self.first_x = self.move(place.over_x, EVERY, place.y, 0, place.slab)
+        self.first_y = self.move(place.over_y, EVERY, place.y, 1, place.slab)
 
     def third(self):
-        place, every = self.place, slice(None)
-        mine, across = self.columns(place.slab), self.columns(place.x_slab)
+        place = self.place
         self.first_x.wait_recv()
         self.last_y = [
-            self.move(place.over_y, every, place.y, 0, every, mine),
-            self.move(place.over_y, every, place.y, 0, every, across),
+            self.move(place.over_y, EVERY, place.y, 0, slab) for slab in (place.slab, place.x_slab)
         ]
         self.first_y.wait_recv()
-        self.last_x = [self.move(place.over_x, every, every, 1, every, mine)]
+        self.last_x = self.move(place.over_x, EVERY, EVERY, 1, place.slab)
 
     def fourth(self):
-        place, every = self.place, slice(None)
-        mine, across = self.columns(place.slab), self.columns(place.x_slab)
+        place = self.place
         wait_all(self.last_y)
-        self.over_core = [
-            self.move(place.over_core, every, every, 0, every, mine),
-            self.move(place.over_core, every, every, 0, every, across),
+        self.last_x.wait_recv()
+        self.copies = [
+            self.move(place.over_core, EVERY, EVERY, EVERY, slab)
+            for slab in (place.slab, place.x_slab)
         ]
-        wait_all(self.last_x)
-        self.over_core += [
-            self.move(place.over_core, every, every, 1, every, mine),
-            self.move(place.over_core, every, every, 1, every, across),
-        ]
-
-    def end(self):
-        wait_all(self.over_core)
-
-
-def add_into(held, index, arrived, arrived_index):
-    lead = arrived.shape[len(arrived_index) : -2]
-    for at in itertools.product(*[range(n) for n in lead]):
-        total = held[index + at].astype(jnp.float32) + arrived[arrived_index + at].astype(jnp.float32)
-        held[index + at] = total.astype(jnp.bfloat16)
+
+    def last(self):
+        wait_all(self.copies)
 
 
 class Scatter:
-    def __init__(self, place, links, held, from_core, first_y, first_x, last_x, last_y, from_z):
-        self.place, self.links, self.held = place, links, held
-        self.from_core, self.first_y, self.first_x = from_core, first_y, first_x
-        self.last_x, self.last_y, self.from_z = last_x, last_y, from_z
-
-    def begin(self):
+    def __init__(self, place, links, buffers, columns):
+        self.place, self.links, self.columns = place, links, columns
+        self.held, self.from_core, self.first_y, self.first_x = buffers[:4]
+        self.last_x, self.last_y, self.from_z = buffers[4:]
+
+    def lanes(self, slab):
+        start, size = self.columns(slab)
+        return pl.ds(pl.multiple_of(start, 128), size)
+
+    def add(self, index, arrived, slab):
+        lanes = self.lanes(slab)
+        index = (slab, *index, EVERY, lanes)
+        self.held[index] = self.held[index] + arrived[..., lanes]
+
+    def first(self):
         place = self.place
-        self.copies = [
-            self.links.send(
-                self.held.at[2 * x + 1 - place.core], self.from_core.at[x], place.over_core
-            )
-            for x in range(2)
-        ]
+        self.copies = []
+        for x in range(2):
+            slab = 2 * x + 1 - place.core
+            lanes = self.lanes(slab)
+            source = self.held.at[slab, :, :, :, :, lanes]
+            target = self.from_core.at[x, :, :, :, :, lanes]
+            self.copies.append(self.links.send(source, target, place.over_core))
 
     def second(self):
         place = self.place
         for x in range(2):
             self.copies[x].wait_recv()
-            add_into(self.held, (2 * x + place.core,), self.from_core, (x,))
-        self.copies_a = [
-            self.links.send(
-                self.held.at[2 * x + place.core, 1 - place.y, 0], self.first_y.at[x], place.over_y
-            )
-            for x in range(2)
-        ]
-        self.copies_b = [
-            self.links.send(
-                self.held.at[place.x_slab, y, 1], self.first_x.at[y], place.over_x
-            )
-            for y in range(2)
-        ]
+            self.add((EVERY, EVERY, EVERY), self.from_core.at[x], 2 * x + place.core)
+        self.copies = []
+        for x in range(2):
+            slab = 2 * x + place.core
+            lanes = self.lanes(slab)
+            source = self.held.at[slab, 1 - place.y, 0, :, :, lanes]
+            target = self.first_y.at[x, :, :, lanes]
+            self.copies.append(self.links.send(source, target, place.over_y))
+        lanes = self.lanes(place.x_slab)
+        source = self.held.at[place.x_slab, :, 1, :, :, lanes]
+        target = self.first_x.at[:, :, :, lanes]
+        self.copy = self.links.send(source, target, place.over_x)
 
     def third(self):
         place = self.place
         for x in range(2):
-            self.copies_a[x].wait_recv()
-            add_into(self.held, (2 * x + place.core, place.y, 0), self.first_y, (x,))
-        self.copy_a = self.links.send(
-            self.held.at[place.x_slab, place.y, 0], self.last_x, place.over_x
-        )
-        for y in range(2):
-            self.copies_b[y].wait_recv()
-            add_into(self.held, (place.slab, y, 1), self.first_x, (y,))
-        self.copy_b = self.links.send(
-            self.held.at[place.slab, 1 - place.y, 1], self.last_y, place.over_y
-        )
+            self.copies[x].wait_recv()
+            self.add((place.y, 0, EVERY), self.first_y.at[x], 2 * x + place.core)
+        lanes = self.lanes(place.x_slab)
+        source = self.held.at[place.x_slab, place.y, 0, :, :, lanes]
+        copy_x = self.links.send(source, self.last_x.at[:, :, lanes], place.over_x)
+        self.copy.wait_recv()
+        self.add((EVERY, 1, EVERY), self.first_x, place.slab)
+        lanes = self.lanes(place.slab)
+        source = self.held.at[place.slab, 1 - place.y, 1, :, :, lanes]
+        copy_y = self.links.send(source, self.last_y.at[:, :, lanes], place.over_y)
+        self.copies = [copy_x, copy_y]
 
     def fourth(self):
         place = self.place
+        lanes = self.lanes(place.slab)
+        for half, arrived in enumerate((self.last_x, self.last_y)):
+            self.copies[half].wait_recv()
+            self.add((place.y, half, EVERY), arrived, place.slab)
         self.copies = []
-        for half, copy, arrived in ((0, self.copy_a, self.last_x), (1, self.copy_b, self.last_y)):
-            copy.wait_recv()
-            add_into(self.held, (place.slab, place.y, half), arrived, ())
-            self.copies.append([
-                self.links.send(
-                    self.held.at[place.slab, place.y, half, place.z_at(step)],
-                    self.from_z.at[half, step - 1],
-                    place.over_z(step),
-                )
-                for step in range(1, place.depth)
-            ])
-
-    def end(self):
-        place, parts = self.place, []
-        for half in range(2):
-            total = self.held[place.slab, place.y, half, place.z].astype(jnp.float32)
-            for step in range(1, place.depth):
-                self.copies[half][step - 1].wait_recv()
-                total += self.from_z[half, step - 1].astype(jnp.float32)
-            parts.append(total)
-        return parts
+        for step in range(1, place.depth):
+            source = self.held.at[place.slab, place.y, :, place.z_at(step), :, lanes]
+            target = self.from_z.at[step - 1, :, :, lanes]
+            self.copies.append(self.links.send(source, target, place.over_z(step)))
+
+    def last(self):
+        place = self.place
+        lanes = self.lanes(place.slab)
+        total = self.held[place.slab, place.y, :, place.z, :, lanes].astype(jnp.float32)
+        for step in range(1, place.depth):
+            self.copies[step - 1].wait_recv()
+            total += self.from_z[step - 1, :, :, lanes].astype(jnp.float32)
+        return total, lanes
 
 
 class Small:
@@ -333,7 +314,7 @@
         self.place, self.links, self.held = place, links, held
         self.arrived, self.line = arrived, line
 
-    def begin(self):
+    def first(self):
         self.copy = self.links.send(self.held.at[0], self.arrived.at[0], self.place.over_core)
 
     def second(self):
@@ -355,12 +336,49 @@
             for step in range(1, place.depth)
         ]
 
-    def end(self):
+    def last(self):
         wait_all(self.copies)
         total = self.line[0]
         for z in range(1, self.place.depth):
             total += self.line[z]
         return total
+
+
+class Queue:
+    def __init__(self, steps):
+        self.steps = list(steps)
+
+    def take(self, count=1):
+        for _ in range(min(count, len(self.steps))):
+            for stage in self.steps.pop(0):
+                stage()
+
+    def until(self, stage):
+        while any(stage in step for step in self.steps):
+            self.take()
+
+
+def staggered(flows, ahead, lag):
+    steps = []
+    for k in range(len(flows) + lag):
+        step = [flows[k].third] if k < len(flows) else []
+        step += [flows[k + ahead].second] if k + ahead < len(flows) else []
+        step += [flows[k - lag].fourth] if 0 <= k - lag < len(flows) else []
+        steps.append(step)
+    return steps
+
+
+EVERY = slice(None)
+
+
+def cut(total, count):
+    size = total // count
+    return [lambda slab, k=k: (k * size, size) for k in range(count)]
+
+
+def turned(total, count):
+    size = total // count
+    return [lambda slab, k=k: (lax.rem(slab + k, count) * size, size) for k in range(count)]
 
 
 def scatter_buffers(shape):
@@ -371,7 +389,7 @@
         pltpu.VMEM((2, depth, rows, columns), jnp.bfloat16),
         pltpu.VMEM((depth, rows, columns), jnp.bfloat16),
         pltpu.VMEM((depth, rows, columns), jnp.bfloat16),
-        pltpu.VMEM((2, depth - 1, rows, columns), jnp.bfloat16),
+        pltpu.VMEM((depth - 1, 2, rows, columns), jnp.bfloat16),
     ]
 
 
@@ -487,8 +505,13 @@
     s = Held(*rest[: len(Held._fields)])
     rest = rest[len(Held._fields) :]
     small = Small(place, links, rest.pop(0), rest.pop(0), rest.pop(0))
-    flows = [Scatter(place, links, *[rest.pop(0) for _ in range(7)]) for _ in masters]
-    qkv_flow, proj_flow, up_flow, down_flow = flows
+    qkv_parts, proj_parts, up_parts, down_parts = [
+        [rest.pop(0) for _ in range(7)] for _ in masters
+    ]
+    qkv_flows = [Scatter(place, links, qkv_parts, c) for c in turned(masters[0].shape[1], 3)]
+    proj_flow = Scatter(place, links, proj_parts, cut(masters[1].shape[1], 1)[0])
+    up_flows = [Scatter(place, links, up_parts, c) for c in cut(masters[2].shape[1], 2)]
+    down_flows = [Scatter(place, links, down_parts, c) for c in cut(masters[3].shape[0], 2)]
     xb, eb, own, bias = s.xb, s.eb, s.own, s.bias
     tok, width = xb.shape
     unit = SHORT // slabs * BINS
@@ -510,14 +533,42 @@
     for load in loads:
         load.start()
     place.greet()
-    gathers = [
-        Gather(place, links, whole, master.shape[1])
-        for whole, master in zip(
-            (s.whole_qkv, s.whole_proj, s.whole_up, s.whole_down), masters
-        )
-    ]
-    qkv_copy, proj_copy, up_copy, down_copy = gathers
-    qkv_copy.begin(masters[0])
+    wholes = (s.whole_qkv, s.whole_proj, s.whole_up, s.whole_down)
+    for whole, master in zip(wholes, masters):
+        rows, width_own = whole.shape[3], master.shape[1]
+        lanes = pl.ds(pl.multiple_of(place.slab * width_own, 128), width_own)
+        for h in range(2):
+            block = master[h * rows : (h + 1) * rows, :].astype(jnp.bfloat16)
+            whole[place.z, place.y, h, :, lanes] = block
+
+    def gathers(index, ranges, rows=(EVERY,)):
+        return [
+            Gather(place, links, wholes[index], masters[index].shape[1], r, c)
+            for r in rows
+            for c in ranges
+        ]
+
+    qkv_copies = gathers(0, turned(masters[0].shape[1], 3))
+    proj_copies = gathers(1, cut(masters[1].shape[1], 1))
+    up_copies = gathers(2, cut(masters[2].shape[1], 4))
+    quarter = s.whole_down.shape[3] // 4
+    down_copies = gathers(
+        3, cut(masters[3].shape[1], 1), [pl.ds(k * quarter, quarter) for k in range(4)]
+    )
+    later = proj_copies + up_copies
+    later = proj_copies + up_copies + down_copies
+    queue = Queue(
+        [
+            [flow.first for flow in qkv_copies],
+            [flow.second for flow in qkv_copies] + [flow.first for flow in later[:3]],
+            [flow.third for flow in qkv_copies] + [flow.first for flow in later[3:]],
+            [flow.second for flow in later[:3]],
+            [flow.fourth for flow in qkv_copies],
+        ]
+        + staggered(later, 3, 2)
+    )
+    place.meet()
+    queue.until(qkv_copies[-1].first)
 
     heads = [units[HEADS_AT, i] for i in range(slots)]
     tails = [units[TAILS_AT, i] for i in range(slots)]
@@ -563,9 +614,7 @@
         put_rows(s.attn_in, i, low)
         s.attn_in_t[:, span(i, chunk)] = low.T
 
-    qkv_copy.second()
-    proj_copy.begin(masters[1])
-    up_copy.begin(masters[2])
+    queue.until(qkv_copies[-1].second)
 
     loads[1].wait()
 
@@ -577,12 +626,9 @@
         eb[span(i, chunk), :] = low
         s.et[:, span(i, chunk)] = low.T
 
-    qkv_copy.third()
-    down_copy.begin(masters[3])
-    proj_copy.second()
-    qkv_copy.fourth()
-    qkv_copy.end()
-    up_copy.second()
+    queue.until(qkv_copies[-1].fourth)
+    for flow in qkv_copies:
+        flow.last()
     whole_qkv, whole_proj = s.whole_qkv, s.whole_proj
     whole_up, whole_down = s.whole_up, s.whole_down
 
@@ -596,11 +642,14 @@
     before = (lax.rem(place.slab + slabs - 1, slabs), place.clip)
     after = (lax.rem(place.slab + 1, slabs), place.clip)
     lend = links.send(s.lent, s.borrowed, before)
+    queue.take()
 
     @pl.loop(0, tok // chunk)
     def _(i):
         rows = mm(rows_of(s.attn_in, i, chunk), flat(whole_qkv)) + qkv_bias
         put_rows(own, i, rows.astype(jnp.bfloat16))
+
+    queue.take()
 
     groups_unit = unit // group
 
@@ -610,52 +659,58 @@
             return blocks(ref, begin, 2)
         return jnp.concatenate([ref[begin], ref[units[SECOND_AT, u]]], 0)
 
-    def forward(u, j):
-        rows = window(own, u, j)
-        wrap = units[WRAP_AT, u] if j == groups_unit - 1 else 0
-        offsets = bias[wrap]
-        place_at = span(u * groups_unit + j, group)
-        for t in range(tiles):
-            cols = slice(128 * t, 128 * (t + 1))
-            queries = stacked(rows[:, cols])
-            keys = rows[:, width + 128 * t : width + 128 * (t + 1)]
-            values = rows[:, 2 * width + 128 * t : 2 * width + 128 * (t + 1)]
-            scores = mm_nt(keys, queries) * score_scale + offsets[:, cols]
-            weights = jnp.exp(scores - jnp.max(scores, 0, keepdims=True))
-            weights = weights / jnp.sum(weights, 0, keepdims=True)
-            s.probs[place_at, cols] = weights
-            mixed = folded(mm_tn(weights.astype(jnp.bfloat16), values))
-            mixed = mixed.astype(jnp.bfloat16).reshape(2, half, 128)
-            s.att_win[span(u * groups_unit + j, 2), :, cols] = mixed
+    def parts(rows):
+        return [
+            [rows[:, k * width + 128 * t : k * width + 128 * (t + 1)] for t in range(tiles)]
+            for k in range(rows.shape[1] // width)
+        ]
+
+    def forward(works):
+        rows = [parts(window(own, u, j)) for u, j in works]
+        wraps = [units[WRAP_AT, u] if j == groups_unit - 1 else 0 for u, j in works]
+        scores = [
+            jnp.concatenate([mm_nt(k, stacked(q)) for q, k in zip(queries, keys)], 1)
+            for queries, keys, _ in rows
+        ]
+        scores = [score * score_scale + bias[wrap] for score, wrap in zip(scores, wraps)]
+        weights = [jnp.exp(score - jnp.max(score, 0, keepdims=True)) for score in scores]
+        weights = [weight * (1.0 / jnp.sum(weight, 0, keepdims=True)) for weight in weights]
+        lows = [weight.astype(jnp.bfloat16) for weight in weights]
+        for (u, j), weight in zip(works, weights):
+            s.probs[span(u * groups_unit + j, group), :] = weight
+        mixed = [
+            [mm_tn(low[:, 128 * t : 128 * (t + 1)], v) for t, v in enumerate(values)]
+            for low, (_, _, values) in zip(lows, rows)
+        ]
+        for (u, j), products in zip(works, mixed):
+            out = jnp.concatenate([folded(product) for product in products], 1)
+            out = out.astype(jnp.bfloat16).reshape(2, half, width)
+            s.att_win[span(u * groups_unit + j, 2)] = out
 
     def sweep(step, exchange, give_back, first, second, third):
         @pl.loop(0, unit_count // 2)
         def _(u):
-            for j in range(groups_unit - 1):
-                step(u, j)
+            step([(u, j) for j in range(groups_unit - 1)])
 
         first()
         exchange()
 
         @pl.loop(0, unit_count // 2)
         def _(u):
-            step(2 * u, groups_unit - 1)
-            step(2 * u + 1, groups_unit - 1)
+            step([(2 * u, groups_unit - 1), (2 * u + 1, groups_unit - 1)])
 
         handle = give_back()
         second()
 
         @pl.loop(unit_count // 2, 3 * unit_count // 4)
         def _(u):
-            for j in range(groups_unit - 1):
-                step(u, j)
+            step([(u, j) for j in range(groups_unit - 1)])
 
         third()
 
         @pl.loop(3 * unit_count // 4, unit_count)
         def _(u):
-            for j in range(groups_unit - 1):
-                step(u, j)
+            step([(u, j) for j in range(groups_unit - 1)])
 
         handle()
 
@@ -684,29 +739,22 @@
 
         return take
 
-    def first():
-        proj_copy.third()
-        up_copy.third()
-
-    def second():
-        down_copy.second()
-        proj_copy.fourth()
-
-    def third():
-        up_copy.fourth()
-        down_copy.third()
+    def taking(source, count):
+        return lambda: source.take(count)
 
     sweep(
         forward,
         take_lent(lend, s.borrowed, own),
         give_back_from(s.att_win, s.att_out, s.att_back),
-        first,
-        second,
-        third,
+        taking(queue, 1),
+        taking(queue, 1),
+        taking(queue, 1),
     )
     from_windows(s.att_win, s.att_rows, s.att_t)
 
-    proj_copy.end()
+    queue.take()
+    for flow in proj_copies:
+        flow.last()
     mid, mlp_in = s.mid, s.mlp_in
 
     @pl.loop(0, tok // chunk)
@@ -719,36 +767,29 @@
         mlp_in[span(i, chunk), :] = low
         s.mlp_in_t[:, span(i, chunk)] = low.T
 
-    up_copy.end()
-    down_copy.fourth()
     act, slope = s.act, s.slope
     wide = act.shape[1] // width
-
-    @pl.loop(0, wide)
-    def _(c):
-        cols = span(c, width)
+    for k, flow in enumerate(up_copies):
+        queue.until(flow.fourth)
+        flow.last()
+        size = width // len(up_copies)
+        lanes = [slice(c * width + k * size, c * width + (k + 1) * size) for c in range(wide)]
+        piece = slice(k * size, (k + 1) * size)
+        shift = jnp.concatenate([vectors[8 + c : 9 + c, piece] for c in range(wide)], 1)
 
         @pl.loop(0, tok // chunk)
         def _(i):
-            pre = mm(mlp_in[span(i, chunk), :], flat(whole_up, cols))
-            value, derivative = gelu_parts(pre + vectors[pl.ds(8 + c, 1), :])
-            act[span(i, chunk), cols] = value.astype(jnp.bfloat16)
-            slope[span(i, chunk), cols] = derivative.astype(jnp.bfloat16)
-
-    out_low = s.out_low
-    down_copy.end()
-
-    @pl.loop(0, tok // chunk)
-    def _(i):
-        rows = mid[span(i, chunk), :] + mm(act[span(i, chunk), :], flat(whole_down))
-        live = lax.broadcasted_iota(jnp.int32, (chunk, width), 0) + i * chunk < used
-        rows = jnp.where(live, rows + vectors[7:8, :], 0.0)
-        out_low[span(i, chunk), :] = rows.astype(jnp.bfloat16)
-
-    store_out = pltpu.make_async_copy(out_low, block_out, s.load_sems.at[0])
-    store_out.start()
-
-    down = down_flow.held
+            weights = jnp.concatenate([flat(whole_up, at) for at in lanes], 1)
+            pre = mm(mlp_in[span(i, chunk), :], weights)
+            value, derivative = gelu_parts(pre + shift)
+            value, derivative = value.astype(jnp.bfloat16), derivative.astype(jnp.bfloat16)
+            for c, at in enumerate(lanes):
+                act[span(i, chunk), at] = value[:, c * size : (c + 1) * size]
+                slope[span(i, chunk), at] = derivative[:, c * size : (c + 1) * size]
+
+        queue.take()
+
+    down = down_parts[0]
 
     @pl.loop(0, clips)
     def _(c):
@@ -758,12 +799,16 @@
         for h in range(2):
             down[:, c % 2, h, c // 2] = part[:, h]
 
-    down_flow.begin()
-
-    @pl.loop(0, wide)
-    def _(c):
+    for flow in down_flows:
+        flow.first()
+
+    queue.until(down_copies[-1].fourth)
+    for flow in down_copies:
+        flow.last()
+
+    def pre_back(c):
         cols = span(c, width)
-        weights = whole_down.reshape(wide, width, width)[c]
+        weights = whole_down[c].reshape(width, width)
 
         def step(i, sums):
             grad = mm_nt(eb[span(i, chunk), :], weights)
@@ -773,9 +818,16 @@
             return sums + jnp.sum(low.astype(jnp.float32), 0, keepdims=True)
 
         sums = lax.fori_loop(0, tok // chunk, step, jnp.zeros((1, width), jnp.float32))
-        s.up_sum[pl.ds(c, 1), :] = sums
-
-    up = up_flow.held
+        s.up_sum[c : c + 1, :] = sums
+
+    for c in range(wide):
+        pre_back(c)
+        if c == 1:
+            down_flows[0].second()
+        if c == 2:
+            down_flows[1].second()
+
+    up = up_parts[0]
 
     def keep(target, slab, part):
         part = (part * grad_scale).astype(jnp.bfloat16)
@@ -788,8 +840,10 @@
     def _(i):
         keep(up, i, mm(s.mlp_in_t[...], slope[:, span(i, act.shape[1] // slabs)]))
 
-    up_flow.begin()
-    down_flow.second()
+    for flow in up_flows:
+        flow.first()
+    down_flows[0].third()
+    down_flows[1].third()
 
     mid_grad, mid_low = s.mid_grad, s.mid_low
 
@@ -811,7 +865,9 @@
     for row, value in zip((4, 5, 6, 7), mid_sums):
         small.held[0, row : row + 1, :] = value * grad_scale
     small.held[0, 8:12, :] = s.up_sum[...] * grad_scale
-    up_flow.second()
+    up_flows[0].second()
+    up_flows[1].second()
+    down_flows[0].fourth()
 
     proj_columns = flat(whole_proj)
     head_low = jnp.concatenate(
@@ -829,45 +885,69 @@
     grad = mm(s.att_t[...], mid_low[...].reshape(tok, width))
     for i in range(slabs):
         keep(proj_flow.held, i, grad[:, i * (width // slabs) : (i + 1) * (width // slabs)])
-    proj_flow.begin()
-    down_flow.third()
+    proj_flow.first()
+    down_flows[1].fourth()
+    up_flows[0].third()
 
     bias_grad, qg_win = s.bias_grad, s.qg_win
     bias_grad[...] = jnp.zeros_like(bias_grad)
 
-    def backward(u, j):
-        rows = window(own, u, j)
-        grads = window(dwin_own, u, j)
-        place_at = span(u * groups_unit + j, group)
-        for t in range(tiles):
-            cols = slice(128 * t, 128 * (t + 1))
-            queries = stacked(rows[:, cols])
-            keys = rows[:, width + 128 * t : width + 128 * (t + 1)]
-            values = rows[:, 2 * width + 128 * t : 2 * width + 128 * (t + 1)]
-            mixed = stacked(grads[:, cols])
-            weights = s.probs[place_at, cols]
-            prob_grad = mm_nt(values, mixed)
-            value_grad = mm(weights.astype(jnp.bfloat16), mixed)
-            inner = jnp.sum(weights * prob_grad, 0, keepdims=True)
-            score = (weights * (prob_grad - inner)).astype(jnp.bfloat16)
-            bias_grad[:, cols] += score.astype(jnp.float32)
-            key_grad = mm(score, queries) * score_scale
-            query_grad = folded(mm_tn(score, keys)) * score_scale
-            for k, value in enumerate((query_grad, key_grad, value_grad)):
-                at = slice(k * width + 128 * t, k * width + 128 * (t + 1))
-                value = value.astype(jnp.bfloat16).reshape(2, half, 128)
-                qg_win[span(u * groups_unit + j, 2), :, at] = value
-
-    def second_back():
+    def backward(works):
+        rows = [parts(window(own, u, j)) for u, j in works]
+        places = [span(u * groups_unit + j, group) for u, j in works]
+        mixed = [[stacked(g) for g in parts(window(dwin_own, u, j))[0]] for u, j in works]
+        weights = [s.probs[at, :] for at in places]
+        lows = [weight.astype(jnp.bfloat16) for weight in weights]
+        prob_grads = [
+            jnp.concatenate([mm_nt(v, g) for v, g in zip(values, grads)], 1)
+            for (_, _, values), grads in zip(rows, mixed)
+        ]
+        value_grads = [
+            [mm(low[:, 128 * t : 128 * (t + 1)], g) for t, g in enumerate(grads)]
+            for low, grads in zip(lows, mixed)
+        ]
+        scores = [
+            (weight * (grad - jnp.sum(weight * grad, 0, keepdims=True))).astype(jnp.bfloat16)
+            for weight, grad in zip(weights, prob_grads)
+        ]
+        bias_grad[...] += sum(score.astype(jnp.float32) for score in scores)
+        key_grads = [
+            [
+                mm(score[:, 128 * t : 128 * (t + 1)], stacked(q)) * score_scale
+                for t, q in enumerate(queries)
+            ]
+            for score, (queries, _, _) in zip(scores, rows)
+        ]
+        query_grads = [
+            [
+                folded(mm_tn(score[:, 128 * t : 128 * (t + 1)], k)) * score_scale
+                for t, k in enumerate(keys)
+            ]
+            for score, (_, keys, _) in zip(scores, rows)
+        ]
+        for (u, j), *grads in zip(works, query_grads, key_grads, value_grads):
+            out = jnp.concatenate([tile for grad in grads for tile in grad], 1)
+            out = out.astype(jnp.bfloat16).reshape(2, half, 3 * width)
+            qg_win[span(u * groups_unit + j, 2)] = out
+
+    def after_first():
+        up_flows[1].third()
         proj_flow.second()
+
+    def after_second():
+        up_flows[0].fourth()
+
+    def after_third():
+        up_flows[1].fourth()
+        proj_flow.third()
 
     sweep(
         backward,
         take_lent(lend_back, s.dborrowed, dwin_own),
         give_back_from(qg_win, s.qg_out, s.qg_back),
-        up_flow.third,
-        second_back,
-        down_flow.fourth,
+        after_first,
+        after_second,
+        after_third,
     )
     qg_rows = s.qg_rows
     from_windows(qg_win, qg_rows)
@@ -877,18 +957,18 @@
         size = 3 * width // slabs
         grad = mm(s.attn_in_t[...], qg_rows[:, i * pair * size : (i + 1) * pair * size])
         for k in range(pair):
-            keep(qkv_flow.held, i * pair + k, grad[:, k * size : (k + 1) * size])
-    qkv_flow.begin()
-    proj_flow.third()
-    up_flow.fourth()
+            keep(qkv_parts[0], i * pair + k, grad[:, k * size : (k + 1) * size])
+    for flow in qkv_flows:
+        flow.first()
+    proj_flow.fourth()
+
 
     def in_step(i, sums):
         rows = qg_rows[span(i, chunk), :]
         grad = mm_nt(rows, flat(whole_qkv))
         normed, inverse = norm_parts(xb[span(i, chunk), :].astype(jnp.float32))
-        mid[span(i, chunk), :] = mid_grad[span(i, chunk), :] + norm_back(
-            normed, inverse, grad * vectors[0:1, :]
-        )
+        back = norm_back(normed, inverse, grad * vectors[0:1, :])
+        mid_grad[span(i, chunk), :] = mid_grad[span(i, chunk), :] + back
         query_part = rows[:, :width].astype(jnp.float32)
         value_part = rows[:, 2 * width :].astype(jnp.float32)
         return tuple(
@@ -897,7 +977,7 @@
         )
 
     in_sums = lax.fori_loop(0, tok // chunk, in_step, (zero,) * 4)
-    store_grad = pltpu.make_async_copy(mid, x_grad, s.load_sems.at[1])
+    store_grad = pltpu.make_async_copy(mid_grad, x_grad, s.load_sems.at[1])
     store_grad.start()
     for row, value in zip((0, 1, 2, 3), in_sums):
         small.held[0, row : row + 1, :] = value * grad_scale
@@ -913,23 +993,45 @@
     for i in range(width // 128):
         small.held[0, 12:16, 128 * i : 128 * (i + 1)] = sums[4 * i : 4 * i + 4, :]
 
-    qkv_flow.second()
-    small.begin()
-    proj_flow.fourth()
+    small.first()
+    for flow in qkv_flows:
+        flow.second()
     small.second()
-    qkv_flow.third()
+
+    out_low = s.out_low
+
+    @pl.loop(0, tok // chunk)
+    def _(i):
+        rows = mid[span(i, chunk), :] + mm(act[span(i, chunk), :], flat(whole_down))
+        live = lax.broadcasted_iota(jnp.int32, (chunk, width), 0) + i * chunk < used
+        rows = jnp.where(live, rows + vectors[7:8, :], 0.0)
+        out_low[span(i, chunk), :] = rows.astype(jnp.bfloat16)
+
+    store_out = pltpu.make_async_copy(out_low, block_out, s.load_sems.at[0])
+    store_out.start()
+
+    for flow in qkv_flows:
+        flow.third()
     small.third()
-    qkv_flow.fourth()
+
+    def finish(flows, out, turn):
+        for flow in flows:
+            total, lanes = flow.last()
+            rows = total.shape[1]
+            if turn:
+                out[lanes, :] = total.reshape(2 * rows, -1).T
+            else:
+                out[:rows, lanes] = total[0]
+                out[rows:, lanes] = total[1]
+
+    finish(down_flows, owned[3], True)
+    finish(up_flows, owned[2], False)
+    finish([proj_flow], owned[1], False)
+    for flow in qkv_flows:
+        flow.fourth()
     small.fourth()
-    for flow, out in zip(flows, owned):
-        first, last = flow.end()
-        if flow is down_flow:
-            out[...] = jnp.concatenate([first, last], 0).T
-        else:
-            rows = first.shape[0]
-            out[:rows, :] = first
-            out[rows:, :] = last
-    small_out[...] = small.end()
+    finish(qkv_flows, owned[0], False)
+    small_out[...] = small.last()
     store_out.wait()
     store_grad.wait()
     links.drain()
@@ -1008,7 +1110,7 @@
         whole_qkv=whole(masters[0]), whole_proj=whole(masters[1]),
         whole_up=whole(masters[2]), whole_down=whole(masters[3]),
     )
-    copies = 4 * (2 * (depth - 1) + 9) + 4 * (2 + 4 + 2 + 2 * (depth - 1)) + 3 + depth - 1 + 4
+    copies = 12 * (depth - 1 + 7) + 8 * (7 + depth - 1) + 3 + depth - 1 + 4
     scratch = [pltpu.SemaphoreType.DMA((copies,)), pltpu.SemaphoreType.DMA((copies,)), *held]
     small = (16, width)
     scratch += [

time: 160 us -> 125 us (0.78)
  Pallas kernels: 143 us -> 108 us
    pallas_call x1, Pallas kernels: 143 us -> 108 us  [block_call(): pl.pallas_call(functools.partial(block_kernel, slab_size, clip_size), out...]
where the time goes in v3:
time: 125 us
  Pallas kernels  108 us (86%)
  other arithmetic  9.58 us (8%)
  local copies, waits for them, and re-layouts  5.82 us (5%)
  between operations  1.57 us (1%)
    pallas_call x1, Pallas kernels, block_call(): pl.pallas_call(functools.partial(block_kernel, slab_size, clip_size), out...  108 us
    sub x6, other arithmetic, adamw(): return (weight - rate * (update + decay * weight), first, second)  7.72 us
    unnamed x45, local copies, waits for them, and re-layouts  3.78 us

profile of v3, /device:TPU:0, one launch (start us, length us, event | category | flops | bytes accessed | tf_op | source)
XLA Modules:
  0.0 124.6 jit_solution(13484898413047256601)
XLA Ops:
  0.7 0.0 copy-start.18
  0.7 0.0 copy-start.5
  0.7 0.0 copy-start.2
  0.7 0.0 copy-start.6
  0.7 0.0 copy-start.4
  0.7 0.0 copy-start.20
  0.7 0.0 copy-start.19
  0.7 0.0 copy-start.15
  0.8 0.0 copy-start.14
  0.8 0.0 copy-start.8
  0.8 0.0 copy-start.17
  0.8 0.0 copy-start.13
  0.8 0.0 copy-start.7
  0.8 0.0 copy-start.16
  0.8 0.0 copy-start.12
  0.8 0.9 and_select_fusion.2
  1.7 0.2 broadcast_in_dim.40
  1.9 0.6 slice.13
  3.2 0.7 minimum_multiply_fusion
  3.8 0.1 select_reduce_fusion
  4.0 0.6 stack.16.refs_2_
  4.6 1.4 %copy.43.refs_4_ = f32[49,16]{1,0:T(8,128)} copy(f32[49,16]{0,1:T(8,128)} %param.39) | data formatting | bytes 6272 | tf_op args[18]
  6.0 0.0 copy-start.3
  6.0 0.0 copy-start.9
  6.0 0.0 copy-start.10
  6.0 107.7 %block.1 = (bf16[1024,512]{1,0:T(8,128)(2,1)}, f32[1024,512]{1,0:T(8,128)}, f32[16,512]{1,0:T(8,128)}, f32[64,384]{1,0:T(8,128)}, f32[64,128]{1,0:T(8,128)}, /*index=5*/f32[64,512]{1,0:T(8,128)}, f32[256,128]{1,0:T(8,128)}) custom-call(bf16[1024,512]{1,0:T(8,128)(2,1)} %bitcast.65, bf16[1024,512]{1,0:T(8,128)(2,1)} %bitcast.66, s32[8,8]{1,0:T(8,128)} %stack.16.refs_2_, ...), custom_call_target="tpu_custom_call" | custom-call | tf_op jit(solution)/shard_map/block/pallas_call | solution.py:1121
  113.7 0.0 copy-start.11
  113.7 0.0 copy-start.1
  113.7 0.8 slice.15
  114.5 0.0 copy-done.18
  114.5 0.0 copy-done.20
  114.5 0.0 copy-done.19
  114.5 0.6 multiply_subtract_fusion.5
  115.2 0.0 copy-done.5
  115.2 0.0 copy-done.15
  115.2 0.0 copy-done.14
  115.2 1.4 %multiply_subtract_fusion.3 = (f32[12,512]{1,0:T(8,128)}, f32[12,512]{1,0:T(8,128)}, f32[12,512]{1,0:T(8,128)}) fusion(f32[12,512]{1,0:T(8,128)S(1)} %copy-done.5, f32[16,512]{1,0:T(8,128)} %get-tuple-element.33, f32[12,512]{1,0:T(8,128)S(1)} %copy-done.14, f32[12,512]{1,0:T(8,128)S(1)} %copy-done.15), kind=kLoop, calls=%fused_computation.18 | loop fusion | flops 86016 | bytes 172032 | tf_op jit(solution)/shard_map/sub | solution.py:122
  116.6 0.0 copy-done.6
  116.6 0.0 copy-done.17
  116.6 0.0 copy-done.16
  116.6 1.4 %multiply_subtract_fusion.4 = (f32[64,128]{1,0:T(8,128)}, f32[64,128]{1,0:T(8,128)}, f32[64,128]{1,0:T(8,128)}) fusion(f32[64,128]{1,0:T(8,128)S(1)} %copy-done.6, f32[64,128]{1,0:T(8,128)} %get-tuple-element.30, f32[64,128]{1,0:T(8,128)S(1)} %copy-done.16, f32[64,128]{1,0:T(8,128)S(1)} %copy-done.17), kind=kLoop, calls=%fused_computation.19 | loop fusion | flops 114688 | bytes 229376 | tf_op jit(solution)/shard_map/sub | solution.py:122
  118.0 0.0 copy-done.4
  118.0 0.0 copy-done.13
  118.0 0.0 copy-done.12
  118.0 1.6 %multiply_subtract_fusion.2 = (f32[64,384]{1,0:T(8,128)}, f32[64,384]{1,0:T(8,128)}, f32[64,384]{1,0:T(8,128)}) fusion(f32[64,384]{1,0:T(8,128)S(1)} %copy-done.4, f32[64,384]{1,0:T(8,128)} %get-tuple-element.29, f32[64,384]{1,0:T(8,128)S(1)} %copy-done.12, f32[64,384]{1,0:T(8,128)S(1)} %copy-done.13), kind=kLoop, calls=%fused_computation.11 | loop fusion | flops 344064 | bytes 688128 | tf_op jit(solution)/shard_map/sub | solution.py:122
  119.6 0.0 copy-start
  119.7 0.0 copy-done.2
  119.7 0.0 copy-done.8
  119.7 0.0 copy-done.7
  119.7 1.8 %multiply_subtract_fusion.1 = (f32[64,512]{1,0:T(8,128)}, f32[64,512]{1,0:T(8,128)}, f32[64,512]{1,0:T(8,128)}) fusion(f32[64,512]{1,0:T(8,128)S(1)} %copy-done.2, f32[64,512]{1,0:T(8,128)} %get-tuple-element.31, f32[64,512]{1,0:T(8,128)S(1)} %copy-done.7, f32[64,512]{1,0:T(8,128)S(1)} %copy-done.8), kind=kLoop, calls=%fused_computation.9 | loop fusion | flops 458752 | bytes 917504 | tf_op jit(solution)/shard_map/sub | solution.py:122
  121.5 0.0 copy-done.3
  121.5 0.0 copy-done.9
  121.5 0.0 copy-done.10
  121.5 0.0 copy-done.11
  121.5 0.8 multiply_subtract_fusion
  122.3 0.0 copy-done.1
  122.3 1.0 copy.47
  123.3 0.0 copy-done
  123.3 1.3 %copy.48 = f32[1,1,1024,512]{3,2,1,0:T(8,128)} copy(f32[1,1,1024,512]{3,2,1,0:T(8,128)S(1)} %bitcast.64) | data formatting | bytes 4194304
  (8 shorter events, 0.1 us)
Async XLA Ops:
  0.7 113.9 %copy-start.18 = (f32[49,16]{0,1:T(8,128)S(1)}, f32[49,16]{0,1:T(8,128)}, u32[]{:S(2)}) copy-start(f32[49,16]{0,1:T(8,128)} %param.39) | copy-start | bytes 9412
  0.7 114.5 %copy-start.5 = (f32[12,512]{1,0:T(8,128)S(1)}, f32[12,512]{1,0:T(8,128)}, u32[]{:S(2)}) copy-start(f32[12,512]{1,0:T(8,128)} %refs_3_.1) | copy-start | bytes 73732
  0.7 119.0 %copy-start.2 = (f32[64,512]{1,0:T(8,128)S(1)}, f32[64,512]{1,0:T(8,128)}, u32[]{:S(2)}) copy-start(f32[64,512]{1,0:T(8,128)} %refs_7_.1) | copy-start | bytes 393220
  0.7 115.9 %copy-start.6 = (f32[64,128]{1,0:T(8,128)S(1)}, f32[64,128]{1,0:T(8,128)}, u32[]{:S(2)}) copy-start(f32[64,128]{1,0:T(8,128)} %refs_6_.1) | copy-start | bytes 98308
  0.7 117.3 %copy-start.4 = (f32[64,384]{1,0:T(8,128)S(1)}, f32[64,384]{1,0:T(8,128)}, u32[]{:S(2)}) copy-start(f32[64,384]{1,0:T(8,128)} %refs_5_.1) | copy-start | bytes 294916
  0.7 113.8 %copy-start.20 = (f32[49,16]{0,1:T(8,128)S(1)}, f32[49,16]{0,1:T(8,128)}, u32[]{:S(2)}) copy-start(f32[49,16]{0,1:T(8,128)} %param.41) | copy-start | bytes 9412
  0.7 113.8 %copy-start.19 = (f32[49,16]{0,1:T(8,128)S(1)}, f32[49,16]{0,1:T(8,128)}, u32[]{:S(2)}) copy-start(f32[49,16]{0,1:T(8,128)} %param.40) | copy-start | bytes 9412
  0.7 114.4 %copy-start.15 = (f32[12,512]{1,0:T(8,128)S(1)}, f32[12,512]{1,0:T(8,128)}, u32[]{:S(2)}) copy-start(f32[12,512]{1,0:T(8,128)} %param.38) | copy-start | bytes 73732
  0.8 114.4 %copy-start.14 = (f32[12,512]{1,0:T(8,128)S(1)}, f32[12,512]{1,0:T(8,128)}, u32[]{:S(2)}) copy-start(f32[12,512]{1,0:T(8,128)} %param.37) | copy-start | bytes 73732
  0.8 118.9 %copy-start.8 = (f32[64,512]{1,0:T(8,128)S(1)}, f32[64,512]{1,0:T(8,128)}, u32[]{:S(2)}) copy-start(f32[64,512]{1,0:T(8,128)} %param.34) | copy-start | bytes 393220
  0.8 115.8 %copy-start.17 = (f32[64,128]{1,0:T(8,128)S(1)}, f32[64,128]{1,0:T(8,128)}, u32[]{:S(2)}) copy-start(f32[64,128]{1,0:T(8,128)} %param.33) | copy-start | bytes 98308
  0.8 117.2 %copy-start.13 = (f32[64,384]{1,0:T(8,128)S(1)}, f32[64,384]{1,0:T(8,128)}, u32[]{:S(2)}) copy-start(f32[64,384]{1,0:T(8,128)} %param.32) | copy-start | bytes 294916
  0.8 118.9 %copy-start.7 = (f32[64,512]{1,0:T(8,128)S(1)}, f32[64,512]{1,0:T(8,128)}, u32[]{:S(2)}) copy-start(f32[64,512]{1,0:T(8,128)} %param.30) | copy-start | bytes 393220
  0.8 115.8 %copy-start.16 = (f32[64,128]{1,0:T(8,128)S(1)}, f32[64,128]{1,0:T(8,128)}, u32[]{:S(2)}) copy-start(f32[64,128]{1,0:T(8,128)} %param.29) | copy-start | bytes 98308
  0.8 117.2 %copy-start.12 = (f32[64,384]{1,0:T(8,128)S(1)}, f32[64,384]{1,0:T(8,128)}, u32[]{:S(2)}) copy-start(f32[64,384]{1,0:T(8,128)} %param.28) | copy-start | bytes 294916
  6.0 115.5 %copy-start.3 = (f32[256,128]{1,0:T(8,128)S(1)}, f32[256,128]{1,0:T(8,128)}, u32[]{:S(2)}) copy-start(f32[256,128]{1,0:T(8,128)} %refs_8_.1) | copy-start | bytes 393220
  6.0 115.5 %copy-start.9 = (f32[256,128]{1,0:T(8,128)S(1)}, f32[256,128]{1,0:T(8,128)}, u32[]{:S(2)}) copy-start(f32[256,128]{1,0:T(8,128)} %param.31) | copy-start | bytes 393220
  6.0 115.5 %copy-start.10 = (f32[256,128]{1,0:T(8,128)S(1)}, f32[256,128]{1,0:T(8,128)}, u32[]{:S(2)}) copy-start(f32[256,128]{1,0:T(8,128)} %param.35) | copy-start | bytes 393220
  113.7 7.9 %copy-start.11 = (f32[256,128]{1,0:T(8,128)S(1)}, f32[256,128]{1,0:T(8,128)}, u32[]{:S(2)}) copy-start(f32[256,128]{1,0:T(8,128)} %get-tuple-element.32) | copy-start | bytes 393220
  113.7 8.7 %copy-start.1 = (bf16[1024,512]{1,0:T(8,128)(2,1)S(1)}, bf16[1024,512]{1,0:T(8,128)(2,1)}, u32[]{:S(2)}) copy-start(bf16[1024,512]{1,0:T(8,128)(2,1)} %get-tuple-element.27) | copy-start | bytes 3145732
  119.6 3.7 %copy-start = (f32[1024,512]{1,0:T(8,128)S(1)}, f32[1024,512]{1,0:T(8,128)}, u32[]{:S(2)}) copy-start(f32[1024,512]{1,0:T(8,128)} %get-tuple-element.28) | copy-start | bytes 6291460

commit v4 on v3

--- a/solution.py
+++ b/solution.py
@@ -378,7 +378,7 @@
 
 def turned(total, count):
     size = total // count
-    return [lambda slab, k=k: (lax.rem(slab + k, count) * size, size) for k in range(count)]
+    return [lambda slab, k=k: ((slab + k) % count * size, size) for k in range(count)]
 
 
 def scatter_buffers(shape):
@@ -485,7 +485,7 @@
     bias_grad: typing.Any
     up_sum: typing.Any
     att_sum: typing.Any
-    out_low: typing.Any
+    units: typing.Any
     load_sems: typing.Any
     whole_qkv: typing.Any
     whole_proj: typing.Any
@@ -495,7 +495,7 @@
 
 def block_kernel(slabs, clips, *refs):
     refs = list(refs)
-    tokens, y_grad, units, vectors, table = refs[:5]
+    tokens, y_grad, clip_rows, vectors, table = refs[:5]
     masters = refs[5:9]
     block_out, x_grad, small_out = refs[9:12]
     owned = refs[12:16]
@@ -524,7 +524,7 @@
     tiles = width // 128
     score_scale = head**-0.5
     grad_scale = float(tok * slabs * clips) ** -0.5
-    slots = s.lent.shape[0]
+    slots = s.lent.shape[1]
 
     loads = [
         pltpu.make_async_copy(tokens, xb, s.load_sems.at[0]),
@@ -557,26 +557,48 @@
     )
     later = proj_copies + up_copies
     later = proj_copies + up_copies + down_copies
+    copy_0, copy_1, copy_2 = qkv_copies
     queue = Queue(
         [
             [flow.first for flow in qkv_copies],
             [flow.second for flow in qkv_copies] + [flow.first for flow in later[:3]],
             [flow.third for flow in qkv_copies] + [flow.first for flow in later[3:]],
-            [flow.second for flow in later[:3]],
-            [flow.fourth for flow in qkv_copies],
+            [copy_0.fourth, copy_1.fourth] + [flow.second for flow in later[:3]],
+            [copy_2.fourth],
         ]
         + staggered(later, 3, 2)
     )
     place.meet()
     queue.until(qkv_copies[-1].first)
 
-    heads = [units[HEADS_AT, i] for i in range(slots)]
-    tails = [units[TAILS_AT, i] for i in range(slots)]
-    used = units[USED_AT, 0]
+    units, count = s.units, tok // unit
+    starts, ends, position = [], [], 0
+    for slot in range(slots):
+        starts.append(position)
+        position = position + clip_rows[0, slot] // (slabs * unit // BINS)
+        ends.append(position)
+    for u in range(count):
+        inside, last, first = 0, 0, 0
+        for slot in range(slots):
+            here = jnp.where((starts[slot] <= u) & (u < ends[slot]), 1, 0)
+            inside += here
+            last += here * jnp.where(ends[slot] == u + 1, 1 + slot, 0)
+            first += here * jnp.where(starts[slot] == u, 1 + slot, 0)
+        begin, back = u * per_unit + inside, u * per_unit - inside
+        units[BEGIN_AT, u] = begin
+        units[SECOND_AT, u] = jnp.where(last > 0, tok // half + last - 1, begin + per_unit - 1)
+        units[FRONT_AT, u] = jnp.where(first > 0, tok // half + first - 1, jnp.maximum(back, 0))
+        units[BACK_AT, u] = back + 1
+        units[WRAP_AT, u] = jnp.where((last > 0) & (place.slab == slabs - 1), 1, 0)
+    heads = [jnp.minimum(starts[slot], count - 1) * per_unit for slot in range(slots)]
+    tails = [jnp.maximum(ends[slot] * per_unit - 1, 0) for slot in range(slots)]
+    used = position * unit
 
     heads_of = lax.broadcasted_iota(jnp.int32, (HEADS, width), 1) // head
     spread = (heads_of == lax.broadcasted_iota(jnp.int32, (HEADS, width), 0)).astype(jnp.float32)
-    by_offset = jnp.dot(table[...], spread, precision=HIGHEST)
+    by_offset = lax.dot_general(
+        table[...], spread, (((0,), (0,)), ((), ())), precision=HIGHEST
+    )
     key = lax.broadcasted_iota(jnp.int32, (group, width), 0)
     query = lax.broadcasted_iota(jnp.int32, (group, width), 1) % group
     key_row, key_bin, query_row, query_bin = key // BINS, key % BINS, query // BINS, query % BINS
@@ -590,8 +612,10 @@
     for r in range(RELS):
         total = jnp.where(offset == r, by_offset[r : r + 1, :], total)
     total = jnp.where(same, total, masked_score)
-    bias[0] = total
-    bias[1] = jnp.where(key_row // (WIN // 2) == query_row // (WIN // 2), total, masked_score)
+    apart = jnp.where(key_row // (WIN // 2) == query_row // (WIN // 2), total, masked_score)
+    for t in range(tiles):
+        bias[2 * t] = total[:, 128 * t : 128 * (t + 1)]
+        bias[2 * t + 1] = apart[:, 128 * t : 128 * (t + 1)]
     lane = lax.broadcasted_iota(jnp.int32, (group, 128), 1) // head
     picks = [(lane == h).astype(jnp.bfloat16) for h in range(pack)]
 
@@ -605,7 +629,7 @@
         return result
 
     loads[0].wait()
-    chunk = 256
+    chunk, wide_chunk = 256, 512
 
     @pl.loop(0, tok // chunk)
     def _(i):
@@ -626,146 +650,144 @@
         eb[span(i, chunk), :] = low
         s.et[:, span(i, chunk)] = low.T
 
-    queue.until(qkv_copies[-1].fourth)
-    for flow in qkv_copies:
-        flow.last()
+    queue.until(copy_0.fourth)
     whole_qkv, whole_proj = s.whole_qkv, s.whole_proj
     whole_up, whole_down = s.whole_up, s.whole_down
+    before = (lax.rem(place.slab + slabs - 1, slabs), place.clip)
+    after = (lax.rem(place.slab + 1, slabs), place.clip)
 
     qkv_bias = jnp.concatenate(
         [vectors[2:3, :], jnp.zeros((1, width), jnp.float32), vectors[3:4, :]], 1
     )
-    head_in = jnp.concatenate(
-        [s.attn_in[heads[i]] for i in range(slots)], 0
-    )
-    put_rows(s.lent, 0, (mm(head_in, flat(whole_qkv)) + qkv_bias).astype(jnp.bfloat16))
-    before = (lax.rem(place.slab + slabs - 1, slabs), place.clip)
-    after = (lax.rem(place.slab + 1, slabs), place.clip)
-    lend = links.send(s.lent, s.borrowed, before)
-    queue.take()
-
-    @pl.loop(0, tok // chunk)
-    def _(i):
-        rows = mm(rows_of(s.attn_in, i, chunk), flat(whole_qkv)) + qkv_bias
-        put_rows(own, i, rows.astype(jnp.bfloat16))
-
-    queue.take()
+    head_in = jnp.concatenate([s.attn_in[heads[i]] for i in range(slots)], 0)
+    lends, lends_back, gives, gives_back = {}, {}, {}, {}
+
+    def ranges(t):
+        return [slice(k * width + 128 * t, k * width + 128 * (t + 1)) for k in range(3)]
+
+    def project(t):
+        shift = jnp.concatenate([qkv_bias[:, at] for at in ranges(t)], 1)
+        weights = jnp.concatenate([flat(whole_qkv, at) for at in ranges(t)], 1)
+        rows = (mm(head_in, weights) + shift).astype(jnp.bfloat16)
+        s.lent[t] = rows.reshape(slots, half, -1)
+        lends[t] = links.send(s.lent.at[t], s.borrowed.at[t], before)
+
+        @pl.loop(0, tok // wide_chunk)
+        def _(i):
+            weights = jnp.concatenate([flat(whole_qkv, at) for at in ranges(t)], 1)
+            rows = (mm(rows_of(s.attn_in, i, wide_chunk), weights) + shift).astype(jnp.bfloat16)
+            own[t, span(i, wide_chunk // half)] = rows.reshape(wide_chunk // half, half, -1)
 
     groups_unit = unit // group
 
-    def window(ref, u, j):
+    def window(ref, t, u, j):
         begin = units[BEGIN_AT, u] + 2 * j
-        if j < groups_unit - 1:
-            return blocks(ref, begin, 2)
-        return jnp.concatenate([ref[begin], ref[units[SECOND_AT, u]]], 0)
+        second = begin + 1 if j < groups_unit - 1 else units[SECOND_AT, u]
+        return jnp.concatenate([ref[t, begin], ref[t, second]], 0)
 
     def parts(rows):
-        return [
-            [rows[:, k * width + 128 * t : k * width + 128 * (t + 1)] for t in range(tiles)]
-            for k in range(rows.shape[1] // width)
-        ]
-
-    def forward(works):
-        rows = [parts(window(own, u, j)) for u, j in works]
+        return [rows[:, 128 * k : 128 * (k + 1)] for k in range(3)]
+
+    def forward(t, works):
+        rows = [parts(window(own, t, u, j)) for u, j in works]
         wraps = [units[WRAP_AT, u] if j == groups_unit - 1 else 0 for u, j in works]
-        scores = [
-            jnp.concatenate([mm_nt(k, stacked(q)) for q, k in zip(queries, keys)], 1)
-            for queries, keys, _ in rows
-        ]
-        scores = [score * score_scale + bias[wrap] for score, wrap in zip(scores, wraps)]
+        scores = [mm_nt(k, stacked(q)) for q, k, _ in rows]
+        scores = [score * score_scale + bias[2 * t + wrap] for score, wrap in zip(scores, wraps)]
         weights = [jnp.exp(score - jnp.max(score, 0, keepdims=True)) for score in scores]
         weights = [weight * (1.0 / jnp.sum(weight, 0, keepdims=True)) for weight in weights]
-        lows = [weight.astype(jnp.bfloat16) for weight in weights]
         for (u, j), weight in zip(works, weights):
-            s.probs[span(u * groups_unit + j, group), :] = weight
+            s.probs[span(u * groups_unit + j, group), 128 * t : 128 * (t + 1)] = weight
         mixed = [
-            [mm_tn(low[:, 128 * t : 128 * (t + 1)], v) for t, v in enumerate(values)]
-            for low, (_, _, values) in zip(lows, rows)
+            mm_tn(weight.astype(jnp.bfloat16), v) for weight, (_, _, v) in zip(weights, rows)
         ]
-        for (u, j), products in zip(works, mixed):
-            out = jnp.concatenate([folded(product) for product in products], 1)
-            out = out.astype(jnp.bfloat16).reshape(2, half, width)
-            s.att_win[span(u * groups_unit + j, 2)] = out
-
-    def sweep(step, exchange, give_back, first, second, third):
-        @pl.loop(0, unit_count // 2)
-        def _(u):
-            step([(u, j) for j in range(groups_unit - 1)])
-
-        first()
-        exchange()
-
-        @pl.loop(0, unit_count // 2)
-        def _(u):
-            step([(2 * u, groups_unit - 1), (2 * u + 1, groups_unit - 1)])
-
-        handle = give_back()
-        second()
-
-        @pl.loop(unit_count // 2, 3 * unit_count // 4)
-        def _(u):
-            step([(u, j) for j in range(groups_unit - 1)])
-
-        third()
-
-        @pl.loop(3 * unit_count // 4, unit_count)
-        def _(u):
-            step([(u, j) for j in range(groups_unit - 1)])
-
-        handle()
-
-    def give_back_from(ref, out, arrived):
-        def send():
-            for slot in range(slots):
-                out[slot] = ref[tails[slot]]
-            return take_lent(links.send(out, arrived, after), arrived, ref)
-
-        return send
-
-    def from_windows(ref, target, target_t=None):
+        for (u, j), product in zip(works, mixed):
+            out = folded(product).astype(jnp.bfloat16).reshape(2, half, 128)
+            s.att_win[t, span(u * groups_unit + j, 2)] = out
+
+    units_step = 4
+
+    def inner(step, t):
+        @pl.loop(0, unit_count // units_step)
+        def _(i):
+            step(
+                t,
+                [
+                    (i * units_step + k, j)
+                    for k in range(units_step)
+                    for j in range(groups_unit - 1)
+                ],
+            )
+
+    def outer(step, t, lent, arrived, ref):
+        if lent is not None:
+            lent.wait_recv()
+            ref[t, tok // half :] = arrived[t]
+        step(t, [(u, groups_unit - 1) for u in range(unit_count)])
+
+    def give_back(ref, t, out, arrived):
+        for slot in range(slots):
+            out[t, slot] = ref[t, tails[slot]]
+        return links.send(out.at[t], arrived.at[t], after)
+
+    def from_windows(ref, t, given, arrived, store):
+        given.wait_recv()
+        ref[t, tok // half :] = arrived[t]
+
         @pl.loop(0, unit_count)
         def _(u):
-            front = ref[units[FRONT_AT, u]]
-            back = blocks(ref, units[BACK_AT, u], per_unit - 1)
-            rows = jnp.concatenate([front, back], 0)
-            target[span(u, unit), :] = rows
-            if target_t is not None:
-                target_t[:, span(u, unit)] = rows.T
-
-    def take_lent(copy, arrived, ref):
-        def take():
-            copy.wait_recv()
-            ref[tok // half :] = arrived[...]
-
-        return take
-
-    def taking(source, count):
-        return lambda: source.take(count)
-
-    sweep(
-        forward,
-        take_lent(lend, s.borrowed, own),
-        give_back_from(s.att_win, s.att_out, s.att_back),
-        taking(queue, 1),
-        taking(queue, 1),
-        taking(queue, 1),
-    )
-    from_windows(s.att_win, s.att_rows, s.att_t)
+            back = units[BACK_AT, u]
+            rows = [ref[t, units[FRONT_AT, u]]] + [ref[t, back + k] for k in range(per_unit - 1)]
+            store(t, u, jnp.concatenate(rows, 0))
+
+    def place_attended(t, u, rows):
+        cols = slice(128 * t, 128 * (t + 1))
+        s.att_rows[span(u, unit), cols] = rows
+        s.att_t[cols, span(u, unit)] = rows.T
+
+    def outer_forward(t):
+        outer(forward, t, lends[t], s.borrowed, own)
+        gives[t] = give_back(s.att_win, t, s.att_out, s.att_back)
+
+    copy_0.last()
+    project(0)
+    inner(forward, 0)
+    queue.until(copy_2.fourth)
+    copy_1.last()
+    project(1)
+    queue.take()
+    inner(forward, 1)
+    copy_2.last()
+    outer_forward(0)
+    for t in range(2, tiles):
+        project(t)
+    queue.take()
+    inner(forward, 2)
+    queue.take()
+    outer_forward(1)
+    outer_forward(2)
+    queue.take()
+    for t in range(3, tiles):
+        outer_forward(t)
+        queue.take()
+        inner(forward, t)
+    queue.take()
+    for t in range(tiles):
+        from_windows(s.att_win, t, gives[t], s.att_back, place_attended)
 
     queue.take()
     for flow in proj_copies:
         flow.last()
     mid, mlp_in = s.mid, s.mlp_in
 
-    @pl.loop(0, tok // chunk)
+    @pl.loop(0, tok // wide_chunk)
     def _(i):
-        rows = mm(s.att_rows[span(i, chunk), :], flat(whole_proj))
-        rows = xb[span(i, chunk), :].astype(jnp.float32) + rows + vectors[4:5, :]
-        mid[span(i, chunk), :] = rows
+        rows = mm(s.att_rows[span(i, wide_chunk), :], flat(whole_proj))
+        rows = xb[span(i, wide_chunk), :].astype(jnp.float32) + rows + vectors[4:5, :]
+        mid[span(i, wide_chunk), :] = rows
         normed, _ = norm_parts(rows)
         low = (normed * vectors[5:6, :] + vectors[6:7, :]).astype(jnp.bfloat16)
-        mlp_in[span(i, chunk), :] = low
-        s.mlp_in_t[:, span(i, chunk)] = low.T
+        mlp_in[span(i, wide_chunk), :] = low
+        s.mlp_in_t[:, span(i, wide_chunk)] = low.T
 
     act, slope = s.act, s.slope
     wide = act.shape[1] // width
@@ -777,15 +799,15 @@
         piece = slice(k * size, (k + 1) * size)
         shift = jnp.concatenate([vectors[8 + c : 9 + c, piece] for c in range(wide)], 1)
 
-        @pl.loop(0, tok // chunk)
+        @pl.loop(0, 1)
         def _(i):
             weights = jnp.concatenate([flat(whole_up, at) for at in lanes], 1)
-            pre = mm(mlp_in[span(i, chunk), :], weights)
+            pre = mm(mlp_in[span(i, tok), :], weights)
             value, derivative = gelu_parts(pre + shift)
             value, derivative = value.astype(jnp.bfloat16), derivative.astype(jnp.bfloat16)
             for c, at in enumerate(lanes):
-                act[span(i, chunk), at] = value[:, c * size : (c + 1) * size]
-                slope[span(i, chunk), at] = derivative[:, c * size : (c + 1) * size]
+                act[span(i, tok), at] = value[:, c * size : (c + 1) * size]
+                slope[span(i, tok), at] = derivative[:, c * size : (c + 1) * size]
 
         queue.take()
 
@@ -811,49 +833,46 @@
         weights = whole_down[c].reshape(width, width)
 
         def step(i, sums):
-            grad = mm_nt(eb[span(i, chunk), :], weights)
-            low = grad * slope[span(i, chunk), cols].astype(jnp.float32)
+            grad = mm_nt(eb[span(i, tok), :], weights)
+            low = grad * slope[span(i, tok), cols].astype(jnp.float32)
             low = low.astype(jnp.bfloat16)
-            slope[span(i, chunk), cols] = low
+            slope[span(i, tok), cols] = low
             return sums + jnp.sum(low.astype(jnp.float32), 0, keepdims=True)
 
-        sums = lax.fori_loop(0, tok // chunk, step, jnp.zeros((1, width), jnp.float32))
+        sums = lax.fori_loop(0, 1, step, jnp.zeros((1, width), jnp.float32))
         s.up_sum[c : c + 1, :] = sums
 
     for c in range(wide):
         pre_back(c)
-        if c == 1:
-            down_flows[0].second()
-        if c == 2:
-            down_flows[1].second()
 
     up = up_parts[0]
 
-    def keep(target, slab, part):
+    def keep(target, slab, part, lanes=EVERY):
         part = (part * grad_scale).astype(jnp.bfloat16)
         part = part.reshape(clips // 2, 2, 2, -1, part.shape[-1])
         for y in range(2):
             for h in range(2):
-                target[slab, y, h] = part[:, y, h]
-
-    @pl.loop(0, slabs)
-    def _(i):
+                target[slab, y, h, :, :, lanes] = part[:, y, h]
+
+    def up_grad(i):
         keep(up, i, mm(s.mlp_in_t[...], slope[:, span(i, act.shape[1] // slabs)]))
 
+    pl.loop(0, slabs // 2)(up_grad)
+    for flow in down_flows:
+        flow.second()
+    pl.loop(slabs // 2, slabs)(up_grad)
     for flow in up_flows:
         flow.first()
-    down_flows[0].third()
-    down_flows[1].third()
 
     mid_grad, mid_low = s.mid_grad, s.mid_low
 
     def mid_step(i, sums):
-        grad = mm_nt(slope[span(i, chunk), :], flat(whole_up))
-        normed, inverse = norm_parts(mid[span(i, chunk), :])
-        out_grad = eb[span(i, chunk), :].astype(jnp.float32)
+        grad = mm_nt(slope[span(i, tok), :], flat(whole_up))
+        normed, inverse = norm_parts(mid[span(i, tok), :])
+        out_grad = eb[span(i, tok), :].astype(jnp.float32)
         rows = out_grad + norm_back(normed, inverse, grad * vectors[5:6, :])
         low = rows.astype(jnp.bfloat16)
-        mid_grad[span(i, chunk), :] = rows
+        mid_grad[span(i, tok), :] = rows
         put_rows(mid_low, i, low)
         return tuple(
             old + jnp.sum(new, 0, keepdims=True)
@@ -861,114 +880,114 @@
         )
 
     zero = jnp.zeros((1, width), jnp.float32)
-    mid_sums = lax.fori_loop(0, tok // chunk, mid_step, (zero,) * 4)
+    mid_sums = lax.fori_loop(0, 1, mid_step, (zero,) * 4)
     for row, value in zip((4, 5, 6, 7), mid_sums):
         small.held[0, row : row + 1, :] = value * grad_scale
     small.held[0, 8:12, :] = s.up_sum[...] * grad_scale
-    up_flows[0].second()
-    up_flows[1].second()
-    down_flows[0].fourth()
 
     proj_columns = flat(whole_proj)
     head_low = jnp.concatenate(
         [mid_low[heads[i]] for i in range(slots)], 0
     )
-    put_rows(s.dlent, 0, mm_nt(head_low, proj_columns).astype(jnp.bfloat16))
+    rows = mm_nt(head_low, proj_columns).astype(jnp.bfloat16)
+    for t in range(tiles):
+        s.dlent[t] = rows[:, 128 * t : 128 * (t + 1)].reshape(slots, half, 128)
     lend_back = links.send(s.dlent, s.dborrowed, before)
     dwin_own = s.dwin_own
 
-    @pl.loop(0, tok // chunk)
+    @pl.loop(0, tok // wide_chunk)
     def _(i):
-        rows = mm_nt(rows_of(mid_low, i, chunk), flat(whole_proj))
-        put_rows(dwin_own, i, rows.astype(jnp.bfloat16))
+        rows = mm_nt(rows_of(mid_low, i, wide_chunk), flat(whole_proj))
+        rows = rows.astype(jnp.bfloat16)
+        for t in range(tiles):
+            part = rows[:, 128 * t : 128 * (t + 1)].reshape(-1, half, 128)
+            dwin_own[t, span(i, part.shape[0])] = part
 
     grad = mm(s.att_t[...], mid_low[...].reshape(tok, width))
     for i in range(slabs):
         keep(proj_flow.held, i, grad[:, i * (width // slabs) : (i + 1) * (width // slabs)])
     proj_flow.first()
-    down_flows[1].fourth()
-    up_flows[0].third()
+    for flow in up_flows:
+        flow.second()
 
     bias_grad, qg_win = s.bias_grad, s.qg_win
     bias_grad[...] = jnp.zeros_like(bias_grad)
 
-    def backward(works):
-        rows = [parts(window(own, u, j)) for u, j in works]
-        places = [span(u * groups_unit + j, group) for u, j in works]
-        mixed = [[stacked(g) for g in parts(window(dwin_own, u, j))[0]] for u, j in works]
-        weights = [s.probs[at, :] for at in places]
-        lows = [weight.astype(jnp.bfloat16) for weight in weights]
-        prob_grads = [
-            jnp.concatenate([mm_nt(v, g) for v, g in zip(values, grads)], 1)
-            for (_, _, values), grads in zip(rows, mixed)
-        ]
-        value_grads = [
-            [mm(low[:, 128 * t : 128 * (t + 1)], g) for t, g in enumerate(grads)]
-            for low, grads in zip(lows, mixed)
-        ]
+    def backward(t, works):
+        cols = slice(128 * t, 128 * (t + 1))
+        rows = [parts(window(own, t, u, j)) for u, j in works]
+        mixed = [stacked(window(dwin_own, t, u, j)) for u, j in works]
+        weights = [s.probs[span(u * groups_unit + j, group), cols] for u, j in works]
+        prob_grads = [mm_nt(v, g) for (_, _, v), g in zip(rows, mixed)]
+        value_grads = [mm(weight.astype(jnp.bfloat16), g) for weight, g in zip(weights, mixed)]
         scores = [
             (weight * (grad - jnp.sum(weight * grad, 0, keepdims=True))).astype(jnp.bfloat16)
             for weight, grad in zip(weights, prob_grads)
         ]
-        bias_grad[...] += sum(score.astype(jnp.float32) for score in scores)
-        key_grads = [
-            [
-                mm(score[:, 128 * t : 128 * (t + 1)], stacked(q)) * score_scale
-                for t, q in enumerate(queries)
-            ]
-            for score, (queries, _, _) in zip(scores, rows)
-        ]
+        bias_grad[:, cols] += sum(score.astype(jnp.float32) for score in scores)
+        key_grads = [mm(score, stacked(q)) * score_scale for score, (q, _, _) in zip(scores, rows)]
         query_grads = [
-            [
-                folded(mm_tn(score[:, 128 * t : 128 * (t + 1)], k)) * score_scale
-                for t, k in enumerate(keys)
-            ]
-            for score, (_, keys, _) in zip(scores, rows)
+            folded(mm_tn(score, k)) * score_scale for score, (_, k, _) in zip(scores, rows)
         ]
         for (u, j), *grads in zip(works, query_grads, key_grads, value_grads):
-            out = jnp.concatenate([tile for grad in grads for tile in grad], 1)
-            out = out.astype(jnp.bfloat16).reshape(2, half, 3 * width)
-            qg_win[span(u * groups_unit + j, 2)] = out
-
-    def after_first():
-        up_flows[1].third()
-        proj_flow.second()
-
-    def after_second():
-        up_flows[0].fourth()
-
-    def after_third():
-        up_flows[1].fourth()
-        proj_flow.third()
-
-    sweep(
-        backward,
-        take_lent(lend_back, s.dborrowed, dwin_own),
-        give_back_from(qg_win, s.qg_out, s.qg_back),
-        after_first,
-        after_second,
-        after_third,
-    )
+            out = jnp.concatenate(grads, 1).astype(jnp.bfloat16)
+            qg_win[t, span(u * groups_unit + j, 2)] = out.reshape(2, half, -1)
+
     qg_rows = s.qg_rows
-    from_windows(qg_win, qg_rows)
-
-    pair = 2
-    for i in range(slabs // pair):
-        size = 3 * width // slabs
-        grad = mm(s.attn_in_t[...], qg_rows[:, i * pair * size : (i + 1) * pair * size])
-        for k in range(pair):
-            keep(qkv_parts[0], i * pair + k, grad[:, k * size : (k + 1) * size])
-    for flow in qkv_flows:
-        flow.first()
-    proj_flow.fourth()
-
+
+    def place_grads(t, u, rows):
+        for k, at in enumerate(ranges(t)):
+            qg_rows[span(u, unit), at] = rows[:, 128 * k : 128 * (k + 1)]
+
+    def qkv_grad(flow):
+        starts = []
+        for slab in range(slabs):
+            start, size = flow.columns(slab)
+            starts.append((int(start) + slab * 3 * width // slabs, int(start), size))
+        rows = jnp.concatenate([qg_rows[:, at : at + size] for at, _, size in starts], 1)
+        grad = mm(s.attn_in_t[...], rows)
+        for slab, (_, start, size) in enumerate(starts):
+            part = grad[:, slab * size : (slab + 1) * size]
+            keep(qkv_parts[0], slab, part, slice(start, start + size))
+
+    inner(backward, 0)
+    for flow in down_flows:
+        flow.third()
+    lend_back.wait_recv()
+    dwin_own[:, tok // half :] = s.dborrowed[...]
+    for t in range(tiles):
+        outer(backward, t, None, None, None)
+        gives_back[t] = give_back(qg_win, t, s.qg_out, s.qg_back)
+    proj_flow.second()
+    inner(backward, 1)
+    for flow in up_flows:
+        flow.third()
+    for t in range(2):
+        from_windows(qg_win, t, gives_back[t], s.qg_back, place_grads)
+    qkv_grad(qkv_flows[0])
+    qkv_flows[0].first()
+    inner(backward, 2)
+    for flow in down_flows:
+        flow.fourth()
+    from_windows(qg_win, 2, gives_back[2], s.qg_back, place_grads)
+    qkv_grad(qkv_flows[1])
+    qkv_flows[1].first()
+    qkv_flows[0].second()
+    inner(backward, 3)
+    from_windows(qg_win, 3, gives_back[3], s.qg_back, place_grads)
+    qkv_grad(qkv_flows[2])
+    qkv_flows[2].first()
+    qkv_flows[1].second()
+    proj_flow.third()
+    for flow in up_flows:
+        flow.fourth()
 
     def in_step(i, sums):
-        rows = qg_rows[span(i, chunk), :]
+        rows = qg_rows[span(i, wide_chunk), :]
         grad = mm_nt(rows, flat(whole_qkv))
-        normed, inverse = norm_parts(xb[span(i, chunk), :].astype(jnp.float32))
+        normed, inverse = norm_parts(xb[span(i, wide_chunk), :].astype(jnp.float32))
         back = norm_back(normed, inverse, grad * vectors[0:1, :])
-        mid_grad[span(i, chunk), :] = mid_grad[span(i, chunk), :] + back
+        mid_grad[span(i, wide_chunk), :] = mid_grad[span(i, wide_chunk), :] + back
         query_part = rows[:, :width].astype(jnp.float32)
         value_part = rows[:, 2 * width :].astype(jnp.float32)
         return tuple(
@@ -976,7 +995,7 @@
             for old, new in zip(sums, (grad * normed, grad, query_part, value_part))
         )
 
-    in_sums = lax.fori_loop(0, tok // chunk, in_step, (zero,) * 4)
+    in_sums = lax.fori_loop(0, tok // wide_chunk, in_step, (zero,) * 4)
     store_grad = pltpu.make_async_copy(mid_grad, x_grad, s.load_sems.at[1])
     store_grad.start()
     for row, value in zip((0, 1, 2, 3), in_sums):
@@ -994,25 +1013,23 @@
         small.held[0, 12:16, 128 * i : 128 * (i + 1)] = sums[4 * i : 4 * i + 4, :]
 
     small.first()
-    for flow in qkv_flows:
-        flow.second()
+    qkv_flows[2].second()
+    qkv_flows[0].third()
+    qkv_flows[1].third()
+    proj_flow.fourth()
     small.second()
 
-    out_low = s.out_low
-
-    @pl.loop(0, tok // chunk)
+    out_low = s.att_rows
+
+    @pl.loop(0, tok // wide_chunk)
     def _(i):
-        rows = mid[span(i, chunk), :] + mm(act[span(i, chunk), :], flat(whole_down))
-        live = lax.broadcasted_iota(jnp.int32, (chunk, width), 0) + i * chunk < used
+        rows = mid[span(i, wide_chunk), :] + mm(act[span(i, wide_chunk), :], flat(whole_down))
+        live = lax.broadcasted_iota(jnp.int32, (wide_chunk, width), 0) + i * wide_chunk < used
         rows = jnp.where(live, rows + vectors[7:8, :], 0.0)
-        out_low[span(i, chunk), :] = rows.astype(jnp.bfloat16)
+        out_low[span(i, wide_chunk), :] = rows.astype(jnp.bfloat16)
 
     store_out = pltpu.make_async_copy(out_low, block_out, s.load_sems.at[0])
     store_out.start()
-
-    for flow in qkv_flows:
-        flow.third()
-    small.third()
 
     def finish(flows, out, turn):
         for flow in flows:
@@ -1025,10 +1042,13 @@
                 out[rows:, lanes] = total[1]
 
     finish(down_flows, owned[3], True)
+    qkv_flows[2].third()
+    qkv_flows[0].fourth()
+    qkv_flows[1].fourth()
+    small.third()
     finish(up_flows, owned[2], False)
     finish([proj_flow], owned[1], False)
-    for flow in qkv_flows:
-        flow.fourth()
+    qkv_flows[2].fourth()
     small.fourth()
     finish(qkv_flows, owned[0], False)
     small_out[...] = small.last()
@@ -1037,35 +1057,7 @@
     links.drain()
 
 
-BEGIN_AT, SECOND_AT, FRONT_AT, BACK_AT, WRAP_AT, HEADS_AT, TAILS_AT, USED_AT = range(8)
-
-
-def unit_table(lengths, slab_size, tok):
-    unit, half = SHORT // slab_size * BINS, WIN // 2 * BINS
-    count, size = tok // unit, unit // half
-    at = jnp.arange(count, dtype=jnp.int32)
-    segment = lengths // slab_size * BINS // unit
-    ends = jnp.cumsum(segment)
-    starts = ends - segment
-    slots = jnp.arange(1, lengths.shape[0] + 1, dtype=jnp.int32)
-    here = (starts[:, None] <= at) & (at < ends[:, None])
-    inside = jnp.sum(here, 0)
-    last = jnp.sum(jnp.where(here & (ends[:, None] == at + 1), slots[:, None], 0), 0)
-    first = jnp.sum(jnp.where(here & (starts[:, None] == at), slots[:, None], 0), 0)
-    begin = at * size + inside
-    front = jnp.maximum(at * size - inside, 0)
-    blocks_own = tok // half
-    pad = (0, count - lengths.shape[0])
-    return jnp.stack([
-        begin,
-        jnp.where(last > 0, blocks_own + last - 1, begin + size - 1),
-        jnp.where(first > 0, blocks_own + first - 1, front),
-        at * size - inside + 1,
-        ((last > 0) & (lax.axis_index(SLAB) == slab_size - 1)).astype(jnp.int32),
-        jnp.pad(jnp.minimum(starts, count - 1) * size, pad),
-        jnp.pad(jnp.maximum(ends * size - 1, 0), pad),
-        jnp.full((count,), ends[-1] * unit),
-    ]).astype(jnp.int32)
+BEGIN_AT, SECOND_AT, FRONT_AT, BACK_AT, WRAP_AT = range(5)
 
 
 def block_call(tokens, y_grad, clip_rows, vectors, table, masters, slab_size, clip_size):
@@ -1079,6 +1071,7 @@
     hidden = masters[2].shape[1] * slab_size
     slots = clip_rows.shape[1]
     half = WIN // 2 * BINS
+    tiles = width // 128
     low, full = jnp.bfloat16, jnp.float32
     helds = []
     for position, master in enumerate(masters):
@@ -1094,23 +1087,23 @@
     held = Held(
         xb=buffer(tok, width), eb=buffer(tok, width), et=buffer(width, tok),
         attn_in=buffer(tok // half, half, width), attn_in_t=buffer(width, tok),
-        own=buffer(tok // half + slots, half, 3 * width), lent=buffer(slots, half, 3 * width),
-        borrowed=buffer(slots, half, 3 * width),
-        probs=buffer(tok, width, full), att_win=buffer(tok // half + slots, half, width),
-        att_out=buffer(slots, half, width), att_back=buffer(slots, half, width), att_rows=buffer(tok, width), att_t=buffer(width, tok),
+        own=buffer(tiles, tok // half + slots, half, 384), lent=buffer(tiles, slots, half, 384),
+        borrowed=buffer(tiles, slots, half, 384),
+        probs=buffer(tok, width, full), att_win=buffer(tiles, tok // half + slots, half, 128),
+        att_out=buffer(tiles, slots, half, 128), att_back=buffer(tiles, slots, half, 128), att_rows=buffer(tok, width), att_t=buffer(width, tok),
         mid=buffer(tok, width, full), mlp_in=buffer(tok, width), mlp_in_t=buffer(width, tok),
         act=buffer(tok, hidden), slope=buffer(tok, hidden), mid_grad=buffer(tok, width, full),
-        mid_low=buffer(tok // half, half, width), dwin_own=buffer(tok // half + slots, half, width), dlent=buffer(slots, half, width),
-        dborrowed=buffer(slots, half, width), qg_win=buffer(tok // half + slots, half, 3 * width),
-        qg_out=buffer(slots, half, 3 * width), qg_back=buffer(slots, half, 3 * width), qg_rows=buffer(tok, 3 * width),
-        bias=buffer(2, WIN * BINS, width, full), bias_grad=buffer(WIN * BINS, width, full),
+        mid_low=buffer(tok // half, half, width), dwin_own=buffer(tiles, tok // half + slots, half, 128), dlent=buffer(tiles, slots, half, 128),
+        dborrowed=buffer(tiles, slots, half, 128), qg_win=buffer(tiles, tok // half + slots, half, 384),
+        qg_out=buffer(tiles, slots, half, 384), qg_back=buffer(tiles, slots, half, 384), qg_rows=buffer(tok, 3 * width),
+        bias=buffer(2 * tiles, WIN * BINS, 128, full), bias_grad=buffer(WIN * BINS, width, full),
         up_sum=buffer(hidden // width, width, full), att_sum=buffer(128, width, full),
-        out_low=buffer(tok, width),
+        units=pltpu.SMEM((5, tok // (SHORT // slab_size * BINS)), jnp.int32),
         load_sems=pltpu.SemaphoreType.DMA((2,)),
         whole_qkv=whole(masters[0]), whole_proj=whole(masters[1]),
         whole_up=whole(masters[2]), whole_down=whole(masters[3]),
     )
-    copies = 12 * (depth - 1 + 7) + 8 * (7 + depth - 1) + 3 + depth - 1 + 4
+    copies = 12 * (depth - 1 + 7) + 8 * (7 + depth - 1) + 3 + depth - 1 + 16
     scratch = [pltpu.SemaphoreType.DMA((copies,)), pltpu.SemaphoreType.DMA((copies,)), *held]
     small = (16, width)
     scratch += [
@@ -1133,7 +1126,58 @@
             collective_id=0, has_side_effects=True, vmem_limit_bytes=62 << 20
         ),
         name="block",
-    )(tokens, y_grad, unit_table(clip_rows[0], slab_size, tok), vectors, table, *masters)
+    )(tokens, y_grad, clip_rows, vectors, table.T, *masters)
+
+
+def finish_kernel(block_out, x_grad, small, *refs):
+    weights, grads = refs[:18], refs[18:22]
+    block_out_to, x_grad_to = refs[22:24]
+    results, (held_out, held_grad, sems) = refs[24:-3], refs[-3:]
+    passing = [
+        pltpu.make_async_copy(block_out, held_out, sems.at[0]),
+        pltpu.make_async_copy(x_grad, held_grad, sems.at[1]),
+    ]
+    for copy in passing:
+        copy.start()
+    rows = weights[12].shape[0]
+    table = jnp.concatenate(
+        [small[rows:, 128 * i : 128 * (i + 1)] for i in range(small.shape[1] // 128)], 0
+    )
+    values = [grad[...] for grad in grads] + [small[:rows, :], table[:, :RELS]]
+    for k, grad in enumerate(values):
+        weight, first, second = [ref[...] for ref in weights[3 * k : 3 * k + 3]]
+        rate, decay = (rate_matrix, weight_decay) if k < len(grads) else (rate_vector, 0.0)
+        for ref, value in zip(
+            results[3 * k : 3 * k + 3], adamw(weight, first, second, grad, rate, decay)
+        ):
+            ref[...] = value
+    passed = [
+        pltpu.make_async_copy(held_out, block_out_to, sems.at[2]),
+        pltpu.make_async_copy(held_grad, x_grad_to, sems.at[3]),
+    ]
+    for before, after in zip(passing, passed):
+        before.wait()
+        after.start()
+    for copy in passed:
+        copy.wait()
+
+
+def finish_call(block_out, x_grad, small, weights, grads):
+    vmem, anywhere = pl.BlockSpec(memory_space=pltpu.VMEM), pl.BlockSpec(memory_space=pl.ANY)
+    like = [jax.ShapeDtypeStruct(a.shape, a.dtype) for a in (block_out, x_grad, *weights)]
+    return pl.pallas_call(
+        finish_kernel,
+        out_shape=like,
+        in_specs=[anywhere, anywhere] + [vmem] * (1 + len(weights) + len(grads)),
+        out_specs=[anywhere, anywhere] + [vmem] * len(weights),
+        scratch_shapes=[
+            pltpu.VMEM(block_out.shape, block_out.dtype),
+            pltpu.VMEM(x_grad.shape, x_grad.dtype),
+            pltpu.SemaphoreType.DMA((4,)),
+        ],
+        compiler_params=pltpu.CompilerParams(vmem_limit_bytes=62 << 20),
+        name="finish",
+    )(block_out, x_grad, small, *weights, *grads)
 
 
 def shards(
@@ -1167,16 +1211,14 @@
         block_out, x_grad, small, *owned = block_call(
             tokens[0, 0], y_grad[0, 0], clip_rows, vectors, table, masters, slab_size, clip_size
         )
-        results = [block_out[None, None], x_grad[None, None]]
-        moments = ((qkv_m, qkv_v), (proj_m, proj_v), (up_m, up_v), (down_m, down_v))
-        for master, (first, second), grad in zip(masters, moments, owned):
-            results += adamw(master, first, second, grad, rate_matrix, weight_decay)
-        rows = vectors.shape[0]
-        results += adamw(vectors, vectors_m, vectors_v, small[:rows], rate_vector, 0.0)
-        by_head = small[rows : rows + 4].reshape(4, -1, 128).transpose(1, 0, 2).reshape(-1, 128)
-        results += adamw(
-            table, table_m, table_v, by_head[: table.shape[1], :RELS].T, rate_vector, 0.0
+        weights = (
+            qkv_weight, qkv_m, qkv_v, proj_weight, proj_m, proj_v,
+            up_weight, up_m, up_v, down_weight, down_m, down_v,
+            vectors, vectors_m, vectors_v, table.T, table_m.T, table_v.T,
         )
+        results = finish_call(block_out, x_grad, small, weights, owned)
+        results = [results[0][None, None], results[1][None, None], *results[2:]]
+        results[-3:] = [result.T for result in results[-3:]]
         return tuple(results)
     lengths = clip_rows[0]
     slab_count = lax.axis_size(SLAB)

time: 125 us -> 107 us (0.86)
  other arithmetic: 9.58 us -> 0 us
  local copies, waits for them, and re-layouts: 5.82 us -> 0 us
  Pallas kernels: 108 us -> 106 us
    pallas_call x1, Pallas kernels: 108 us -> 99.6 us  [block_call(): pl.pallas_call(functools.partial(block_kernel, slab_size, clip_size), out...]
    sub x6 -> x0, other arithmetic: 7.72 us -> none  [adamw(): return (weight - rate * (update + decay * weight), first, second)]
    pallas_call x0 -> x1, Pallas kernels: none -> 5.96 us  [finish_call(): pl.pallas_call(finish_kernel, out_shape=like, in_specs=[anywhere, anywher...]
    unnamed x45 -> x0, local copies, waits for them, and re-layouts: 3.78 us -> none
    slice x2 -> x0, local copies, waits for them, and re-layouts: 1.4 us -> none  [the longest x1 0.82 us: shards(): small[rows:rows + 4].reshape(4, -1, 128).transpose(1, 0, 2).reshape(-1, 128)]
where the time goes in v4:
time: 107 us; the launch traced here: 106 us
  Pallas kernels  106 us (99%)
    pallas_call x1, Pallas kernels, block_call(): pl.pallas_call(functools.partial(block_kernel, slab_size, clip_size), out...  99.6 us
    pallas_call x1, Pallas kernels, finish_call(): pl.pallas_call(finish_kernel, out_shape=like, in_specs=[anywhere, anywher...  5.96 us

profile of v4, /device:TPU:0, one launch (start us, length us, event | category | flops | bytes accessed | tf_op | source)
XLA Modules:
  0.0 106.4 jit_solution(4810246358288861358)
XLA Ops:
  0.7 99.6 %block.1 = (bf16[1024,512]{1,0:T(8,128)(2,1)}, f32[1024,512]{1,0:T(8,128)}, f32[16,512]{1,0:T(8,128)}, f32[64,384]{1,0:T(8,128)}, f32[64,128]{1,0:T(8,128)}, /*index=5*/f32[64,512]{1,0:T(8,128)}, f32[256,128]{1,0:T(8,128)}) custom-call(bf16[1024,512]{1,0:T(8,128)(2,1)} %bitcast.10, bf16[1024,512]{1,0:T(8,128)(2,1)} %bitcast.11, s32[1,4]{1,0:T(1,128)} %refs_2_.2, ...), custom_call_target="tpu_custom_call" | custom-call | tf_op jit(solution)/shard_map/block/pallas_call | solution.py:1114
  100.2 6.0 %finish.1 = (bf16[1024,512]{1,0:T(8,128)(2,1)}, f32[1024,512]{1,0:T(8,128)}, f32[64,384]{1,0:T(8,128)}, f32[64,384]{1,0:T(8,128)}, f32[64,384]{1,0:T(8,128)}, /*...) custom-call(bf16[1024,512]{1,0:T(8,128)(2,1)} %get-tuple-element.47., ...), custom_call_target="tpu_custom_call" | custom-call | tf_op jit(solution)/shard_map/finish/pallas_call | solution.py:1168
